TPU v7x, 32 devices: a whole 2x2x4 slice. The times are simulated.
32 devices in a mesh: grp: 4 (over z), dev: 8 (over y, x, core).
Axes of the slice: x: 2, y: 2, z: 4, core: 2. Of those that a mesh axis runs over, the one named last changes fastest.
Arguments:
- fields: float32 [128, 6, 16, 256], P(('grp', 'dev')), may hold values from 0 to 1
- swap_dev: int32 [32], P(('grp', 'dev')), may hold values from 0 to 1, as said below
- swap_grp: int32 [32], P(('grp', 'dev')), may hold values from 0 to 1, as said below
- neighbors: int32 [128, 6], P(('grp', 'dev')), may hold values from -1 to 127, as said below
- orient: int32 [128], P(('grp', 'dev')), may hold values from 0 to 7
Outputs:
- advanced: float32 [128, 6, 16, 256], P(('grp', 'dev'))
Inputs may be any that keep to these rules, and one draw needn't show every extreme that they name: `swap_dev`: equal on devices 2i and 2i+1 of each group. `swap_grp`: equal on the devices of one dev index in groups 2j and 2j+1. `neighbors`: adjacency is mutual: b names n across a face exactly when n names b across the opposite face. Neighbours across -x and -y lie on the same device or the previous dev index of the same group, across +x and +y on the same device or the next dev index of the same group; across -z and +z on the same dev index of the previous and the next group.
All inputs are finite; a program needn't handle non-finite values.
Results may differ from a plain program's by a relative error of at most 0.0001.
Values sent between devices are 32-bit elements; how exact they have to be, the bound alone decides.
No kernel may reach another device: no remote copies, remote signals or barrier semaphores. Data moves between devices by JAX's collectives and lax.ppermute only.
A program may use at most 64 MiB of HBM per device.

v0:
```python
import functools
import math

import jax
import jax.numpy as jnp
from jax import lax
from jax.experimental import pallas as pl
from jax.experimental.pallas import tpu as pltpu
from jax.sharding import PartitionSpec as P

NPHASE = 4
NCONC = 2
NFIELD = NPHASE + NCONC
STEPS = 2
EDGE = 16
PLANE = EDGE * EDGE
HALF = PLANE // 2
GROUPS = HALF // EDGE
SLOTS = 4
ROWS = NFIELD * SLOTS

phase_rate = 0.05
closure = 0.1
coupling = (0.5, -0.5, 1.0, -1.0)
conc_rates = (0.08, 0.04)

STATE = (2, EDGE * ROWS, HALF)
FACE = (ROWS, PLANE)
SIDE = (3, ROWS, PLANE)
SOURCES = 4


def partners(axis, offset):
    sizes = (lax.axis_size("grp"), lax.axis_size("dev"))
    along = ("grp", "dev").index(axis)
    route = []
    for grp in range(sizes[0]):
        for dev in range(sizes[1]):
            own = (grp, dev)
            step = 1 if (own[along] - offset) % 2 == 0 else -1
            partner = list(own)
            partner[along] += step
            if not 0 <= partner[along] < sizes[along]:
                partner = list(own)
                partner[1 - along] ^= 1
                if partner[1 - along] >= sizes[1 - along]:
                    partner = list(own)
            route.append((grp * sizes[1] + dev, partner[0] * sizes[1] + partner[1]))
    return route


def exchange(block, axis, offset):
    return lax.ppermute(block, ("grp", "dev"), partners(axis, offset))


def iota(shape, dim):
    return lax.broadcasted_iota(jnp.int32, shape, dim)


def plane_at(ref, x):
    rows = pl.ds(x * ROWS, ROWS)
    return ref[0, rows, :], ref[1, rows, :]


def turned(value, shift):
    shift %= HALF
    return pltpu.roll(value, shift, 1) if shift else value


class Packer:
    def __init__(self):
        lane = iota((ROWS, HALF), 1)
        self.lane, self.group, self.place = lane, lane // EDGE, lane % EDGE
        self.y = [[None, None], [None, None]]
        self.z = [[None, None], [None, None]]

    def add(self, x, left, right):
        odd, half, at = x % 2, x // GROUPS, x % GROUPS
        ends = turned(jnp.where(self.lane < EDGE, left, right), EDGE * at)
        taken = (self.group == at) | (self.group == (at + GROUPS - 1) % GROUPS)
        before = self.y[half][odd]
        self.y[half][odd] = ends if before is None else jnp.where(taken, ends, before)
        taken = (self.place == x) | (self.place == (x + EDGE - 1) % EDGE)
        for h, value in enumerate((left, right)):
            moved = turned(value, x)
            before = self.z[h][odd]
            self.z[h][odd] = moved if before is None else jnp.where(taken, moved, before)

    def tables(self, h):
        even_group, even_place = self.group % 2 == 0, self.place % 2 == 0
        (y_even, y_odd), (z_even, z_odd) = self.y[h], self.z[h]
        low = (jnp.where(even_group, y_even, y_odd), jnp.where(even_place, z_even, z_odd))
        y_high, z_high = jnp.where(even_group, y_odd, y_even), jnp.where(even_place, z_odd, z_even)
        return low, (turned(y_high, EDGE), turned(z_high, 1 - EDGE))


def emit_faces(packer, state, own, sends):
    low, high = own
    for h in range(2):
        lanes = pl.ds(h * HALF, HALF)
        for ref, x in ((low, 0), (high, EDGE - 1)):
            ref[0, :, lanes] = state[h, pl.ds(x * ROWS, ROWS), :]
        for ref, (y_table, z_table) in zip(own, packer.tables(h)):
            ref[1, :, lanes] = y_table
            ref[2, :, lanes] = z_table
    flat_a, flat_b, deep_a, deep_b = sends
    even = lax.rem(lax.axis_index("dev"), 2) == 0
    for face in range(2):
        flat_a[face] = jnp.where(even, high[face], low[face])
        flat_b[face] = jnp.where(even, low[face], high[face])
    even = lax.rem(lax.axis_index("grp"), 2) == 0
    deep_a[...] = jnp.where(even, high[2], low[2])
    deep_b[...] = jnp.where(even, low[2], high[2])


def migrate_kernel(swap_dev, swap_grp, scale, fields, last, first, state, *outs):
    del scale
    own, sends = outs[0:2], outs[2:6]
    for slot in range(SLOTS):
        for f in range(NFIELD):
            value = fields[slot, f]
            if slot == 0:
                value = jnp.where(swap_grp[0] == 1, first[0, f], value)
            if slot == SLOTS - 1:
                value = jnp.where(swap_dev[0] == 1, last[0, f], value)
            for h in range(2):
                state[h, pl.ds(f * SLOTS + slot, EDGE, stride=ROWS), :] = value[:, h * HALF : (h + 1) * HALF]
    packer = Packer()
    for x in range(EDGE):
        packer.add(x, *plane_at(state, x))
    emit_faces(packer, state, own, sends)


def cos_quarter(number):
    turn = number & 7
    size = jnp.where((turn & 3) == 0, 1.0, jnp.where((turn & 3) == 2, 0.0, math.sqrt(0.5)))
    return jnp.where((turn > 2) & (turn < 6), -size, size)


def plan_kernel(neighbors, orient, scale, select):
    shape = (ROWS, HALF)
    slot, field, column = iota(shape, 0) % SLOTS, iota(shape, 0) // SLOTS, iota(shape, 1)
    grp, dev = lax.axis_index("grp"), lax.axis_index("dev")
    rank = grp * lax.axis_size("dev") + dev

    def by_slot(values):
        rows = values[0]
        for number in range(1, SLOTS):
            rows = jnp.where(slot == number, values[number], rows)
        return rows

    spread = []
    for number in range(SLOTS):
        turn = 0.5 * cos_quarter(orient[number])
        lift = 0.5 * cos_quarter(orient[number] + 6)
        spread.append((1.0 + turn, 1.0 - turn, 1.0 + lift))
    conc = jnp.where(field == NPHASE, conc_rates[0], conc_rates[1])
    weights = [jnp.where(field < NPHASE, phase_rate * by_slot([own[axis] for own in spread]), conc) for axis in range(3)]
    for axis in range(3):
        scale[axis] = weights[axis]
    scale[3] = 1.0 - 2.0 * (weights[0] + weights[1] + weights[2])
    for face in range(6):
        first = []
        came = 2 + lax.rem(lax.rem(dev if face < 4 else grp, 2) + face % 2 + 1, 2)
        for number in range(SLOTS):
            target = neighbors[number, face]
            source = jnp.where(target < 0, 0, jnp.where(target // SLOTS == rank, 1, came))
            first.append(source * ROWS + jnp.where(target < 0, number, target & (SLOTS - 1)))
        select[face] = jnp.where(column == by_slot(first) + field * SLOTS, weights[face // 2], 0.0)


def inner_kernel(state, scale, partial):
    lane = iota((ROWS, HALF), 1)
    start_y, end_y = lane < EDGE, lane >= HALF - EDGE
    start_z, end_z = lane % EDGE == 0, lane % EDGE == EDGE - 1
    weight_x, weight_y, weight_z, weight = (scale[number] for number in range(4))
    tile = 2 * SLOTS
    planes = {0: plane_at(state, 0)}
    for x in range(EDGE):
        if x + 1 < EDGE:
            planes[x + 1] = plane_at(state, x + 1)
        left, right = planes[x]
        up = [turned(half, EDGE) for half in (left, right)]
        down = [turned(half, -EDGE) for half in (left, right)]
        sum_y = (
            jnp.where(start_y, 0.0, up[0]) + jnp.where(end_y, down[1], down[0]),
            jnp.where(start_y, up[0], up[1]) + jnp.where(end_y, 0.0, down[1]),
        )
        for h, half in enumerate((left, right)):
            sum_z = jnp.where(start_z, 0.0, turned(half, 1)) + jnp.where(end_z, 0.0, turned(half, -1))
            if x == 0:
                sum_x = planes[1][h]
            elif x == EDGE - 1:
                sum_x = planes[x - 1][h]
            else:
                sum_x = planes[x - 1][h] + planes[x + 1][h]
            flow = weight * half + weight_x * sum_x + weight_y * sum_y[h] + weight_z * sum_z
            phases, conc = (half[:tile], half[tile : 2 * tile]), half[2 * tile :]
            drive = conc - pltpu.roll(conc, SLOTS, 0)
            total = phases[0] + phases[1]
            total = total + pltpu.roll(total, SLOTS, 0)
            tail = (phase_rate * closure) * (1.0 - total)
            rows = x * ROWS
            for number, value in enumerate(phases):
                gain = value * (1.0 - value) * (coupling[2 * number] * drive + (2.0 * value - 1.0))
                part = flow[number * tile : (number + 1) * tile]
                partial[h, pl.ds(rows + number * tile, tile), :] = part + (phase_rate * gain + tail)
            partial[h, pl.ds(rows + 2 * tile, tile), :] = flow[2 * tile :]


def finish_kernel(last_step, select, partial, *refs):
    own, got_flat, got_deep = refs[0:2], refs[2:4], refs[4:6]
    if last_step:
        result, done, blocks, sent = refs[6:10]
    else:
        done, outs, sends = refs[6], refs[7:9], refs[9:13]
    ghosts = []
    for face in range(6):
        axis, side = face // 2, face % 2
        got = [ref[axis] for ref in got_flat] if axis < 2 else [ref[...] for ref in got_deep]
        tables = jnp.concatenate([own[side][axis], own[1 - side][axis], *got], axis=0)
        chosen = select[face][:, : SOURCES * ROWS]
        ghosts.append(jnp.dot(chosen, tables, precision=lax.Precision.HIGHEST, preferred_element_type=jnp.float32))
    lane = iota((ROWS, HALF), 1)
    start_y, end_y = lane < EDGE, lane >= HALF - EDGE
    ends_z = (lane % EDGE == 0) | (lane % EDGE == EDGE - 1)
    even_group, even_place = (lane // EDGE) % 2 == 0, lane % 2 == 0
    y_pairs, z_pairs = [], []
    for h in range(2):
        lanes = slice(h * HALF, (h + 1) * HALF)
        low, high = ghosts[2][:, lanes], turned(ghosts[3][:, lanes], -EDGE)
        y_pairs.append((jnp.where(even_group, low, high), jnp.where(even_group, high, low)))
        low, high = ghosts[4][:, lanes], turned(ghosts[5][:, lanes], EDGE - 1)
        z_pairs.append((jnp.where(even_place, low, high), jnp.where(even_place, high, low)))
    packer = None if last_step else Packer()
    copies = []
    for x in range(EDGE):
        halves = list(plane_at(partial, x))
        ends = turned(y_pairs[x // GROUPS][x % 2], -EDGE * (x % GROUPS))
        for h in range(2):
            value = halves[h] + jnp.where(start_y if h == 0 else end_y, ends, 0.0)
            value = value + jnp.where(ends_z, turned(z_pairs[h][x % 2], -x), 0.0)
            if x == 0:
                value = value + ghosts[0][:, h * HALF : (h + 1) * HALF]
            if x == EDGE - 1:
                value = value + ghosts[1][:, h * HALF : (h + 1) * HALF]
            done[h, pl.ds(x * ROWS, ROWS), :] = value
            halves[h] = value
        if not last_step:
            packer.add(x, *halves)
        elif x % 8 == 7:
            first = x - 7
            for slot in range(SLOTS):
                for f in range(NFIELD):
                    rows = pl.ds(first * ROWS + f * SLOTS + slot, 8, stride=ROWS)
                    for h in range(2):
                        lanes = pl.ds(h * HALF, HALF)
                        blocks[slot, f, first : first + 8, lanes] = done[h, rows, :]
            part = pl.ds(first, 8)
            copy = pltpu.make_async_copy(blocks.at[:, :, part], result.at[:, :, part], sent.at[x // 8])
            copy.start()
            copies.append(copy)
    for copy in copies:
        copy.wait()
    if not last_step:
        emit_faces(packer, done, outs, sends)


def spec(space):
    return pl.BlockSpec(memory_space=space)


VECTOR, SCALAR = pltpu.VMEM, pltpu.SMEM
SMALL = pltpu.CompilerParams(vmem_limit_bytes=8 << 20)
FLAT = (2, ROWS, PLANE)
TABLES = (STATE, SIDE, SIDE, FLAT, FLAT, FACE, FACE)


def shaped(shape):
    return jax.ShapeDtypeStruct(shape, jnp.float32)


def cost(flops):
    return pl.CostEstimate(flops=flops, bytes_accessed=2 << 20, transcendentals=0)


def body(fields, swap_dev, swap_grp, neighbors, orient):
    first = exchange(fields[:1], "grp", 0)
    last = exchange(fields[SLOTS - 1 :], "dev", 0)
    scale, select = pl.pallas_call(
        plan_kernel,
        name="plan",
        compiler_params=SMALL,
        out_shape=[shaped((4, ROWS, HALF)), shaped((6, ROWS, HALF))],
        in_specs=[spec(SCALAR)] * 2,
        out_specs=[spec(VECTOR)] * 2,
        cost_estimate=cost(1 << 20),
    )(neighbors, orient)
    state, *tables = pl.pallas_call(
        migrate_kernel,
        name="migrate",
        compiler_params=SMALL,
        out_shape=[shaped(shape) for shape in TABLES],
        in_specs=[spec(SCALAR)] * 2 + [spec(VECTOR)] * 4,
        out_specs=[spec(VECTOR)] * 7,
    )(swap_dev, swap_grp, scale, fields, last, first)
    for step in range(STEPS):
        last_step = step == STEPS - 1
        own, sends = tables[:2], tables[2:]
        got = [exchange(sends[number], "dev" if number < 2 else "grp", number % 2) for number in range(4)]
        partial = pl.pallas_call(
            inner_kernel,
            name=f"inner_{step}",
            compiler_params=SMALL,
            out_shape=shaped(STATE),
            in_specs=[spec(VECTOR)] * 2,
            out_specs=spec(VECTOR),
            cost_estimate=cost(4 << 20),
        )(state, scale)
        finish = functools.partial(finish_kernel, last_step)
        in_specs = [spec(VECTOR)] * 8
        if last_step:
            return pl.pallas_call(
                finish,
                name=f"finish_{step}",
                compiler_params=SMALL,
                out_shape=shaped(fields.shape),
                in_specs=in_specs,
                out_specs=spec(pl.ANY),
                scratch_shapes=[
                    pltpu.VMEM(STATE, jnp.float32),
                    pltpu.VMEM(fields.shape, jnp.float32),
                    pltpu.SemaphoreType.DMA((2,)),
                ],
            )(select, partial, *own, *got)
        state, *tables = pl.pallas_call(
            finish,
            name=f"finish_{step}",
            compiler_params=SMALL,
            out_shape=[shaped(shape) for shape in TABLES],
            in_specs=in_specs,
            out_specs=[spec(VECTOR)] * 7,
        )(select, partial, *own, *got)


def solution(mesh):
    in_specs = (
        P(("grp", "dev"), None, None, None),
        P(("grp", "dev")),
        P(("grp", "dev")),
        P(("grp", "dev"), None),
        P(("grp", "dev")),
    )
    out_specs = P(("grp", "dev"), None, None, None)
    return jax.shard_map(body, mesh=mesh, in_specs=in_specs, out_specs=out_specs, check_vma=False)
```

profile of v0, /device:TPU:0, one launch (start us, length us, event | category | flops | bytes accessed | tf_op | source)
XLA Modules:
  0.0 21.3 jit_solution(8900087829466293435)
XLA Ops:
  0.0 0.0 copy-start
  0.0 1.0 %fusion = (f32[1,6,16,256]{3,2,1,0:T(8,128)S(1)}, f32[1,6,16,256]{3,2,1,0:T(8,128)S(1)}) fusion(f32[4,6,16,256]{3,2,1,0:T(8,128)} %fields.1), kind=kLoop, calls=%fused_computation | loop fusion | bytes 393216 | tf_op jit(solution)/shard_map/slice | solution.py:288
  1.0 3.1 %collective-permute-start.1 = (f32[1,6,16,256]{3,2,1,0:T(8,128)S(1)}, f32[1,6,16,256]{3,2,1,0:T(8,128)S(1)}, u32[]{:S(2)}, u32[]{:S(2)}) collective-permute-start(f32[1,6,16,256]{3,2,1,0:T(8,128)S(1)} %get-tuple-element.37), channel_id=1, source_target_pairs={{0,8},{1,9},{2,10},{3,11},{4,12},{5,13},{6,14},{7,15},{8,0},{9,1},... | collective-permute-start | bytes 294920 | tf_op jit(solution)/shard_map/ppermute | solution.py:53
  4.1 0.0 copy-start.1
  4.1 0.0 collective-permute-start
  4.8 0.0 copy-start.2
  5.4 0.0 copy-done.1
  5.4 0.0 copy-done.2
  5.5 0.8 %plan.1 = (f32[4,24,128]{2,1,0:T(8,128)S(1)}, f32[6,24,128]{2,1,0:T(8,128)S(1)}) custom-call(s32[4,6]{1,0:T(4,128)S(1)} %copy-done.1, s32[4]{0:T(128)S(1)} %copy-done.2), custom_call_target="tpu_custom_call" | custom-call | flops 1048576 | bytes 2097152 | tf_op jit(solution)/shard_map/plan/pallas_call | solution.py:290
  6.2 0.6 %collective-permute-done.1.first = f32[1,6,16,256]{3,2,1,0:T(8,128)S(1)} collective-permute-done((f32[1,6,16,256]{3,2,1,0:T(8,128)S(1)}, f32[1,6,16,256]{3,2,1,0:T(8,128)S(1)}, u32[]{:S(2)}, u32[]{:S(2)}) %collective-permute-start.1) | collective-permute-done | bytes 98336 | tf_op jit(solution)/shard_map/ppermute | solution.py:53
  6.9 0.0 collective-permute-done.last
  6.9 0.0 copy-done
  6.9 0.3 %migrate.1 = (f32[2,384,128]{2,1,0:T(8,128)S(1)}, f32[3,24,256]{2,1,0:T(8,128)S(1)}, f32[3,24,256]{2,1,0:T(8,128)S(1)}, f32[2,24,256]{2,1,0:T(8,128)S(1)}, f32[2...) custom-call(s32[1]{0:T(128)S(6)} %copy.6.swap_dev, s32[1]{0:T(128)S(6)} %copy.7.swap_grp, ...), custom_call_target="tpu_custom_call" | custom-call | tf_op jit(solution)/shard_map/migrate/pallas_call | solution.py:299
  7.2 0.1 collective-permute-start.2
  7.3 1.9 %collective-permute-start.3 = (f32[2,24,256]{2,1,0:T(8,128)S(1)}, f32[2,24,256]{2,1,0:T(8,128)S(1)}, u32[]{:S(2)}, u32[]{:S(2)}) collective-permute-start(f32[2,24,256]{2,1,0:T(8,128)S(1)} %get-tuple-element.27), channel_id=1, source_target_pairs={{0,8},{1,2},{2,1},{3,4},{4,3},{5,6},{6,5},{7,15},{8,0},{9,10},{10,... | collective-permute-start | bytes 147464 | tf_op jit(solution)/shard_map/ppermute | solution.py:53
  9.2 0.2 collective-permute-start.4
  9.4 1.1 %collective-permute-start.5 = (f32[24,256]{1,0:T(8,128)S(1)}, f32[24,256]{1,0:T(8,128)S(1)}, u32[]{:S(2)}, u32[]{:S(2)}) collective-permute-start(f32[24,256]{1,0:T(8,128)S(1)} %get-tuple-element.29), channel_id=1, source_target_pairs={{0,1},{1,0},{2,3},{3,2},{4,5},{5,4},{6,7},{7,6},{8,16},{9,17},{10,... | collective-permute-start | bytes 73736 | tf_op jit(solution)/shard_map/ppermute | solution.py:53
  10.5 0.5 %inner_0.1.partial = f32[2,384,128]{2,1,0:T(8,128)S(1)} custom-call(f32[2,384,128]{2,1,0:T(8,128)S(1)} %get-tuple-element.23.state, f32[4,24,128]{2,1,0:T(8,128)S(1)} %get-tuple-element.22.scale), custom_call_target="tpu_custom_call" | custom-call | flops 4194304 | bytes 2097152 | tf_op jit(solution)/shard_map/inner_0/pallas_call | solution.py:311
  11.0 2.0 %collective-permute-done.4.refs_4_ = f32[24,256]{1,0:T(8,128)S(1)} collective-permute-done((f32[24,256]{1,0:T(8,128)S(1)}, f32[24,256]{1,0:T(8,128)S(1)}, u32[]{:S(2)}, u32[]{:S(2)}) %collective-permute-start.4) | collective-permute-done | bytes 24608 | tf_op jit(solution)/shard_map/ppermute | solution.py:53
  13.0 0.0 collective-permute-done.5.refs_5_
  13.0 0.0 collective-permute-done.2.refs_2_
  13.0 0.0 collective-permute-done.3.refs_3_
  13.1 0.8 %finish_0.1 = (f32[2,384,128]{2,1,0:T(8,128)S(1)}, f32[3,24,256]{2,1,0:T(8,128)S(1)}, f32[3,24,256]{2,1,0:T(8,128)S(1)}, f32[2,24,256]{2,1,0:T(8,128)S(1)}, f32[...) custom-call(f32[6,24,128]{2,1,0:T(8,128)S(1)} %get-tuple-element.21.select, ...), custom_call_target="tpu_custom_call" | custom-call | tf_op jit(solution)/shard_map/finish_0/pallas_call | solution.py:336
  13.9 0.0 collective-permute-start.6
  13.9 2.1 %collective-permute-start.7 = (f32[2,24,256]{2,1,0:T(8,128)S(1)}, f32[2,24,256]{2,1,0:T(8,128)S(1)}, u32[]{:S(2)}, u32[]{:S(2)}) collective-permute-start(f32[2,24,256]{2,1,0:T(8,128)S(1)} %get-tuple-element.34), channel_id=1, source_target_pairs={{0,8},{1,2},{2,1},{3,4},{4,3},{5,6},{6,5},{7,15},{8,0},{9,10},{10,... | collective-permute-start | bytes 147464 | tf_op jit(solution)/shard_map/ppermute | solution.py:53
  16.0 0.1 collective-permute-start.8
  16.1 1.2 %collective-permute-start.9 = (f32[24,256]{1,0:T(8,128)S(1)}, f32[24,256]{1,0:T(8,128)S(1)}, u32[]{:S(2)}, u32[]{:S(2)}) collective-permute-start(f32[24,256]{1,0:T(8,128)S(1)} %get-tuple-element.36), channel_id=1, source_target_pairs={{0,1},{1,0},{2,3},{3,2},{4,5},{5,4},{6,7},{7,6},{8,16},{9,17},{10,... | collective-permute-start | bytes 73736 | tf_op jit(solution)/shard_map/ppermute | solution.py:53
  17.2 0.5 %inner_1.1.partial = f32[2,384,128]{2,1,0:T(8,128)S(1)} custom-call(f32[2,384,128]{2,1,0:T(8,128)S(1)} %get-tuple-element.30.state, f32[4,24,128]{2,1,0:T(8,128)S(1)} %get-tuple-element.22.scale), custom_call_target="tpu_custom_call" | custom-call | flops 4194304 | bytes 2097152 | tf_op jit(solution)/shard_map/inner_1/pallas_call | solution.py:311
  17.7 2.1 %collective-permute-done.8.refs_4_ = f32[24,256]{1,0:T(8,128)S(1)} collective-permute-done((f32[24,256]{1,0:T(8,128)S(1)}, f32[24,256]{1,0:T(8,128)S(1)}, u32[]{:S(2)}, u32[]{:S(2)}) %collective-permute-start.8) | collective-permute-done | bytes 24608 | tf_op jit(solution)/shard_map/ppermute | solution.py:53
  19.8 0.0 collective-permute-done.9.refs_5_
  19.8 0.0 collective-permute-done.6.refs_2_
  19.8 0.0 collective-permute-done.7.refs_3_
  19.9 1.4 %finish_1.1 = f32[4,6,16,256]{3,2,1,0:T(8,128)} custom-call(f32[6,24,128]{2,1,0:T(8,128)S(1)} %get-tuple-element.21.select, f32[2,384,128]{2,1,0:T(8,128)S(1)} %inner_1.1.partial, f32[3,24,256]{2,1,0:T(8,128)S(1)} %get-tuple-element.31.refs_0_, f32[3,24,256]{2,1,0:T(8,128)S(1)} %get-tuple-element.32.refs_1_, ...), custom_call_target="tpu_custom_call" | custom-call | tf_op jit(solution)/shard_map/finish_1/pallas_call | solution.py:323
Async XLA Ops:
  0.0 6.9 %copy-start = (f32[4,6,16,256]{3,2,1,0:T(8,128)S(1)}, f32[4,6,16,256]{3,2,1,0:T(8,128)}, u32[]{:S(2)}) copy-start(f32[4,6,16,256]{3,2,1,0:T(8,128)} %fields.1) | copy-start | bytes 1179652
  1.0 5.9 %collective-permute-start.1 = (f32[1,6,16,256]{3,2,1,0:T(8,128)S(1)}, f32[1,6,16,256]{3,2,1,0:T(8,128)S(1)}, u32[]{:S(2)}, u32[]{:S(2)}) collective-permute-start(f32[1,6,16,256]{3,2,1,0:T(8,128)S(1)} %get-tuple-element.37), channel_id=1, source_target_pairs={{0,8},{1,9},{2,10},{3,11},{4,12},{5,13},{6,14},{7,15},{8,0},{9,1},... | collective-permute-start | bytes 294920 | tf_op jit(solution)/shard_map/ppermute | solution.py:53
  4.1 1.3 %copy-start.1 = (s32[4,6]{1,0:T(4,128)S(1)}, s32[4,6]{1,0:T(4,128)}, u32[]{:S(2)}) copy-start(s32[4,6]{1,0:T(4,128)} %neighbors.1) | copy-start | bytes 292
  4.1 2.8 %collective-permute-start = (f32[1,6,16,256]{3,2,1,0:T(8,128)S(1)}, f32[1,6,16,256]{3,2,1,0:T(8,128)S(1)}, u32[]{:S(2)}, u32[]{:S(2)}) collective-permute-start(f32[1,6,16,256]{3,2,1,0:T(8,128)S(1)} %get-tuple-element.38), channel_id=1, source_target_pairs={{0,1},{1,0},{2,3},{3,2},{4,5},{5,4},{6,7},{7,6},{8,9},{9,8},{10,11... | collective-permute-start | bytes 294920 | tf_op jit(solution)/shard_map/ppermute | solution.py:53
  4.8 0.7 %copy-start.2 = (s32[4]{0:T(128)S(1)}, s32[4]{0:T(128)}, u32[]{:S(2)}) copy-start(s32[4]{0:T(128)} %orient.1) | copy-start | bytes 52
  7.2 5.8 %collective-permute-start.2 = (f32[2,24,256]{2,1,0:T(8,128)S(1)}, f32[2,24,256]{2,1,0:T(8,128)S(1)}, u32[]{:S(2)}, u32[]{:S(2)}) collective-permute-start(f32[2,24,256]{2,1,0:T(8,128)S(1)} %get-tuple-element.26), channel_id=1, source_target_pairs={{0,1},{1,0},{2,3},{3,2},{4,5},{5,4},{6,7},{7,6},{8,9},{9,8},{10,11... | collective-permute-start | bytes 147464 | tf_op jit(solution)/shard_map/ppermute | solution.py:53
  7.3 5.7 %collective-permute-start.3 = (f32[2,24,256]{2,1,0:T(8,128)S(1)}, f32[2,24,256]{2,1,0:T(8,128)S(1)}, u32[]{:S(2)}, u32[]{:S(2)}) collective-permute-start(f32[2,24,256]{2,1,0:T(8,128)S(1)} %get-tuple-element.27), channel_id=1, source_target_pairs={{0,8},{1,2},{2,1},{3,4},{4,3},{5,6},{6,5},{7,15},{8,0},{9,10},{10,... | collective-permute-start | bytes 147464 | tf_op jit(solution)/shard_map/ppermute | solution.py:53
  9.2 3.8 %collective-permute-start.4 = (f32[24,256]{1,0:T(8,128)S(1)}, f32[24,256]{1,0:T(8,128)S(1)}, u32[]{:S(2)}, u32[]{:S(2)}) collective-permute-start(f32[24,256]{1,0:T(8,128)S(1)} %get-tuple-element.28), channel_id=1, source_target_pairs={{0,8},{1,9},{2,10},{3,11},{4,12},{5,13},{6,14},{7,15},{8,0},{9,1},... | collective-permute-start | bytes 73736 | tf_op jit(solution)/shard_map/ppermute | solution.py:53
  9.4 3.6 %collective-permute-start.5 = (f32[24,256]{1,0:T(8,128)S(1)}, f32[24,256]{1,0:T(8,128)S(1)}, u32[]{:S(2)}, u32[]{:S(2)}) collective-permute-start(f32[24,256]{1,0:T(8,128)S(1)} %get-tuple-element.29), channel_id=1, source_target_pairs={{0,1},{1,0},{2,3},{3,2},{4,5},{5,4},{6,7},{7,6},{8,16},{9,17},{10,... | collective-permute-start | bytes 73736 | tf_op jit(solution)/shard_map/ppermute | solution.py:53
  13.9 6.0 %collective-permute-start.6 = (f32[2,24,256]{2,1,0:T(8,128)S(1)}, f32[2,24,256]{2,1,0:T(8,128)S(1)}, u32[]{:S(2)}, u32[]{:S(2)}) collective-permute-start(f32[2,24,256]{2,1,0:T(8,128)S(1)} %get-tuple-element.33), channel_id=1, source_target_pairs={{0,1},{1,0},{2,3},{3,2},{4,5},{5,4},{6,7},{7,6},{8,9},{9,8},{10,11... | collective-permute-start | bytes 147464 | tf_op jit(solution)/shard_map/ppermute | solution.py:53
  13.9 5.9 %collective-permute-start.7 = (f32[2,24,256]{2,1,0:T(8,128)S(1)}, f32[2,24,256]{2,1,0:T(8,128)S(1)}, u32[]{:S(2)}, u32[]{:S(2)}) collective-permute-start(f32[2,24,256]{2,1,0:T(8,128)S(1)} %get-tuple-element.34), channel_id=1, source_target_pairs={{0,8},{1,2},{2,1},{3,4},{4,3},{5,6},{6,5},{7,15},{8,0},{9,10},{10,... | collective-permute-start | bytes 147464 | tf_op jit(solution)/shard_map/ppermute | solution.py:53
  16.0 3.8 %collective-permute-start.8 = (f32[24,256]{1,0:T(8,128)S(1)}, f32[24,256]{1,0:T(8,128)S(1)}, u32[]{:S(2)}, u32[]{:S(2)}) collective-permute-start(f32[24,256]{1,0:T(8,128)S(1)} %get-tuple-element.35), channel_id=1, source_target_pairs={{0,8},{1,9},{2,10},{3,11},{4,12},{5,13},{6,14},{7,15},{8,0},{9,1},... | collective-permute-start | bytes 73736 | tf_op jit(solution)/shard_map/ppermute | solution.py:53
  16.1 3.8 %collective-permute-start.9 = (f32[24,256]{1,0:T(8,128)S(1)}, f32[24,256]{1,0:T(8,128)S(1)}, u32[]{:S(2)}, u32[]{:S(2)}) collective-permute-start(f32[24,256]{1,0:T(8,128)S(1)} %get-tuple-element.36), channel_id=1, source_target_pairs={{0,1},{1,0},{2,3},{3,2},{4,5},{5,4},{6,7},{7,6},{8,16},{9,17},{10,... | collective-permute-start | bytes 73736 | tf_op jit(solution)/shard_map/ppermute | solution.py:53
where the time goes:
time: 21.4 us; the launch traced here: 21.3 us
  starting transfers between devices  9.74 us (46%)
  waiting for transfers between devices  4.8 us (22%)
  Pallas kernels  4.31 us (20%)
  between operations  1.41 us (7%)
  local copies, waits for them, and re-layouts  1.02 us (5%)
    ppermute x10, starting transfers between devices, exchange(): return lax.ppermute(block, ('grp', 'dev'), partners(axis, offset))  9.74 us
    ppermute x10, waiting for transfers between devices, exchange(): return lax.ppermute(block, ('grp', 'dev'), partners(axis, offset))  4.8 us
    pallas_call x2, Pallas kernels, body(): pl.pallas_call(finish, name=f'finish_{step}', compiler_params=SMALL, out_...  2.24 us
    slice x1, local copies, waits for them, and re-layouts, body(): first = exchange(fields[:1], 'grp', 0)  1 us
    pallas_call x2, Pallas kernels, body(): pl.pallas_call(inner_kernel, name=f'inner_{step}', compiler_params=SMALL,...  0.95 us
    pallas_call x1, Pallas kernels, body(): pl.pallas_call(plan_kernel, name='plan', compiler_params=SMALL, out_shape...  0.78 us
  transfers between devices with their start and end apart: 10, of which 3 were waited for; matrix products, arithmetic and copies ran while one was open for 0% of the time, Pallas kernels for 8%

commit v1 on v0

--- a/solution.py
+++ b/solution.py
@@ -103,19 +103,30 @@
         for ref, (y_table, z_table) in zip(own, packer.tables(h)):
             ref[1, :, lanes] = y_table
             ref[2, :, lanes] = z_table
-    flat_a, flat_b, deep_a, deep_b = sends
+    flat_a, flat_b, deep = sends
     even = lax.rem(lax.axis_index("dev"), 2) == 0
     for face in range(2):
         flat_a[face] = jnp.where(even, high[face], low[face])
         flat_b[face] = jnp.where(even, low[face], high[face])
-    even = lax.rem(lax.axis_index("grp"), 2) == 0
-    deep_a[...] = jnp.where(even, high[2], low[2])
-    deep_b[...] = jnp.where(even, low[2], high[2])
+    grp = lax.axis_index("grp")
+    for to in range(deep.shape[0]):
+        deep[to] = jnp.where(grp < to, high[2], low[2])
+
+
+def cut_kernel(fields, first, last, done):
+    copies = [
+        pltpu.make_async_copy(fields.at[pl.ds(slot, 1)], ref, done.at[number])
+        for number, (slot, ref) in enumerate(((0, first), (SLOTS - 1, last)))
+    ]
+    for copy in copies:
+        copy.start()
+    for copy in copies:
+        copy.wait()
 
 
 def migrate_kernel(swap_dev, swap_grp, scale, fields, last, first, state, *outs):
     del scale
-    own, sends = outs[0:2], outs[2:6]
+    own, sends = outs[0:2], outs[2:5]
     for slot in range(SLOTS):
         for f in range(NFIELD):
             value = fields[slot, f]
@@ -209,15 +220,18 @@
 
 
 def finish_kernel(last_step, select, partial, *refs):
-    own, got_flat, got_deep = refs[0:2], refs[2:4], refs[4:6]
+    own, got_flat, deep = refs[0:2], refs[2:4], refs[4]
     if last_step:
-        result, done, blocks, sent = refs[6:10]
+        result, done, blocks, sent = refs[5:9]
     else:
-        done, outs, sends = refs[6], refs[7:9], refs[9:13]
+        done, outs, sends = refs[5], refs[6:8], refs[8:11]
+    grp, even = lax.axis_index("grp"), lax.rem(lax.axis_index("grp"), 2) == 0
+    before, after = deep[jnp.maximum(grp - 1, 0)], deep[jnp.minimum(grp + 1, deep.shape[0] - 1)]
+    got_deep = jnp.where(even, after, before), jnp.where(even, before, after)
     ghosts = []
     for face in range(6):
         axis, side = face // 2, face % 2
-        got = [ref[axis] for ref in got_flat] if axis < 2 else [ref[...] for ref in got_deep]
+        got = [ref[axis] for ref in got_flat] if axis < 2 else list(got_deep)
         tables = jnp.concatenate([own[side][axis], own[1 - side][axis], *got], axis=0)
         chosen = select[face][:, : SOURCES * ROWS]
         ghosts.append(jnp.dot(chosen, tables, precision=lax.Precision.HIGHEST, preferred_element_type=jnp.float32))
@@ -273,7 +287,7 @@
 VECTOR, SCALAR = pltpu.VMEM, pltpu.SMEM
 SMALL = pltpu.CompilerParams(vmem_limit_bytes=8 << 20)
 FLAT = (2, ROWS, PLANE)
-TABLES = (STATE, SIDE, SIDE, FLAT, FLAT, FACE, FACE)
+TABLES = (STATE, SIDE, SIDE, FLAT, FLAT)
 
 
 def shaped(shape):
@@ -285,8 +299,17 @@
 
 
 def body(fields, swap_dev, swap_grp, neighbors, orient):
-    first = exchange(fields[:1], "grp", 0)
-    last = exchange(fields[SLOTS - 1 :], "dev", 0)
+    first, last = pl.pallas_call(
+        cut_kernel,
+        name="cut",
+        compiler_params=SMALL,
+        out_shape=[shaped((1, *fields.shape[1:]))] * 2,
+        in_specs=[spec(pltpu.HBM)],
+        out_specs=[spec(VECTOR)] * 2,
+        scratch_shapes=[pltpu.SemaphoreType.DMA((2,))],
+    )(pltpu.with_memory_space_constraint(fields, pltpu.HBM))
+    first = exchange(first, "grp", 0)
+    last = exchange(last, "dev", 0)
     scale, select = pl.pallas_call(
         plan_kernel,
         name="plan",
@@ -300,14 +323,15 @@
         migrate_kernel,
         name="migrate",
         compiler_params=SMALL,
-        out_shape=[shaped(shape) for shape in TABLES],
+        out_shape=[shaped(shape) for shape in (*TABLES, (lax.axis_size("grp"), *FACE))],
         in_specs=[spec(SCALAR)] * 2 + [spec(VECTOR)] * 4,
-        out_specs=[spec(VECTOR)] * 7,
+        out_specs=[spec(VECTOR)] * 6,
     )(swap_dev, swap_grp, scale, fields, last, first)
     for step in range(STEPS):
         last_step = step == STEPS - 1
         own, sends = tables[:2], tables[2:]
-        got = [exchange(sends[number], "dev" if number < 2 else "grp", number % 2) for number in range(4)]
+        got = [exchange(sends[number], "dev", number) for number in range(2)]
+        got.append(lax.all_to_all(sends[2], "grp", 0, 0))
         partial = pl.pallas_call(
             inner_kernel,
             name=f"inner_{step}",
@@ -318,7 +342,7 @@
             cost_estimate=cost(4 << 20),
         )(state, scale)
         finish = functools.partial(finish_kernel, last_step)
-        in_specs = [spec(VECTOR)] * 8
+        in_specs = [spec(VECTOR)] * 7
         if last_step:
             return pl.pallas_call(
                 finish,
@@ -337,9 +361,9 @@
             finish,
             name=f"finish_{step}",
             compiler_params=SMALL,
-            out_shape=[shaped(shape) for shape in TABLES],
+            out_shape=[shaped(shape) for shape in (*TABLES, (lax.axis_size("grp"), *FACE))],
             in_specs=in_specs,
-            out_specs=[spec(VECTOR)] * 7,
+            out_specs=[spec(VECTOR)] * 6,
         )(select, partial, *own, *got)
 
 

time: 21.4 us -> 31.8 us (1.49)
  starting transfers between devices: 9.74 us -> 15.6 us
  waiting for transfers between devices: 4.8 us -> 7.88 us
  Pallas kernels: 4.31 us -> 6.57 us
  local copies, waits for them, and re-layouts: 1.02 us -> 0.01 us
    all_to_all x0 -> x2, starting transfers between devices: none -> 8.41 us  [body(): got.append(lax.all_to_all(sends[2], 'grp', 0, 0))]
    ppermute x10 -> x6, starting transfers between devices: 9.74 us -> 7.22 us  [exchange(): return lax.ppermute(block, ('grp', 'dev'), partners(axis, offset))]
    all_to_all x0 -> x2, waiting for transfers between devices: none -> 1.75 us  [body(): got.append(lax.all_to_all(sends[2], 'grp', 0, 0))]
    ppermute x10 -> x6, waiting for transfers between devices: 4.8 us -> 6.13 us  [exchange(): return lax.ppermute(block, ('grp', 'dev'), partners(axis, offset))]
    pallas_call x0 -> x1, Pallas kernels: none -> 1.01 us  [body(): pl.pallas_call(cut_kernel, name='cut', compiler_params=SMALL, out_shape=[...]
    slice x1 -> x0, local copies, waits for them, and re-layouts: 1 us -> none  [body(): first = exchange(fields[:1], 'grp', 0)]
    pallas_call x1, Pallas kernels: 0.34 us -> 0.97 us  [body(): pl.pallas_call(migrate_kernel, name='migrate', compiler_params=SMALL, out...]
    pallas_call x2, Pallas kernels: 2.24 us -> 2.87 us  [body(): pl.pallas_call(finish, name=f'finish_{step}', compiler_params=SMALL, out_...]
  transfers between devices with their start and end apart: 10 -> 8, of which waited for: 3 -> 5; matrix products, arithmetic and copies ran while one was open for 0% -> 0% of each run, Pallas kernels for 8% -> 5%
where the time goes in v1:
time: 31.8 us; the launch traced here: 31.5 us
  starting transfers between devices  15.6 us (49%)
  waiting for transfers between devices  7.88 us (25%)
  Pallas kernels  6.57 us (21%)
  between operations  1.4 us (4%)
    all_to_all x2, starting transfers between devices, body(): got.append(lax.all_to_all(sends[2], 'grp', 0, 0))  8.41 us
    ppermute x6, starting transfers between devices, exchange(): return lax.ppermute(block, ('grp', 'dev'), partners(axis, offset))  7.22 us
    ppermute x6, waiting for transfers between devices, exchange(): return lax.ppermute(block, ('grp', 'dev'), partners(axis, offset))  6.13 us
    pallas_call x2, Pallas kernels, body(): pl.pallas_call(finish, name=f'finish_{step}', compiler_params=SMALL, out_...  2.87 us
    all_to_all x2, waiting for transfers between devices, body(): got.append(lax.all_to_all(sends[2], 'grp', 0, 0))  1.75 us
    pallas_call x1, Pallas kernels, body(): pl.pallas_call(cut_kernel, name='cut', compiler_params=SMALL, out_shape=[...  1.01 us
    pallas_call x1, Pallas kernels, body(): pl.pallas_call(migrate_kernel, name='migrate', compiler_params=SMALL, out...  0.97 us
    pallas_call x2, Pallas kernels, body(): pl.pallas_call(inner_kernel, name=f'inner_{step}', compiler_params=SMALL,...  0.94 us
  transfers between devices with their start and end apart: 8, of which 5 were waited for; matrix products, arithmetic and copies ran while one was open for 0% of the time, Pallas kernels for 5%

profile of v1, /device:TPU:0, one launch (start us, length us, event | category | flops | bytes accessed | tf_op | source)
XLA Modules:
  0.0 31.5 jit_solution(15617888805782040995)
XLA Ops:
  0.0 0.0 copy-start
  0.0 1.0 %cut.1 = (f32[1,6,16,256]{3,2,1,0:T(8,128)S(1)}, f32[1,6,16,256]{3,2,1,0:T(8,128)S(1)}) custom-call(f32[4,6,16,256]{3,2,1,0:T(8,128)} %fields.3), custom_call_target="tpu_custom_call" | custom-call | tf_op jit(solution)/shard_map/cut/pallas_call | solution.py:302
  1.0 0.5 %collective-permute-start = (f32[1,6,16,256]{3,2,1,0:T(8,128)S(1)}, f32[1,6,16,256]{3,2,1,0:T(8,128)S(1)}, u32[]{:S(2)}, u32[]{:S(2)}) collective-permute-start(f32[1,6,16,256]{3,2,1,0:T(8,128)S(1)} %get-tuple-element.23), channel_id=1, source_target_pairs={{0,1},{1,0},{2,3},{3,2},{4,5},{5,4},{6,7},{7,6},{8,9},{9,8},{10,11... | collective-permute-start | bytes 294920 | tf_op jit(solution)/shard_map/ppermute | solution.py:53
  1.5 0.0 copy-start.1
  1.5 2.7 %collective-permute-start.1 = (f32[1,6,16,256]{3,2,1,0:T(8,128)S(1)}, f32[1,6,16,256]{3,2,1,0:T(8,128)S(1)}, u32[]{:S(2)}, u32[]{:S(2)}) collective-permute-start(f32[1,6,16,256]{3,2,1,0:T(8,128)S(1)} %get-tuple-element.24), channel_id=1, source_target_pairs={{0,8},{1,9},{2,10},{3,11},{4,12},{5,13},{6,14},{7,15},{8,0},{9,1},... | collective-permute-start | bytes 294920 | tf_op jit(solution)/shard_map/ppermute | solution.py:53
  4.8 0.0 copy-start.2
  5.5 0.0 copy-done.1
  5.5 0.0 copy-done.2
  5.5 0.8 %plan.1 = (f32[4,24,128]{2,1,0:T(8,128)S(1)}, f32[6,24,128]{2,1,0:T(8,128)S(1)}) custom-call(s32[4,6]{1,0:T(4,128)S(1)} %copy-done.1, s32[4]{0:T(128)S(1)} %copy-done.2), custom_call_target="tpu_custom_call" | custom-call | flops 1048576 | bytes 2097152 | tf_op jit(solution)/shard_map/plan/pallas_call | solution.py:313
  6.3 0.0 collective-permute-done.last
  6.3 1.2 %collective-permute-done.1.first = f32[1,6,16,256]{3,2,1,0:T(8,128)S(1)} collective-permute-done((f32[1,6,16,256]{3,2,1,0:T(8,128)S(1)}, f32[1,6,16,256]{3,2,1,0:T(8,128)S(1)}, u32[]{:S(2)}, u32[]{:S(2)}) %collective-permute-start.1) | collective-permute-done | bytes 98336 | tf_op jit(solution)/shard_map/ppermute | solution.py:53
  7.6 0.0 copy-done
  7.6 1.0 %migrate.1 = (f32[2,384,128]{2,1,0:T(8,128)S(1)}, f32[3,24,256]{2,1,0:T(8,128)S(1)}, f32[3,24,256]{2,1,0:T(8,128)S(1)}, f32[2,24,256]{2,1,0:T(8,128)S(1)}, f32[2...) custom-call(s32[1]{0:T(128)S(6)} %copy.6.swap_dev, s32[1]{0:T(128)S(6)} %copy.7.swap_grp, ...), custom_call_target="tpu_custom_call" | custom-call | tf_op jit(solution)/shard_map/migrate/pallas_call | solution.py:322
  8.6 5.1 %all-to-all-start = ((f32[4,24,256]{2,1,0:T(8,128)}), f32[4,24,256]{2,1,0:T(8,128)S(1)}, u32[]{:S(2)}, u32[]{:S(2)}) async-start(f32[4,24,256]{2,1,0:T(8,128)} %get-tuple-element.30), calls=%async_computation | async-start | bytes 196608 | tf_op jit(solution)/shard_map/all_to_all | solution.py:334
  13.6 0.0 collective-permute-start.2
  13.6 2.0 %collective-permute-start.3 = (f32[2,24,256]{2,1,0:T(8,128)S(1)}, f32[2,24,256]{2,1,0:T(8,128)S(1)}, u32[]{:S(2)}, u32[]{:S(2)}) collective-permute-start(f32[2,24,256]{2,1,0:T(8,128)S(1)} %get-tuple-element.29), channel_id=1, source_target_pairs={{0,8},{1,2},{2,1},{3,4},{4,3},{5,6},{6,5},{7,15},{8,0},{9,10},{10,... | collective-permute-start | bytes 147464 | tf_op jit(solution)/shard_map/ppermute | solution.py:53
  15.6 0.5 %inner_0.1.partial = f32[2,384,128]{2,1,0:T(8,128)S(1)} custom-call(f32[2,384,128]{2,1,0:T(8,128)S(1)} %get-tuple-element.25.state, f32[4,24,128]{2,1,0:T(8,128)S(1)} %get-tuple-element.22.scale), custom_call_target="tpu_custom_call" | custom-call | flops 4194304 | bytes 2097152 | tf_op jit(solution)/shard_map/inner_0/pallas_call | solution.py:335
  16.1 0.0 collective-permute-done.2.refs_2_
  16.1 2.3 %collective-permute-done.3.refs_3_ = f32[2,24,256]{2,1,0:T(8,128)S(1)} collective-permute-done((f32[2,24,256]{2,1,0:T(8,128)S(1)}, f32[2,24,256]{2,1,0:T(8,128)S(1)}, u32[]{:S(2)}, u32[]{:S(2)}) %collective-permute-start.3) | collective-permute-done | bytes 49184 | tf_op jit(solution)/shard_map/ppermute | solution.py:53
  18.4 1.0 %all-to-all-done.refs_4_ = f32[4,24,256]{2,1,0:T(8,128)S(1)} async-done(((f32[4,24,256]{2,1,0:T(8,128)}), f32[4,24,256]{2,1,0:T(8,128)S(1)}, u32[]{:S(2)}, u32[]{:S(2)}) %all-to-all-start) | async-done | bytes 98336 | tf_op jit(solution)/shard_map/all_to_all | solution.py:334
  19.4 1.5 %finish_0.1 = (f32[2,384,128]{2,1,0:T(8,128)S(1)}, f32[3,24,256]{2,1,0:T(8,128)S(1)}, f32[3,24,256]{2,1,0:T(8,128)S(1)}, f32[2,24,256]{2,1,0:T(8,128)S(1)}, f32[...) custom-call(f32[6,24,128]{2,1,0:T(8,128)S(1)} %get-tuple-element.21.select, f32[2,384,128]{2,1,0:T(8,128)S(1)} %inner_0.1.partial, ...), custom_call_target="tpu_custom_call" | custom-call | tf_op jit(solution)/shard_map/finish_0/pallas_call | solution.py:360
  20.9 3.4 %all-to-all-start.1 = ((f32[4,24,256]{2,1,0:T(8,128)}), f32[4,24,256]{2,1,0:T(8,128)S(1)}, u32[]{:S(2)}, u32[]{:S(2)}) async-start(f32[4,24,256]{2,1,0:T(8,128)} %get-tuple-element.36), calls=%async_computation.1 | async-start | bytes 196608 | tf_op jit(solution)/shard_map/all_to_all | solution.py:334
  24.3 0.0 collective-permute-start.4
  24.3 2.0 %collective-permute-start.5 = (f32[2,24,256]{2,1,0:T(8,128)S(1)}, f32[2,24,256]{2,1,0:T(8,128)S(1)}, u32[]{:S(2)}, u32[]{:S(2)}) collective-permute-start(f32[2,24,256]{2,1,0:T(8,128)S(1)} %get-tuple-element.35), channel_id=1, source_target_pairs={{0,8},{1,2},{2,1},{3,4},{4,3},{5,6},{6,5},{7,15},{8,0},{9,10},{10,... | collective-permute-start | bytes 147464 | tf_op jit(solution)/shard_map/ppermute | solution.py:53
  26.3 0.5 %inner_1.1.partial = f32[2,384,128]{2,1,0:T(8,128)S(1)} custom-call(f32[2,384,128]{2,1,0:T(8,128)S(1)} %get-tuple-element.31.state, f32[4,24,128]{2,1,0:T(8,128)S(1)} %get-tuple-element.22.scale), custom_call_target="tpu_custom_call" | custom-call | flops 4194304 | bytes 2097152 | tf_op jit(solution)/shard_map/inner_1/pallas_call | solution.py:335
  26.8 0.0 collective-permute-done.4.refs_2_
  26.8 2.6 %collective-permute-done.5.refs_3_ = f32[2,24,256]{2,1,0:T(8,128)S(1)} collective-permute-done((f32[2,24,256]{2,1,0:T(8,128)S(1)}, f32[2,24,256]{2,1,0:T(8,128)S(1)}, u32[]{:S(2)}, u32[]{:S(2)}) %collective-permute-start.5) | collective-permute-done | bytes 49184 | tf_op jit(solution)/shard_map/ppermute | solution.py:53
  29.3 0.7 %all-to-all-done.1.refs_4_ = f32[4,24,256]{2,1,0:T(8,128)S(1)} async-done(((f32[4,24,256]{2,1,0:T(8,128)}), f32[4,24,256]{2,1,0:T(8,128)S(1)}, u32[]{:S(2)}, u32[]{:S(2)}) %all-to-all-start.1) | async-done | bytes 98336 | tf_op jit(solution)/shard_map/all_to_all | solution.py:334
  30.1 1.4 %finish_1.1 = f32[4,6,16,256]{3,2,1,0:T(8,128)} custom-call(f32[6,24,128]{2,1,0:T(8,128)S(1)} %get-tuple-element.21.select, f32[2,384,128]{2,1,0:T(8,128)S(1)} %inner_1.1.partial, f32[3,24,256]{2,1,0:T(8,128)S(1)} %get-tuple-element.32.refs_0_, f32[3,24,256]{2,1,0:T(8,128)S(1)} %get-tuple-element.33.refs_1_, ...), custom_call_target="tpu_custom_call" | custom-call | tf_op jit(solution)/shard_map/finish_1/pallas_call | solution.py:347
Async XLA Ops:
  0.0 7.6 %copy-start = (f32[4,6,16,256]{3,2,1,0:T(8,128)S(1)}, f32[4,6,16,256]{3,2,1,0:T(8,128)}, u32[]{:S(2)}) copy-start(f32[4,6,16,256]{3,2,1,0:T(8,128)} %fields.3) | copy-start | bytes 1179652
  1.0 5.3 %collective-permute-start = (f32[1,6,16,256]{3,2,1,0:T(8,128)S(1)}, f32[1,6,16,256]{3,2,1,0:T(8,128)S(1)}, u32[]{:S(2)}, u32[]{:S(2)}) collective-permute-start(f32[1,6,16,256]{3,2,1,0:T(8,128)S(1)} %get-tuple-element.23), channel_id=1, source_target_pairs={{0,1},{1,0},{2,3},{3,2},{4,5},{5,4},{6,7},{7,6},{8,9},{9,8},{10,11... | collective-permute-start | bytes 294920 | tf_op jit(solution)/shard_map/ppermute | solution.py:53
  1.5 4.0 %copy-start.1 = (s32[4,6]{1,0:T(4,128)S(1)}, s32[4,6]{1,0:T(4,128)}, u32[]{:S(2)}) copy-start(s32[4,6]{1,0:T(4,128)} %neighbors.1) | copy-start | bytes 292
  1.5 6.0 %collective-permute-start.1 = (f32[1,6,16,256]{3,2,1,0:T(8,128)S(1)}, f32[1,6,16,256]{3,2,1,0:T(8,128)S(1)}, u32[]{:S(2)}, u32[]{:S(2)}) collective-permute-start(f32[1,6,16,256]{3,2,1,0:T(8,128)S(1)} %get-tuple-element.24), channel_id=1, source_target_pairs={{0,8},{1,9},{2,10},{3,11},{4,12},{5,13},{6,14},{7,15},{8,0},{9,1},... | collective-permute-start | bytes 294920 | tf_op jit(solution)/shard_map/ppermute | solution.py:53
  4.8 0.7 %copy-start.2 = (s32[4]{0:T(128)S(1)}, s32[4]{0:T(128)}, u32[]{:S(2)}) copy-start(s32[4]{0:T(128)} %orient.1) | copy-start | bytes 52
  8.6 10.9 %all-to-all-start = ((f32[4,24,256]{2,1,0:T(8,128)}), f32[4,24,256]{2,1,0:T(8,128)S(1)}, u32[]{:S(2)}, u32[]{:S(2)}) async-start(f32[4,24,256]{2,1,0:T(8,128)} %get-tuple-element.30), calls=%async_computation | async-start | bytes 196608 | tf_op jit(solution)/shard_map/all_to_all | solution.py:334
  13.6 2.5 %collective-permute-start.2 = (f32[2,24,256]{2,1,0:T(8,128)S(1)}, f32[2,24,256]{2,1,0:T(8,128)S(1)}, u32[]{:S(2)}, u32[]{:S(2)}) collective-permute-start(f32[2,24,256]{2,1,0:T(8,128)S(1)} %get-tuple-element.28), channel_id=1, source_target_pairs={{0,1},{1,0},{2,3},{3,2},{4,5},{5,4},{6,7},{7,6},{8,9},{9,8},{10,11... | collective-permute-start | bytes 147464 | tf_op jit(solution)/shard_map/ppermute | solution.py:53
  13.6 4.8 %collective-permute-start.3 = (f32[2,24,256]{2,1,0:T(8,128)S(1)}, f32[2,24,256]{2,1,0:T(8,128)S(1)}, u32[]{:S(2)}, u32[]{:S(2)}) collective-permute-start(f32[2,24,256]{2,1,0:T(8,128)S(1)} %get-tuple-element.29), channel_id=1, source_target_pairs={{0,8},{1,2},{2,1},{3,4},{4,3},{5,6},{6,5},{7,15},{8,0},{9,10},{10,... | collective-permute-start | bytes 147464 | tf_op jit(solution)/shard_map/ppermute | solution.py:53
  20.9 9.2 %all-to-all-start.1 = ((f32[4,24,256]{2,1,0:T(8,128)}), f32[4,24,256]{2,1,0:T(8,128)S(1)}, u32[]{:S(2)}, u32[]{:S(2)}) async-start(f32[4,24,256]{2,1,0:T(8,128)} %get-tuple-element.36), calls=%async_computation.1 | async-start | bytes 196608 | tf_op jit(solution)/shard_map/all_to_all | solution.py:334
  24.3 2.5 %collective-permute-start.4 = (f32[2,24,256]{2,1,0:T(8,128)S(1)}, f32[2,24,256]{2,1,0:T(8,128)S(1)}, u32[]{:S(2)}, u32[]{:S(2)}) collective-permute-start(f32[2,24,256]{2,1,0:T(8,128)S(1)} %get-tuple-element.34), channel_id=1, source_target_pairs={{0,1},{1,0},{2,3},{3,2},{4,5},{5,4},{6,7},{7,6},{8,9},{9,8},{10,11... | collective-permute-start | bytes 147464 | tf_op jit(solution)/shard_map/ppermute | solution.py:53
  24.3 5.1 %collective-permute-start.5 = (f32[2,24,256]{2,1,0:T(8,128)S(1)}, f32[2,24,256]{2,1,0:T(8,128)S(1)}, u32[]{:S(2)}, u32[]{:S(2)}) collective-permute-start(f32[2,24,256]{2,1,0:T(8,128)S(1)} %get-tuple-element.35), channel_id=1, source_target_pairs={{0,8},{1,2},{2,1},{3,4},{4,3},{5,6},{6,5},{7,15},{8,0},{9,10},{10,... | collective-permute-start | bytes 147464 | tf_op jit(solution)/shard_map/ppermute | solution.py:53

commit v2 on v0

--- a/solution.py
+++ b/solution.py
@@ -11,7 +11,6 @@
 NPHASE = 4
 NCONC = 2
 NFIELD = NPHASE + NCONC
-STEPS = 2
 EDGE = 16
 PLANE = EDGE * EDGE
 HALF = PLANE // 2
@@ -94,7 +93,7 @@
         return low, (turned(y_high, EDGE), turned(z_high, 1 - EDGE))
 
 
-def emit_faces(packer, state, own, sends):
+def write_tables(packer, state, own):
     low, high = own
     for h in range(2):
         lanes = pl.ds(h * HALF, HALF)
@@ -103,32 +102,96 @@
         for ref, (y_table, z_table) in zip(own, packer.tables(h)):
             ref[1, :, lanes] = y_table
             ref[2, :, lanes] = z_table
+
+
+def emit_faces(packer, state, own, sends):
+    write_tables(packer, state, own)
+    low, high = own
     flat_a, flat_b, deep_a, deep_b = sends
-    even = lax.rem(lax.axis_index("dev"), 2) == 0
+    even = even_place("dev")
     for face in range(2):
         flat_a[face] = jnp.where(even, high[face], low[face])
         flat_b[face] = jnp.where(even, low[face], high[face])
-    even = lax.rem(lax.axis_index("grp"), 2) == 0
+    even = even_place("grp")
     deep_a[...] = jnp.where(even, high[2], low[2])
     deep_b[...] = jnp.where(even, low[2], high[2])
 
 
-def migrate_kernel(swap_dev, swap_grp, scale, fields, last, first, state, *outs):
-    del scale
-    own, sends = outs[0:2], outs[2:6]
-    for slot in range(SLOTS):
+def fill_state(state, blocks):
+    for slot, block in enumerate(blocks):
         for f in range(NFIELD):
-            value = fields[slot, f]
-            if slot == 0:
-                value = jnp.where(swap_grp[0] == 1, first[0, f], value)
-            if slot == SLOTS - 1:
-                value = jnp.where(swap_dev[0] == 1, last[0, f], value)
+            value = block(f)
             for h in range(2):
                 state[h, pl.ds(f * SLOTS + slot, EDGE, stride=ROWS), :] = value[:, h * HALF : (h + 1) * HALF]
+
+
+def slot_rows():
+    return iota(FACE, 0) % SLOTS
+
+
+def shifted(value, rows):
+    rows %= ROWS
+    return pltpu.roll(value, rows, 0) if rows else value
+
+
+def gathered(tables, slot):
+    rows = slot_rows()
+    out = shifted(tables[0], -slot)
+    for number in range(1, len(tables)):
+        out = jnp.where(rows == number, shifted(tables[number], number - slot), out)
+    return out
+
+
+def scattered(table, number, slot):
+    return shifted(table, slot - number)
+
+
+def even_place(axis):
+    return lax.rem(lax.axis_index(axis), 2) == 0
+
+
+def pack_kernel(fields, low, high, faces_grp, faces_dev, state):
+    fill_state(state, [lambda f, slot=slot: fields[slot, f] for slot in range(SLOTS)])
     packer = Packer()
     for x in range(EDGE):
         packer.add(x, *plane_at(state, x))
-    emit_faces(packer, state, own, sends)
+    write_tables(packer, state, (low, high))
+    faces_grp[0] = gathered([low[0], high[0], low[1], high[1]], 0)
+    faces_grp[1] = jnp.where(even_place("grp"), high[2], low[2])
+    faces_dev[0] = gathered([low[0], high[0], low[1], high[1]], SLOTS - 1)
+    faces_dev[1] = gathered([low[2], high[2]], SLOTS - 1)
+
+
+def block_kernel(swap_dev, fields, low, high, to_dev, to_grp):
+    last, size = SLOTS - 1, NFIELD * EDGE
+    for f in range(NFIELD):
+        to_dev[f * EDGE : (f + 1) * EDGE] = fields[last, f]
+        to_grp[f * EDGE : (f + 1) * EDGE] = fields[0, f]
+    away = jnp.where(even_place("grp"), low[2], high[2])
+    to_grp[size : size + ROWS] = jnp.where(slot_rows() == 0, away, jnp.where(swap_dev[0] == 1, 1.0, 0.0))
+
+
+def faces_kernel(swap_dev, swap_grp, scale, low, high, faces, faces_dev, *outs):
+    del scale
+    new_low, new_high, flat_a, flat_b, deep_b = outs
+    rows, last = slot_rows(), SLOTS - 1
+    first_rows = (rows == 0) & (swap_grp[0] == 1)
+    last_rows = (rows == last) & (swap_dev[0] == 1)
+    even = even_place("grp")
+    got_first, got_last, got_last_z = faces[0], faces_dev[0], faces_dev[1]
+    for side, (raw, new) in enumerate(((low, new_low), (high, new_high))):
+        for axis in range(2):
+            number = 2 * axis + side
+            table = jnp.where(first_rows, scattered(got_first, number, 0), raw[axis])
+            new[axis] = jnp.where(last_rows, scattered(got_last, number, last), table)
+        table = jnp.where(first_rows & (even if side == 0 else ~even), faces[1], raw[2])
+        new[2] = jnp.where(last_rows, scattered(got_last_z, side, last), table)
+    even_dev = even_place("dev")
+    for axis in range(2):
+        flat_a[axis] = jnp.where(even_dev, new_high[axis], new_low[axis])
+        flat_b[axis] = jnp.where(even_dev, new_low[axis], new_high[axis])
+    flat_a[2] = faces[1]
+    deep_b[...] = jnp.where(even, new_low[2], new_high[2])
 
 
 def cos_quarter(number):
@@ -167,6 +230,32 @@
             source = jnp.where(target < 0, 0, jnp.where(target // SLOTS == rank, 1, came))
             first.append(source * ROWS + jnp.where(target < 0, number, target & (SLOTS - 1)))
         select[face] = jnp.where(column == by_slot(first) + field * SLOTS, weights[face // 2], 0.0)
+
+
+def first_inner_kernel(swap_dev, swap_grp, scale, fields, block_dev, block_grp, faces, low, high, new_low, new_high, *refs):
+    partial, got_deep, relayed, z_low, z_high, state = refs
+    size = NFIELD * EDGE
+
+    def block(slot):
+        def of(f):
+            value = fields[slot, f]
+            if slot == 0:
+                value = jnp.where(swap_grp[0] == 1, block_grp[f * EDGE : (f + 1) * EDGE], value)
+            if slot == SLOTS - 1:
+                value = jnp.where(swap_dev[0] == 1, block_dev[f * EDGE : (f + 1) * EDGE], value)
+            return value
+
+        return of
+
+    fill_state(state, [block(slot) for slot in range(SLOTS)])
+    rows, even = slot_rows(), even_place("grp")
+    first_rows = (rows == 0) & (swap_grp[0] == 1)
+    got_deep[...] = jnp.where(first_rows, jnp.where(even, low[2], high[2]), faces[1])
+    other = block_grp[size : size + ROWS]
+    relayed[...] = jnp.where(rows == SLOTS - 1, jnp.broadcast_to(other[1:2], FACE), 0.0)
+    z_low[...] = jnp.where(first_rows & ~even, other, new_low[2])
+    z_high[...] = jnp.where(first_rows & even, other, new_high[2])
+    inner_kernel(state, scale, partial)
 
 
 def inner_kernel(state, scale, partial):
@@ -209,16 +298,22 @@
 
 
 def finish_kernel(last_step, select, partial, *refs):
-    own, got_flat, got_deep = refs[0:2], refs[2:4], refs[4:6]
+    own, got_flat = refs[0:2], refs[2:4]
+    own_deep = [ref[2] for ref in own]
     if last_step:
+        got_deep = [ref[...] for ref in refs[4:6]]
         result, done, blocks, sent = refs[6:10]
     else:
-        done, outs, sends = refs[6], refs[7:9], refs[9:13]
+        known, deep_b, relayed, z_low, z_high = refs[4:9]
+        got_deep = [jnp.where(relayed[...] > 0.5, got_flat[0][2], known[...]), deep_b[...]]
+        own_deep = [z_low[...], z_high[...]]
+        done, outs, sends = refs[9], refs[10:12], refs[12:16]
     ghosts = []
     for face in range(6):
         axis, side = face // 2, face % 2
-        got = [ref[axis] for ref in got_flat] if axis < 2 else [ref[...] for ref in got_deep]
-        tables = jnp.concatenate([own[side][axis], own[1 - side][axis], *got], axis=0)
+        got = [ref[axis] for ref in got_flat] if axis < 2 else got_deep
+        mine = [ref[axis] for ref in own] if axis < 2 else own_deep
+        tables = jnp.concatenate([mine[side], mine[1 - side], *got], axis=0)
         chosen = select[face][:, : SOURCES * ROWS]
         ghosts.append(jnp.dot(chosen, tables, precision=lax.Precision.HIGHEST, preferred_element_type=jnp.float32))
     lane = iota((ROWS, HALF), 1)
@@ -274,6 +369,8 @@
 SMALL = pltpu.CompilerParams(vmem_limit_bytes=8 << 20)
 FLAT = (2, ROWS, PLANE)
 TABLES = (STATE, SIDE, SIDE, FLAT, FLAT, FACE, FACE)
+TO_DEV = (NFIELD * EDGE, PLANE)
+TO_GRP = (NFIELD * EDGE + ROWS, PLANE)
 
 
 def shaped(shape):
@@ -281,66 +378,73 @@
 
 
 def cost(flops):
-    return pl.CostEstimate(flops=flops, bytes_accessed=2 << 20, transcendentals=0)
+    return pl.CostEstimate(flops=flops, bytes_accessed=min(flops, 2 << 20), transcendentals=0)
+
+
+def call(kernel, name, shapes, scalars, vectors, flops=1 << 20, scratch=()):
+    return pl.pallas_call(
+        kernel,
+        name=name,
+        compiler_params=SMALL,
+        out_shape=[shaped(shape) for shape in shapes],
+        in_specs=[spec(SCALAR)] * len(scalars) + [spec(VECTOR)] * len(vectors),
+        out_specs=[spec(VECTOR)] * len(shapes),
+        scratch_shapes=list(scratch),
+        cost_estimate=cost(flops),
+    )(*scalars, *vectors)
 
 
 def body(fields, swap_dev, swap_grp, neighbors, orient):
-    first = exchange(fields[:1], "grp", 0)
-    last = exchange(fields[SLOTS - 1 :], "dev", 0)
-    scale, select = pl.pallas_call(
-        plan_kernel,
-        name="plan",
+    state = pltpu.VMEM(STATE, jnp.float32)
+    low, high, faces, faces_dev = call(pack_kernel, "pack", [SIDE, SIDE, FLAT, FLAT], [], [fields], scratch=[state])
+    faces = exchange(faces, "grp", 0)
+    faces_dev = exchange(faces_dev, "dev", 0)
+    to_dev, to_grp = call(block_kernel, "blocks", [TO_DEV, TO_GRP], [swap_dev], [fields, low, high], 1 << 24)
+    block_grp = exchange(to_grp, "grp", 0)
+    block_dev = exchange(to_dev, "dev", 0)
+    scale, select = call(plan_kernel, "plan", [(4, ROWS, HALF), (6, ROWS, HALF)], [neighbors, orient], [], 0)
+    new_low, new_high, *sends = call(
+        faces_kernel,
+        "faces",
+        [SIDE, SIDE, SIDE, FLAT, FACE],
+        [swap_dev, swap_grp],
+        [scale, low, high, faces, faces_dev],
+        1 << 24,
+    )
+    got_flat = [exchange(sends[number], "dev", number) for number in range(2)]
+    got_b = exchange(sends[2], "grp", 1)
+    partial, got_a, relayed, z_low, z_high = call(
+        first_inner_kernel,
+        "inner_0",
+        [STATE, FACE, FACE, FACE, FACE],
+        [swap_dev, swap_grp],
+        [scale, fields, block_dev, block_grp, faces, low, high, new_low, new_high],
+        4 << 20,
+        [state],
+    )
+    state, *tables = call(
+        functools.partial(finish_kernel, False),
+        "finish_0",
+        TABLES,
+        [],
+        [select, partial, new_low, new_high, *got_flat, got_a, got_b, relayed, z_low, z_high],
+    )
+    own, sends = tables[:2], tables[2:]
+    got = [exchange(sends[number], "dev" if number < 2 else "grp", number % 2) for number in range(4)]
+    (partial,) = call(inner_kernel, "inner_1", [STATE], [], [state, scale], 4 << 20)
+    return pl.pallas_call(
+        functools.partial(finish_kernel, True),
+        name="finish_1",
         compiler_params=SMALL,
-        out_shape=[shaped((4, ROWS, HALF)), shaped((6, ROWS, HALF))],
-        in_specs=[spec(SCALAR)] * 2,
-        out_specs=[spec(VECTOR)] * 2,
-        cost_estimate=cost(1 << 20),
-    )(neighbors, orient)
-    state, *tables = pl.pallas_call(
-        migrate_kernel,
-        name="migrate",
-        compiler_params=SMALL,
-        out_shape=[shaped(shape) for shape in TABLES],
-        in_specs=[spec(SCALAR)] * 2 + [spec(VECTOR)] * 4,
-        out_specs=[spec(VECTOR)] * 7,
-    )(swap_dev, swap_grp, scale, fields, last, first)
-    for step in range(STEPS):
-        last_step = step == STEPS - 1
-        own, sends = tables[:2], tables[2:]
-        got = [exchange(sends[number], "dev" if number < 2 else "grp", number % 2) for number in range(4)]
-        partial = pl.pallas_call(
-            inner_kernel,
-            name=f"inner_{step}",
-            compiler_params=SMALL,
-            out_shape=shaped(STATE),
-            in_specs=[spec(VECTOR)] * 2,
-            out_specs=spec(VECTOR),
-            cost_estimate=cost(4 << 20),
-        )(state, scale)
-        finish = functools.partial(finish_kernel, last_step)
-        in_specs = [spec(VECTOR)] * 8
-        if last_step:
-            return pl.pallas_call(
-                finish,
-                name=f"finish_{step}",
-                compiler_params=SMALL,
-                out_shape=shaped(fields.shape),
-                in_specs=in_specs,
-                out_specs=spec(pl.ANY),
-                scratch_shapes=[
-                    pltpu.VMEM(STATE, jnp.float32),
-                    pltpu.VMEM(fields.shape, jnp.float32),
-                    pltpu.SemaphoreType.DMA((2,)),
-                ],
-            )(select, partial, *own, *got)
-        state, *tables = pl.pallas_call(
-            finish,
-            name=f"finish_{step}",
-            compiler_params=SMALL,
-            out_shape=[shaped(shape) for shape in TABLES],
-            in_specs=in_specs,
-            out_specs=[spec(VECTOR)] * 7,
-        )(select, partial, *own, *got)
+        out_shape=shaped(fields.shape),
+        in_specs=[spec(VECTOR)] * 8,
+        out_specs=spec(pl.ANY),
+        scratch_shapes=[
+            pltpu.VMEM(STATE, jnp.float32),
+            pltpu.VMEM(fields.shape, jnp.float32),
+            pltpu.SemaphoreType.DMA((2,)),
+        ],
+    )(select, partial, *own, *got)
 
 
 def solution(mesh):

time: 21.4 us -> 20.7 us (0.967)
  waiting for transfers between devices: 4.8 us -> 3.89 us
    slice x1 -> x0, local copies, waits for them, and re-layouts: 1 us -> none  [body(): first = exchange(fields[:1], 'grp', 0)]
    unnamed x6 -> x8, local copies, waits for them, and re-layouts: 0.01 us -> 1.01 us
    ppermute x10 -> x11, waiting for transfers between devices: 4.8 us -> 3.89 us  [exchange(): return lax.ppermute(block, ('grp', 'dev'), partners(axis, offset))]
    pallas_call x6 -> x8, Pallas kernels: 4.31 us -> 4.45 us  [the longest x7 3.04 us: call(): pl.pallas_call(kernel, name=name, compiler_params=SMALL, out_shape=[shape...]
    ppermute x10 -> x11, starting transfers between devices: 9.74 us -> 9.73 us  [exchange(): return lax.ppermute(block, ('grp', 'dev'), partners(axis, offset))]
  transfers between devices with their start and end apart: 10 -> 11, of which waited for: 3 -> 3; matrix products, arithmetic and copies ran while one was open for 0% -> 0% of each run, Pallas kernels for 8% -> 9%
where the time goes in v2:
time: 20.7 us; the launch traced here: 20.5 us
  starting transfers between devices  9.73 us (47%)
  Pallas kernels  4.45 us (21%)
  waiting for transfers between devices  3.89 us (19%)
  between operations  1.42 us (7%)
  local copies, waits for them, and re-layouts  1.01 us (5%)
    ppermute x11, starting transfers between devices, exchange(): return lax.ppermute(block, ('grp', 'dev'), partners(axis, offset))  9.73 us
    ppermute x11, waiting for transfers between devices, exchange(): return lax.ppermute(block, ('grp', 'dev'), partners(axis, offset))  3.89 us
    pallas_call x7, Pallas kernels, call(): pl.pallas_call(kernel, name=name, compiler_params=SMALL, out_shape=[shape...  3.04 us
    pallas_call x1, Pallas kernels, body(): pl.pallas_call(functools.partial(finish_kernel, True), name='finish_1', c...  1.41 us
    unnamed x8, local copies, waits for them, and re-layouts  1.01 us
  transfers between devices with their start and end apart: 11, of which 3 were waited for; matrix products, arithmetic and copies ran while one was open for 0% of the time, Pallas kernels for 9%

profile of v2, /device:TPU:0, one launch (start us, length us, event | category | flops | bytes accessed | tf_op | source)
XLA Modules:
  0.0 20.5 jit_solution(1961860262850355601)
XLA Ops:
  0.0 0.0 copy-start
  0.0 1.0 %copy-done = f32[4,6,16,256]{3,2,1,0:T(8,128)S(1)} copy-done((f32[4,6,16,256]{3,2,1,0:T(8,128)S(1)}, f32[4,6,16,256]{3,2,1,0:T(8,128)}, u32[]{:S(2)}) %copy-start) | copy-done | bytes 393240
  1.0 0.0 copy-start.1
  1.0 0.3 %pack.1 = (f32[3,24,256]{2,1,0:T(8,128)S(1)}, f32[3,24,256]{2,1,0:T(8,128)S(1)}, f32[2,24,256]{2,1,0:T(8,128)S(1)}, f32[2,24,256]{2,1,0:T(8,128)S(1)}) custom-call(f32[4,6,16,256]{3,2,1,0:T(8,128)S(1)} %copy-done), custom_call_target="tpu_custom_call" | custom-call | flops 1048576 | bytes 1048576 | tf_op jit(solution)/shard_map/pack/pallas_call | solution.py:385
  1.3 3.1 %collective-permute-start.2 = (f32[2,24,256]{2,1,0:T(8,128)S(1)}, f32[2,24,256]{2,1,0:T(8,128)S(1)}, u32[]{:S(2)}, u32[]{:S(2)}) collective-permute-start(f32[2,24,256]{2,1,0:T(8,128)S(1)} %get-tuple-element.36), channel_id=1, source_target_pairs={{0,8},{1,9},{2,10},{3,11},{4,12},{5,13},{6,14},{7,15},{8,0},{9,1},... | collective-permute-start | bytes 147464 | tf_op jit(solution)/shard_map/ppermute | solution.py:52
  4.4 0.0 collective-permute-start.3
  5.1 0.0 copy-done.1
  5.1 0.0 copy-start.2
  5.1 0.1 collective-permute-start.1
  5.3 0.0 copy-start.3
  5.3 0.5 %collective-permute-start = (f32[96,256]{1,0:T(8,128)S(1)}, f32[96,256]{1,0:T(8,128)S(1)}, u32[]{:S(2)}, u32[]{:S(2)}) collective-permute-start(f32[96,256]{1,0:T(8,128)S(1)} %get-tuple-element.34), channel_id=1, source_target_pairs={{0,1},{1,0},{2,3},{3,2},{4,5},{5,4},{6,7},{7,6},{8,9},{9,8},{10,11... | collective-permute-start | bytes 294920 | tf_op jit(solution)/shard_map/ppermute | solution.py:52
  6.5 0.0 copy-done.2
  6.5 0.0 copy-done.3
  6.5 0.8 %plan.1 = (f32[4,24,128]{2,1,0:T(8,128)S(1)}, f32[6,24,128]{2,1,0:T(8,128)S(1)}) custom-call(s32[4,6]{1,0:T(4,128)S(1)} %copy-done.2, s32[4]{0:T(128)S(1)} %copy-done.3), custom_call_target="tpu_custom_call" | custom-call | tf_op jit(solution)/shard_map/plan/pallas_call | solution.py:385
  7.3 0.0 collective-permute-done.2.faces
  7.3 0.0 collective-permute-done.3.faces_dev
  7.3 0.1 collective-permute-start.4
  7.4 1.9 %collective-permute-start.5 = (f32[2,24,256]{2,1,0:T(8,128)S(1)}, f32[2,24,256]{2,1,0:T(8,128)S(1)}, u32[]{:S(2)}, u32[]{:S(2)}) collective-permute-start(f32[2,24,256]{2,1,0:T(8,128)S(1)} %get-tuple-element.42), channel_id=1, source_target_pairs={{0,8},{1,2},{2,1},{3,4},{4,3},{5,6},{6,5},{7,15},{8,0},{9,10},{10,... | collective-permute-start | bytes 147464 | tf_op jit(solution)/shard_map/ppermute | solution.py:52
  9.3 0.0 collective-permute-start.6
  9.4 0.0 collective-permute-done.block_dev
  9.4 1.6 %collective-permute-done.1.block_grp = f32[120,256]{1,0:T(8,128)S(1)} collective-permute-done((f32[120,256]{1,0:T(8,128)S(1)}, f32[120,256]{1,0:T(8,128)S(1)}, u32[]{:S(2)}, u32[]{:S(2)}) %collective-permute-start.1) | collective-permute-done | bytes 122912 | tf_op jit(solution)/shard_map/ppermute | solution.py:52
  10.9 0.5 %inner_0.1 = (f32[2,384,128]{2,1,0:T(8,128)S(1)}, f32[24,256]{1,0:T(8,128)S(1)}, f32[24,256]{1,0:T(8,128)S(1)}, f32[24,256]{1,0:T(8,128)S(1)}, f32[24,256]{1,0:T(8,128)S(1)}) custom-call(s32[1]{0:T(128)S(6)} %copy.6.swap_dev, s32[1]{0:T(128)S(6)} %copy.7.swap_grp, f32[4,24,128]{2,1,0:T(8,128)S(1)} %get-tuple-element.31.scale, ...), custom_call_target="tpu_custom_call" | custom-call | flops 4194304 | bytes 2097152 | tf_op jit(solution)/shard_map/inner_0/pallas_call | solution.py:385
  11.5 0.0 collective-permute-done.6.refs_5_
  11.5 0.1 collective-permute-done.5.refs_3_
  11.6 0.0 collective-permute-done.4.refs_2_
  11.6 0.8 %finish_0.1 = (f32[2,384,128]{2,1,0:T(8,128)S(1)}, f32[3,24,256]{2,1,0:T(8,128)S(1)}, f32[3,24,256]{2,1,0:T(8,128)S(1)}, f32[2,24,256]{2,1,0:T(8,128)S(1)}, f32[...) custom-call(f32[6,24,128]{2,1,0:T(8,128)S(1)} %get-tuple-element.30.select, ...), custom_call_target="tpu_custom_call" | custom-call | flops 1048576 | bytes 1048576 | tf_op jit(solution)/shard_map/finish_0/pallas_call | solution.py:385
  12.4 0.1 collective-permute-start.7
  12.6 2.7 %collective-permute-start.8 = (f32[2,24,256]{2,1,0:T(8,128)S(1)}, f32[2,24,256]{2,1,0:T(8,128)S(1)}, u32[]{:S(2)}, u32[]{:S(2)}) collective-permute-start(f32[2,24,256]{2,1,0:T(8,128)S(1)} %get-tuple-element.52), channel_id=1, source_target_pairs={{0,8},{1,2},{2,1},{3,4},{4,3},{5,6},{6,5},{7,15},{8,0},{9,10},{10,... | collective-permute-start | bytes 147464 | tf_op jit(solution)/shard_map/ppermute | solution.py:52
  15.2 0.1 collective-permute-start.9
  15.3 1.0 %collective-permute-start.10 = (f32[24,256]{1,0:T(8,128)S(1)}, f32[24,256]{1,0:T(8,128)S(1)}, u32[]{:S(2)}, u32[]{:S(2)}) collective-permute-start(f32[24,256]{1,0:T(8,128)S(1)} %get-tuple-element.54), channel_id=1, source_target_pairs={{0,1},{1,0},{2,3},{3,2},{4,5},{5,4},{6,7},{7,6},{8,16},{9,17},{10,... | collective-permute-start | bytes 73736 | tf_op jit(solution)/shard_map/ppermute | solution.py:52
  16.4 0.5 %inner_1.1.partial = f32[2,384,128]{2,1,0:T(8,128)S(1)} custom-call(f32[2,384,128]{2,1,0:T(8,128)S(1)} %get-tuple-element.48.state, f32[4,24,128]{2,1,0:T(8,128)S(1)} %get-tuple-element.31.scale), custom_call_target="tpu_custom_call" | custom-call | flops 4194304 | bytes 2097152 | tf_op jit(solution)/shard_map/inner_1/pallas_call | solution.py:385
  16.8 2.2 %collective-permute-done.9.refs_4_ = f32[24,256]{1,0:T(8,128)S(1)} collective-permute-done((f32[24,256]{1,0:T(8,128)S(1)}, f32[24,256]{1,0:T(8,128)S(1)}, u32[]{:S(2)}, u32[]{:S(2)}) %collective-permute-start.9) | collective-permute-done | bytes 24608 | tf_op jit(solution)/shard_map/ppermute | solution.py:52
  19.1 0.0 collective-permute-done.10.refs_5_
  19.1 0.0 collective-permute-done.7.refs_2_
  19.1 0.0 collective-permute-done.8.refs_3_
  19.1 1.4 %finish_1.1 = f32[4,6,16,256]{3,2,1,0:T(8,128)} custom-call(f32[6,24,128]{2,1,0:T(8,128)S(1)} %get-tuple-element.30.select, f32[2,384,128]{2,1,0:T(8,128)S(1)} %inner_1.1.partial, f32[3,24,256]{2,1,0:T(8,128)S(1)} %get-tuple-element.49.refs_0_, f32[3,24,256]{2,1,0:T(8,128)S(1)} %get-tuple-element.50.refs_1_, ...), custom_call_target="tpu_custom_call" | custom-call | tf_op jit(solution)/shard_map/finish_1/pallas_call | solution.py:435
  (2 shorter events, 0.1 us)
Async XLA Ops:
  0.0 1.0 %copy-start = (f32[4,6,16,256]{3,2,1,0:T(8,128)S(1)}, f32[4,6,16,256]{3,2,1,0:T(8,128)}, u32[]{:S(2)}) copy-start(f32[4,6,16,256]{3,2,1,0:T(8,128)} %fields.5) | copy-start | bytes 1179652
  1.0 4.1 %copy-start.1 = (f32[4,6,16,256]{3,2,1,0:T(8,128)S(1)}, f32[4,6,16,256]{3,2,1,0:T(8,128)}, u32[]{:S(2)}) copy-start(f32[4,6,16,256]{3,2,1,0:T(8,128)} %fields.5) | copy-start | bytes 1179652
  1.3 5.9 %collective-permute-start.2 = (f32[2,24,256]{2,1,0:T(8,128)S(1)}, f32[2,24,256]{2,1,0:T(8,128)S(1)}, u32[]{:S(2)}, u32[]{:S(2)}) collective-permute-start(f32[2,24,256]{2,1,0:T(8,128)S(1)} %get-tuple-element.36), channel_id=1, source_target_pairs={{0,8},{1,9},{2,10},{3,11},{4,12},{5,13},{6,14},{7,15},{8,0},{9,1},... | collective-permute-start | bytes 147464 | tf_op jit(solution)/shard_map/ppermute | solution.py:52
  4.4 2.8 %collective-permute-start.3 = (f32[2,24,256]{2,1,0:T(8,128)S(1)}, f32[2,24,256]{2,1,0:T(8,128)S(1)}, u32[]{:S(2)}, u32[]{:S(2)}) collective-permute-start(f32[2,24,256]{2,1,0:T(8,128)S(1)} %get-tuple-element.37), channel_id=1, source_target_pairs={{0,1},{1,0},{2,3},{3,2},{4,5},{5,4},{6,7},{7,6},{8,9},{9,8},{10,11... | collective-permute-start | bytes 147464 | tf_op jit(solution)/shard_map/ppermute | solution.py:52
  5.1 1.3 %copy-start.2 = (s32[4,6]{1,0:T(4,128)S(1)}, s32[4,6]{1,0:T(4,128)}, u32[]{:S(2)}) copy-start(s32[4,6]{1,0:T(4,128)} %neighbors.1) | copy-start | bytes 292
  5.1 5.8 %collective-permute-start.1 = (f32[120,256]{1,0:T(8,128)S(1)}, f32[120,256]{1,0:T(8,128)S(1)}, u32[]{:S(2)}, u32[]{:S(2)}) collective-permute-start(f32[120,256]{1,0:T(8,128)S(1)} %get-tuple-element.35), channel_id=1, source_target_pairs={{0,8},{1,9},{2,10},{3,11},{4,12},{5,13},{6,14},{7,15},{8,0},{9,1},... | collective-permute-start | bytes 368648 | tf_op jit(solution)/shard_map/ppermute | solution.py:52
  5.3 1.2 %copy-start.3 = (s32[4]{0:T(128)S(1)}, s32[4]{0:T(128)}, u32[]{:S(2)}) copy-start(s32[4]{0:T(128)} %orient.1) | copy-start | bytes 52
  5.3 4.1 %collective-permute-start = (f32[96,256]{1,0:T(8,128)S(1)}, f32[96,256]{1,0:T(8,128)S(1)}, u32[]{:S(2)}, u32[]{:S(2)}) collective-permute-start(f32[96,256]{1,0:T(8,128)S(1)} %get-tuple-element.34), channel_id=1, source_target_pairs={{0,1},{1,0},{2,3},{3,2},{4,5},{5,4},{6,7},{7,6},{8,9},{9,8},{10,11... | collective-permute-start | bytes 294920 | tf_op jit(solution)/shard_map/ppermute | solution.py:52
  7.3 4.2 %collective-permute-start.4 = (f32[3,24,256]{2,1,0:T(8,128)S(1)}, f32[3,24,256]{2,1,0:T(8,128)S(1)}, u32[]{:S(2)}, u32[]{:S(2)}) collective-permute-start(f32[3,24,256]{2,1,0:T(8,128)S(1)} %get-tuple-element.41), channel_id=1, source_target_pairs={{0,1},{1,0},{2,3},{3,2},{4,5},{5,4},{6,7},{7,6},{8,9},{9,8},{10,11... | collective-permute-start | bytes 221192 | tf_op jit(solution)/shard_map/ppermute | solution.py:52
  7.4 4.2 %collective-permute-start.5 = (f32[2,24,256]{2,1,0:T(8,128)S(1)}, f32[2,24,256]{2,1,0:T(8,128)S(1)}, u32[]{:S(2)}, u32[]{:S(2)}) collective-permute-start(f32[2,24,256]{2,1,0:T(8,128)S(1)} %get-tuple-element.42), channel_id=1, source_target_pairs={{0,8},{1,2},{2,1},{3,4},{4,3},{5,6},{6,5},{7,15},{8,0},{9,10},{10,... | collective-permute-start | bytes 147464 | tf_op jit(solution)/shard_map/ppermute | solution.py:52
  9.3 2.2 %collective-permute-start.6 = (f32[24,256]{1,0:T(8,128)S(1)}, f32[24,256]{1,0:T(8,128)S(1)}, u32[]{:S(2)}, u32[]{:S(2)}) collective-permute-start(f32[24,256]{1,0:T(8,128)S(1)} %get-tuple-element.44), channel_id=1, source_target_pairs={{0,1},{1,0},{2,3},{3,2},{4,5},{5,4},{6,7},{7,6},{8,16},{9,17},{10,... | collective-permute-start | bytes 73736 | tf_op jit(solution)/shard_map/ppermute | solution.py:52
  12.4 6.7 %collective-permute-start.7 = (f32[2,24,256]{2,1,0:T(8,128)S(1)}, f32[2,24,256]{2,1,0:T(8,128)S(1)}, u32[]{:S(2)}, u32[]{:S(2)}) collective-permute-start(f32[2,24,256]{2,1,0:T(8,128)S(1)} %get-tuple-element.51), channel_id=1, source_target_pairs={{0,1},{1,0},{2,3},{3,2},{4,5},{5,4},{6,7},{7,6},{8,9},{9,8},{10,11... | collective-permute-start | bytes 147464 | tf_op jit(solution)/shard_map/ppermute | solution.py:52
  12.6 6.5 %collective-permute-start.8 = (f32[2,24,256]{2,1,0:T(8,128)S(1)}, f32[2,24,256]{2,1,0:T(8,128)S(1)}, u32[]{:S(2)}, u32[]{:S(2)}) collective-permute-start(f32[2,24,256]{2,1,0:T(8,128)S(1)} %get-tuple-element.52), channel_id=1, source_target_pairs={{0,8},{1,2},{2,1},{3,4},{4,3},{5,6},{6,5},{7,15},{8,0},{9,10},{10,... | collective-permute-start | bytes 147464 | tf_op jit(solution)/shard_map/ppermute | solution.py:52
  15.2 3.8 %collective-permute-start.9 = (f32[24,256]{1,0:T(8,128)S(1)}, f32[24,256]{1,0:T(8,128)S(1)}, u32[]{:S(2)}, u32[]{:S(2)}) collective-permute-start(f32[24,256]{1,0:T(8,128)S(1)} %get-tuple-element.53), channel_id=1, source_target_pairs={{0,8},{1,9},{2,10},{3,11},{4,12},{5,13},{6,14},{7,15},{8,0},{9,1},... | collective-permute-start | bytes 73736 | tf_op jit(solution)/shard_map/ppermute | solution.py:52
  15.3 3.8 %collective-permute-start.10 = (f32[24,256]{1,0:T(8,128)S(1)}, f32[24,256]{1,0:T(8,128)S(1)}, u32[]{:S(2)}, u32[]{:S(2)}) collective-permute-start(f32[24,256]{1,0:T(8,128)S(1)} %get-tuple-element.54), channel_id=1, source_target_pairs={{0,1},{1,0},{2,3},{3,2},{4,5},{5,4},{6,7},{7,6},{8,16},{9,17},{10,... | collective-permute-start | bytes 73736 | tf_op jit(solution)/shard_map/ppermute | solution.py:52

commit v3 on v2

--- a/solution.py
+++ b/solution.py
@@ -117,12 +117,11 @@
     deep_b[...] = jnp.where(even, low[2], high[2])
 
 
-def fill_state(state, blocks):
-    for slot, block in enumerate(blocks):
-        for f in range(NFIELD):
-            value = block(f)
-            for h in range(2):
-                state[h, pl.ds(f * SLOTS + slot, EDGE, stride=ROWS), :] = value[:, h * HALF : (h + 1) * HALF]
+def fill_slot(state, slot, block):
+    for f in range(NFIELD):
+        value = block(f)
+        for h in range(2):
+            state[h, pl.ds(f * SLOTS + slot, EDGE, stride=ROWS), :] = value[:, h * HALF : (h + 1) * HALF]
 
 
 def slot_rows():
@@ -150,33 +149,20 @@
     return lax.rem(lax.axis_index(axis), 2) == 0
 
 
-def pack_kernel(fields, low, high, faces_grp, faces_dev, state):
-    fill_state(state, [lambda f, slot=slot: fields[slot, f] for slot in range(SLOTS)])
-    packer = Packer()
-    for x in range(EDGE):
-        packer.add(x, *plane_at(state, x))
-    write_tables(packer, state, (low, high))
-    faces_grp[0] = gathered([low[0], high[0], low[1], high[1]], 0)
-    faces_grp[1] = jnp.where(even_place("grp"), high[2], low[2])
-    faces_dev[0] = gathered([low[0], high[0], low[1], high[1]], SLOTS - 1)
-    faces_dev[1] = gathered([low[2], high[2]], SLOTS - 1)
-
-
-def block_kernel(swap_dev, fields, low, high, to_dev, to_grp):
+def block_kernel(masks, fields, low, high, to_dev, to_grp):
     last, size = SLOTS - 1, NFIELD * EDGE
     for f in range(NFIELD):
         to_dev[f * EDGE : (f + 1) * EDGE] = fields[last, f]
         to_grp[f * EDGE : (f + 1) * EDGE] = fields[0, f]
     away = jnp.where(even_place("grp"), low[2], high[2])
-    to_grp[size : size + ROWS] = jnp.where(slot_rows() == 0, away, jnp.where(swap_dev[0] == 1, 1.0, 0.0))
-
-
-def faces_kernel(swap_dev, swap_grp, scale, low, high, faces, faces_dev, *outs):
-    del scale
-    new_low, new_high, flat_a, flat_b, deep_b = outs
+    to_grp[size : size + ROWS] = jnp.where(slot_rows() == 0, away, masks[0])
+
+
+def faces_kernel(masks, low, high, faces, faces_dev, *outs):
+    new_low, new_high, flat_a, flat_b, deep_b, relay = outs
     rows, last = slot_rows(), SLOTS - 1
-    first_rows = (rows == 0) & (swap_grp[0] == 1)
-    last_rows = (rows == last) & (swap_dev[0] == 1)
+    first_rows = (rows == 0) & (masks[1] > 0.5)
+    last_rows = (rows == last) & (masks[0] > 0.5)
     even = even_place("grp")
     got_first, got_last, got_last_z = faces[0], faces_dev[0], faces_dev[1]
     for side, (raw, new) in enumerate(((low, new_low), (high, new_high))):
@@ -190,7 +176,7 @@
     for axis in range(2):
         flat_a[axis] = jnp.where(even_dev, new_high[axis], new_low[axis])
         flat_b[axis] = jnp.where(even_dev, new_low[axis], new_high[axis])
-    flat_a[2] = faces[1]
+    relay[...] = faces[1]
     deep_b[...] = jnp.where(even, new_low[2], new_high[2])
 
 
@@ -232,24 +218,50 @@
         select[face] = jnp.where(column == by_slot(first) + field * SLOTS, weights[face // 2], 0.0)
 
 
-def first_inner_kernel(swap_dev, swap_grp, scale, fields, block_dev, block_grp, faces, low, high, new_low, new_high, *refs):
+def start_kernel(fields, neighbors, orient, *refs):
+    fetched, low, high, faces_grp, faces_dev, scale, select = refs[:7]
+    state, near, turn, arrived = refs[7:]
+    scalars = ((neighbors, near), (orient, turn))
+    blocks = tuple((fields.at[slot], fetched.at[slot]) for slot in range(SLOTS))
+    copies = [pltpu.make_async_copy(*pair, arrived.at[number]) for number, pair in enumerate((*scalars, *blocks))]
+    for copy in copies:
+        copy.start()
+    for copy in copies[: len(scalars)]:
+        copy.wait()
+    plan_kernel(near, turn, scale, select)
+    for slot in range(SLOTS):
+        copies[len(scalars) + slot].wait()
+        fill_slot(state, slot, lambda f: fetched[slot, f])
+    packer = Packer()
+    for x in range(EDGE):
+        packer.add(x, *plane_at(state, x))
+    write_tables(packer, state, (low, high))
+    faces_grp[0] = gathered([low[0], high[0], low[1], high[1]], 0)
+    faces_grp[1] = jnp.where(even_place("grp"), high[2], low[2])
+    faces_dev[0] = gathered([low[0], high[0], low[1], high[1]], SLOTS - 1)
+    faces_dev[1] = gathered([low[2], high[2]], SLOTS - 1)
+
+
+def first_inner_kernel(masks, scale, fields, block_dev, block_grp, faces, low, high, new_low, new_high, *refs):
     partial, got_deep, relayed, z_low, z_high, state = refs
     size = NFIELD * EDGE
+    swap_dev, swap_grp = masks[0] > 0.5, masks[1] > 0.5
 
     def block(slot):
         def of(f):
             value = fields[slot, f]
             if slot == 0:
-                value = jnp.where(swap_grp[0] == 1, block_grp[f * EDGE : (f + 1) * EDGE], value)
+                value = jnp.where(swap_grp[:EDGE], block_grp[f * EDGE : (f + 1) * EDGE], value)
             if slot == SLOTS - 1:
-                value = jnp.where(swap_dev[0] == 1, block_dev[f * EDGE : (f + 1) * EDGE], value)
+                value = jnp.where(swap_dev[:EDGE], block_dev[f * EDGE : (f + 1) * EDGE], value)
             return value
 
         return of
 
-    fill_state(state, [block(slot) for slot in range(SLOTS)])
+    for slot in range(SLOTS):
+        fill_slot(state, slot, block(slot))
     rows, even = slot_rows(), even_place("grp")
-    first_rows = (rows == 0) & (swap_grp[0] == 1)
+    first_rows = (rows == 0) & swap_grp
     got_deep[...] = jnp.where(first_rows, jnp.where(even, low[2], high[2]), faces[1])
     other = block_grp[size : size + ROWS]
     relayed[...] = jnp.where(rows == SLOTS - 1, jnp.broadcast_to(other[1:2], FACE), 0.0)
@@ -298,16 +310,16 @@
 
 
 def finish_kernel(last_step, select, partial, *refs):
-    own, got_flat = refs[0:2], refs[2:4]
+    own, got_flat = refs[0:2], (refs[3], refs[2])
     own_deep = [ref[2] for ref in own]
     if last_step:
         got_deep = [ref[...] for ref in refs[4:6]]
         result, done, blocks, sent = refs[6:10]
     else:
-        known, deep_b, relayed, z_low, z_high = refs[4:9]
-        got_deep = [jnp.where(relayed[...] > 0.5, got_flat[0][2], known[...]), deep_b[...]]
+        known, deep_b, relay, relayed, z_low, z_high = refs[4:10]
+        got_deep = [jnp.where(relayed[...] > 0.5, relay[...], known[...]), deep_b[...]]
         own_deep = [z_low[...], z_high[...]]
-        done, outs, sends = refs[9], refs[10:12], refs[12:16]
+        done, outs, sends = refs[10], refs[11:13], refs[13:17]
     ghosts = []
     for face in range(6):
         axis, side = face // 2, face % 2
@@ -365,7 +377,7 @@
     return pl.BlockSpec(memory_space=space)
 
 
-VECTOR, SCALAR = pltpu.VMEM, pltpu.SMEM
+VECTOR = pltpu.VMEM
 SMALL = pltpu.CompilerParams(vmem_limit_bytes=8 << 20)
 FLAT = (2, ROWS, PLANE)
 TABLES = (STATE, SIDE, SIDE, FLAT, FLAT, FACE, FACE)
@@ -381,57 +393,77 @@
     return pl.CostEstimate(flops=flops, bytes_accessed=min(flops, 2 << 20), transcendentals=0)
 
 
-def call(kernel, name, shapes, scalars, vectors, flops=1 << 20, scratch=()):
+def call(kernel, name, shapes, vectors, flops=1 << 20, scratch=()):
     return pl.pallas_call(
         kernel,
         name=name,
         compiler_params=SMALL,
         out_shape=[shaped(shape) for shape in shapes],
-        in_specs=[spec(SCALAR)] * len(scalars) + [spec(VECTOR)] * len(vectors),
+        in_specs=[spec(VECTOR)] * len(vectors),
         out_specs=[spec(VECTOR)] * len(shapes),
         scratch_shapes=list(scratch),
         cost_estimate=cost(flops),
-    )(*scalars, *vectors)
+    )(*vectors)
+
+
+def start(arguments):
+    shapes = (arguments[0].shape, SIDE, SIDE, FLAT, FLAT, (4, ROWS, HALF), (6, ROWS, HALF))
+    return pl.pallas_call(
+        start_kernel,
+        name="start",
+        compiler_params=SMALL,
+        out_shape=[shaped(shape) for shape in shapes],
+        in_specs=[spec(pl.ANY)] * len(arguments),
+        out_specs=[spec(VECTOR)] * len(shapes),
+        scratch_shapes=[
+            pltpu.VMEM(STATE, jnp.float32),
+            *(pltpu.SMEM(array.shape, jnp.int32) for array in arguments[1:]),
+            pltpu.SemaphoreType.DMA((len(arguments) - 1 + SLOTS,)),
+        ],
+    )(*(pltpu.with_memory_space_constraint(array, pltpu.HBM) for array in arguments))
 
 
 def body(fields, swap_dev, swap_grp, neighbors, orient):
-    state = pltpu.VMEM(STATE, jnp.float32)
-    low, high, faces, faces_dev = call(pack_kernel, "pack", [SIDE, SIDE, FLAT, FLAT], [], [fields], scratch=[state])
+    fields, low, high, faces, faces_dev, scale, select = start((fields, neighbors, orient))
+    swap_dev, swap_grp, faces = lax.optimization_barrier((swap_dev, swap_grp, faces))
+    flags = jnp.concatenate([swap_dev, swap_grp])
+    masks = jnp.broadcast_to(jnp.where(flags == 1, 1.0, 0.0).reshape(2, 1, 1), (2, *FACE))
     faces = exchange(faces, "grp", 0)
     faces_dev = exchange(faces_dev, "dev", 0)
-    to_dev, to_grp = call(block_kernel, "blocks", [TO_DEV, TO_GRP], [swap_dev], [fields, low, high], 1 << 24)
+    to_dev, to_grp = call(block_kernel, "blocks", [TO_DEV, TO_GRP], [masks, fields, low, high], 1 << 30)
     block_grp = exchange(to_grp, "grp", 0)
     block_dev = exchange(to_dev, "dev", 0)
-    scale, select = call(plan_kernel, "plan", [(4, ROWS, HALF), (6, ROWS, HALF)], [neighbors, orient], [], 0)
     new_low, new_high, *sends = call(
         faces_kernel,
         "faces",
-        [SIDE, SIDE, SIDE, FLAT, FACE],
-        [swap_dev, swap_grp],
-        [scale, low, high, faces, faces_dev],
-        1 << 24,
+        [SIDE, SIDE, FLAT, FLAT, FACE, FACE],
+        [masks, low, high, faces, faces_dev],
+        1 << 30,
     )
-    got_flat = [exchange(sends[number], "dev", number) for number in range(2)]
-    got_b = exchange(sends[2], "grp", 1)
-    partial, got_a, relayed, z_low, z_high = call(
+    flat_b = exchange(sends[1], "dev", 1)
+    deep_b = exchange(sends[2], "grp", 1)
+    flat_a = exchange(sends[0], "dev", 0)
+    relay = exchange(sends[3], "dev", 0)
+    partial, deep_a, relayed, z_low, z_high = call(
         first_inner_kernel,
         "inner_0",
         [STATE, FACE, FACE, FACE, FACE],
-        [swap_dev, swap_grp],
-        [scale, fields, block_dev, block_grp, faces, low, high, new_low, new_high],
+        [masks, scale, fields, block_dev, block_grp, faces, low, high, new_low, new_high],
         4 << 20,
-        [state],
+        [pltpu.VMEM(STATE, jnp.float32)],
     )
     state, *tables = call(
         functools.partial(finish_kernel, False),
         "finish_0",
         TABLES,
-        [],
-        [select, partial, new_low, new_high, *got_flat, got_a, got_b, relayed, z_low, z_high],
+        [select, partial, new_low, new_high, flat_b, flat_a, deep_a, deep_b, relay, relayed, z_low, z_high],
     )
     own, sends = tables[:2], tables[2:]
-    got = [exchange(sends[number], "dev" if number < 2 else "grp", number % 2) for number in range(4)]
-    (partial,) = call(inner_kernel, "inner_1", [STATE], [], [state, scale], 4 << 20)
+    flat_b = exchange(sends[1], "dev", 1)
+    deep_a = exchange(sends[2], "grp", 0)
+    deep_b = exchange(sends[3], "grp", 1)
+    flat_a = exchange(sends[0], "dev", 0)
+    (partial,) = call(inner_kernel, "inner_1", [STATE], [state, scale], 4 << 20)
     return pl.pallas_call(
         functools.partial(finish_kernel, True),
         name="finish_1",
@@ -444,7 +476,7 @@
             pltpu.VMEM(fields.shape, jnp.float32),
             pltpu.SemaphoreType.DMA((2,)),
         ],
-    )(select, partial, *own, *got)
+    )(select, partial, *own, flat_b, flat_a, deep_a, deep_b)
 
 
 def solution(mesh):

time: 20.7 us -> 20.5 us (level)
  local copies, waits for them, and re-layouts: 1.01 us -> 0.07 us
  waiting for transfers between devices: 3.89 us -> 4.36 us
  Pallas kernels: 4.45 us -> 4.73 us
    pallas_call x0 -> x1, Pallas kernels: none -> 1.39 us  [start(): pl.pallas_call(start_kernel, name='start', compiler_params=SMALL, out_sha...]
    pallas_call x7 -> x5, Pallas kernels: 3.04 us -> 1.93 us  [call(): pl.pallas_call(kernel, name=name, compiler_params=SMALL, out_shape=[shape...]
    unnamed x8 -> x0, local copies, waits for them, and re-layouts: 1.01 us -> none
    ppermute x11 -> x12, waiting for transfers between devices: 3.89 us -> 4.36 us  [exchange(): return lax.ppermute(block, ('grp', 'dev'), partners(axis, offset))]
    ppermute x11 -> x12, starting transfers between devices: 9.73 us -> 9.65 us  [exchange(): return lax.ppermute(block, ('grp', 'dev'), partners(axis, offset))]
  transfers between devices with their start and end apart: 11 -> 12, of which waited for: 3 -> 2; matrix products, arithmetic and copies ran while one was open for 0% -> 1% of each run, Pallas kernels for 9% -> 5%
where the time goes in v3:
time: 20.5 us; the launch traced here: 20.3 us
  starting transfers between devices  9.65 us (47%)
  Pallas kernels  4.73 us (23%)
  waiting for transfers between devices  4.36 us (21%)
  between operations  1.37 us (7%)
    ppermute x12, starting transfers between devices, exchange(): return lax.ppermute(block, ('grp', 'dev'), partners(axis, offset))  9.65 us
    ppermute x12, waiting for transfers between devices, exchange(): return lax.ppermute(block, ('grp', 'dev'), partners(axis, offset))  4.36 us
    pallas_call x5, Pallas kernels, call(): pl.pallas_call(kernel, name=name, compiler_params=SMALL, out_shape=[shape...  1.93 us
    pallas_call x1, Pallas kernels, body(): pl.pallas_call(functools.partial(finish_kernel, True), name='finish_1', c...  1.41 us
    pallas_call x1, Pallas kernels, start(): pl.pallas_call(start_kernel, name='start', compiler_params=SMALL, out_sha...  1.39 us
  transfers between devices with their start and end apart: 12, of which 2 were waited for; matrix products, arithmetic and copies ran while one was open for 1% of the time, Pallas kernels for 5%

profile of v3, /device:TPU:0, one launch (start us, length us, event | category | flops | bytes accessed | tf_op | source)
XLA Modules:
  0.0 20.3 jit_solution(17484394087047995394)
XLA Ops:
  0.0 1.4 %start.1 = (f32[4,6,16,256]{3,2,1,0:T(8,128)S(1)}, f32[3,24,256]{2,1,0:T(8,128)S(1)}, f32[3,24,256]{2,1,0:T(8,128)S(1)}, f32[2,24,256]{2,1,0:T(8,128)S(1)}, f32[...) custom-call(f32[4,6,16,256]{3,2,1,0:T(8,128)} %fields.1, s32[4,6]{1,0:T(4,128)} %neighbors.1, ...), custom_call_target="tpu_custom_call" | custom-call | tf_op jit(solution)/shard_map/start/pallas_call | solution.py:411
  1.4 3.1 %collective-permute-start.2 = (f32[2,24,256]{2,1,0:T(8,128)S(1)}, f32[2,24,256]{2,1,0:T(8,128)S(1)}, u32[]{:S(2)}, u32[]{:S(2)}) collective-permute-start(f32[2,24,256]{2,1,0:T(8,128)S(1)} %get-tuple-element.45), channel_id=1, source_target_pairs={{0,8},{1,9},{2,10},{3,11},{4,12},{5,13},{6,14},{7,15},{8,0},{9,1},... | collective-permute-start | bytes 147464 | tf_op jit(solution)/shard_map/ppermute | solution.py:52
  4.5 0.0 collective-permute-start.3
  5.8 0.1 compare_select_fusion
  5.9 0.1 broadcast_in_dim.15.masks
  6.0 0.6 %collective-permute-start = (f32[96,256]{1,0:T(8,128)S(1)}, f32[96,256]{1,0:T(8,128)S(1)}, u32[]{:S(2)}, u32[]{:S(2)}) collective-permute-start(f32[96,256]{1,0:T(8,128)S(1)} %get-tuple-element.43), channel_id=1, source_target_pairs={{0,1},{1,0},{2,3},{3,2},{4,5},{5,4},{6,7},{7,6},{8,9},{9,8},{10,11... | collective-permute-start | bytes 294920 | tf_op jit(solution)/shard_map/ppermute | solution.py:52
  6.5 0.1 collective-permute-start.1
  6.6 0.0 collective-permute-done.2.faces
  6.6 0.0 collective-permute-done.3.faces_dev
  6.6 0.1 faces.1
  6.7 2.0 %collective-permute-start.4 = (f32[2,24,256]{2,1,0:T(8,128)S(1)}, f32[2,24,256]{2,1,0:T(8,128)S(1)}, u32[]{:S(2)}, u32[]{:S(2)}) collective-permute-start(f32[2,24,256]{2,1,0:T(8,128)S(1)} %get-tuple-element.50), channel_id=1, source_target_pairs={{0,8},{1,2},{2,1},{3,4},{4,3},{5,6},{6,5},{7,15},{8,0},{9,10},{10,... | collective-permute-start | bytes 147464 | tf_op jit(solution)/shard_map/ppermute | solution.py:52
  8.7 0.0 collective-permute-start.5
  8.7 0.5 %collective-permute-start.6 = (f32[24,256]{1,0:T(8,128)S(1)}, f32[24,256]{1,0:T(8,128)S(1)}, u32[]{:S(2)}, u32[]{:S(2)}) collective-permute-start(f32[24,256]{1,0:T(8,128)S(1)} %get-tuple-element.53), channel_id=1, source_target_pairs={{0,1},{1,0},{2,3},{3,2},{4,5},{5,4},{6,7},{7,6},{8,16},{9,17},{10,... | collective-permute-start | bytes 73736 | tf_op jit(solution)/shard_map/ppermute | solution.py:52
  9.2 0.0 collective-permute-done.block_dev
  9.2 0.0 collective-permute-start.7
  9.2 2.6 %collective-permute-done.1.block_grp = f32[120,256]{1,0:T(8,128)S(1)} collective-permute-done((f32[120,256]{1,0:T(8,128)S(1)}, f32[120,256]{1,0:T(8,128)S(1)}, u32[]{:S(2)}, u32[]{:S(2)}) %collective-permute-start.1) | collective-permute-done | bytes 122912 | tf_op jit(solution)/shard_map/ppermute | solution.py:52
  11.8 0.6 %inner_0.1 = (f32[2,384,128]{2,1,0:T(8,128)S(1)}, f32[24,256]{1,0:T(8,128)S(1)}, f32[24,256]{1,0:T(8,128)S(1)}, f32[24,256]{1,0:T(8,128)S(1)}, f32[24,256]{1,0:T(8,128)S(1)}) custom-call(f32[2,24,256]{2,1,0:T(8,128)S(1)} %broadcast_in_dim.15.masks, f32[4,24,128]{2,1,0:T(8,128)S(1)} %get-tuple-element.39.scale, ...), custom_call_target="tpu_custom_call" | custom-call | flops 4194304 | bytes 2097152 | tf_op jit(solution)/shard_map/inner_0/pallas_call | solution.py:397
  12.4 0.0 collective-permute-done.6.refs_5_
  12.4 0.0 collective-permute-done.7.refs_6_
  12.4 0.0 collective-permute-done.4.refs_2_
  12.4 0.0 collective-permute-done.5.refs_3_
  12.4 0.8 %finish_0.1 = (f32[2,384,128]{2,1,0:T(8,128)S(1)}, f32[3,24,256]{2,1,0:T(8,128)S(1)}, f32[3,24,256]{2,1,0:T(8,128)S(1)}, f32[2,24,256]{2,1,0:T(8,128)S(1)}, f32[...) custom-call(f32[6,24,128]{2,1,0:T(8,128)S(1)} %get-tuple-element.35.select, ...), custom_call_target="tpu_custom_call" | custom-call | flops 1048576 | bytes 1048576 | tf_op jit(solution)/shard_map/finish_0/pallas_call | solution.py:397
  13.3 1.7 %collective-permute-start.8 = (f32[2,24,256]{2,1,0:T(8,128)S(1)}, f32[2,24,256]{2,1,0:T(8,128)S(1)}, u32[]{:S(2)}, u32[]{:S(2)}) collective-permute-start(f32[2,24,256]{2,1,0:T(8,128)S(1)} %get-tuple-element.61), channel_id=1, source_target_pairs={{0,8},{1,2},{2,1},{3,4},{4,3},{5,6},{6,5},{7,15},{8,0},{9,10},{10,... | collective-permute-start | bytes 147464 | tf_op jit(solution)/shard_map/ppermute | solution.py:52
  15.0 0.0 collective-permute-start.9
  15.0 1.6 %collective-permute-start.10 = (f32[24,256]{1,0:T(8,128)S(1)}, f32[24,256]{1,0:T(8,128)S(1)}, u32[]{:S(2)}, u32[]{:S(2)}) collective-permute-start(f32[24,256]{1,0:T(8,128)S(1)} %get-tuple-element.63), channel_id=1, source_target_pairs={{0,8},{1,9},{2,10},{3,11},{4,12},{5,13},{6,14},{7,15},{8,0},{9,1},... | collective-permute-start | bytes 73736 | tf_op jit(solution)/shard_map/ppermute | solution.py:52
  16.6 0.0 collective-permute-start.11
  16.6 0.5 %inner_1.1.partial = f32[2,384,128]{2,1,0:T(8,128)S(1)} custom-call(f32[2,384,128]{2,1,0:T(8,128)S(1)} %get-tuple-element.58.state, f32[4,24,128]{2,1,0:T(8,128)S(1)} %get-tuple-element.39.scale), custom_call_target="tpu_custom_call" | custom-call | flops 4194304 | bytes 2097152 | tf_op jit(solution)/shard_map/inner_1/pallas_call | solution.py:397
  17.1 1.7 %collective-permute-done.10.refs_4_ = f32[24,256]{1,0:T(8,128)S(1)} collective-permute-done((f32[24,256]{1,0:T(8,128)S(1)}, f32[24,256]{1,0:T(8,128)S(1)}, u32[]{:S(2)}, u32[]{:S(2)}) %collective-permute-start.10) | collective-permute-done | bytes 24608 | tf_op jit(solution)/shard_map/ppermute | solution.py:52
  18.8 0.0 collective-permute-done.11.refs_5_
  18.8 0.0 collective-permute-done.8.refs_2_
  18.9 0.0 collective-permute-done.9.refs_3_
  18.9 1.4 %finish_1.1 = f32[4,6,16,256]{3,2,1,0:T(8,128)} custom-call(f32[6,24,128]{2,1,0:T(8,128)S(1)} %get-tuple-element.35.select, f32[2,384,128]{2,1,0:T(8,128)S(1)} %inner_1.1.partial, f32[3,24,256]{2,1,0:T(8,128)S(1)} %get-tuple-element.59.refs_0_, f32[3,24,256]{2,1,0:T(8,128)S(1)} %get-tuple-element.60.refs_1_, ...), custom_call_target="tpu_custom_call" | custom-call | tf_op jit(solution)/shard_map/finish_1/pallas_call | solution.py:467
  (1 shorter events, 0.0 us)
Async XLA Ops:
  1.4 5.2 %collective-permute-start.2 = (f32[2,24,256]{2,1,0:T(8,128)S(1)}, f32[2,24,256]{2,1,0:T(8,128)S(1)}, u32[]{:S(2)}, u32[]{:S(2)}) collective-permute-start(f32[2,24,256]{2,1,0:T(8,128)S(1)} %get-tuple-element.45), channel_id=1, source_target_pairs={{0,8},{1,9},{2,10},{3,11},{4,12},{5,13},{6,14},{7,15},{8,0},{9,1},... | collective-permute-start | bytes 147464 | tf_op jit(solution)/shard_map/ppermute | solution.py:52
  4.5 2.1 %collective-permute-start.3 = (f32[2,24,256]{2,1,0:T(8,128)S(1)}, f32[2,24,256]{2,1,0:T(8,128)S(1)}, u32[]{:S(2)}, u32[]{:S(2)}) collective-permute-start(f32[2,24,256]{2,1,0:T(8,128)S(1)} %get-tuple-element.46), channel_id=1, source_target_pairs={{0,1},{1,0},{2,3},{3,2},{4,5},{5,4},{6,7},{7,6},{8,9},{9,8},{10,11... | collective-permute-start | bytes 147464 | tf_op jit(solution)/shard_map/ppermute | solution.py:52
  6.0 3.2 %collective-permute-start = (f32[96,256]{1,0:T(8,128)S(1)}, f32[96,256]{1,0:T(8,128)S(1)}, u32[]{:S(2)}, u32[]{:S(2)}) collective-permute-start(f32[96,256]{1,0:T(8,128)S(1)} %get-tuple-element.43), channel_id=1, source_target_pairs={{0,1},{1,0},{2,3},{3,2},{4,5},{5,4},{6,7},{7,6},{8,9},{9,8},{10,11... | collective-permute-start | bytes 294920 | tf_op jit(solution)/shard_map/ppermute | solution.py:52
  6.5 5.3 %collective-permute-start.1 = (f32[120,256]{1,0:T(8,128)S(1)}, f32[120,256]{1,0:T(8,128)S(1)}, u32[]{:S(2)}, u32[]{:S(2)}) collective-permute-start(f32[120,256]{1,0:T(8,128)S(1)} %get-tuple-element.44), channel_id=1, source_target_pairs={{0,8},{1,9},{2,10},{3,11},{4,12},{5,13},{6,14},{7,15},{8,0},{9,1},... | collective-permute-start | bytes 368648 | tf_op jit(solution)/shard_map/ppermute | solution.py:52
  6.7 5.7 %collective-permute-start.4 = (f32[2,24,256]{2,1,0:T(8,128)S(1)}, f32[2,24,256]{2,1,0:T(8,128)S(1)}, u32[]{:S(2)}, u32[]{:S(2)}) collective-permute-start(f32[2,24,256]{2,1,0:T(8,128)S(1)} %get-tuple-element.50), channel_id=1, source_target_pairs={{0,8},{1,2},{2,1},{3,4},{4,3},{5,6},{6,5},{7,15},{8,0},{9,10},{10,... | collective-permute-start | bytes 147464 | tf_op jit(solution)/shard_map/ppermute | solution.py:52
  8.7 3.7 %collective-permute-start.5 = (f32[2,24,256]{2,1,0:T(8,128)S(1)}, f32[2,24,256]{2,1,0:T(8,128)S(1)}, u32[]{:S(2)}, u32[]{:S(2)}) collective-permute-start(f32[2,24,256]{2,1,0:T(8,128)S(1)} %get-tuple-element.51), channel_id=1, source_target_pairs={{0,1},{1,0},{2,3},{3,2},{4,5},{5,4},{6,7},{7,6},{8,9},{9,8},{10,11... | collective-permute-start | bytes 147464 | tf_op jit(solution)/shard_map/ppermute | solution.py:52
  8.7 3.7 %collective-permute-start.6 = (f32[24,256]{1,0:T(8,128)S(1)}, f32[24,256]{1,0:T(8,128)S(1)}, u32[]{:S(2)}, u32[]{:S(2)}) collective-permute-start(f32[24,256]{1,0:T(8,128)S(1)} %get-tuple-element.53), channel_id=1, source_target_pairs={{0,1},{1,0},{2,3},{3,2},{4,5},{5,4},{6,7},{7,6},{8,16},{9,17},{10,... | collective-permute-start | bytes 73736 | tf_op jit(solution)/shard_map/ppermute | solution.py:52
  9.2 3.2 %collective-permute-start.7 = (f32[24,256]{1,0:T(8,128)S(1)}, f32[24,256]{1,0:T(8,128)S(1)}, u32[]{:S(2)}, u32[]{:S(2)}) collective-permute-start(f32[24,256]{1,0:T(8,128)S(1)} %get-tuple-element.54), channel_id=1, source_target_pairs={{0,1},{1,0},{2,3},{3,2},{4,5},{5,4},{6,7},{7,6},{8,9},{9,8},{10,11... | collective-permute-start | bytes 73736 | tf_op jit(solution)/shard_map/ppermute | solution.py:52
  13.3 5.6 %collective-permute-start.8 = (f32[2,24,256]{2,1,0:T(8,128)S(1)}, f32[2,24,256]{2,1,0:T(8,128)S(1)}, u32[]{:S(2)}, u32[]{:S(2)}) collective-permute-start(f32[2,24,256]{2,1,0:T(8,128)S(1)} %get-tuple-element.61), channel_id=1, source_target_pairs={{0,8},{1,2},{2,1},{3,4},{4,3},{5,6},{6,5},{7,15},{8,0},{9,10},{10,... | collective-permute-start | bytes 147464 | tf_op jit(solution)/shard_map/ppermute | solution.py:52
  15.0 3.8 %collective-permute-start.9 = (f32[2,24,256]{2,1,0:T(8,128)S(1)}, f32[2,24,256]{2,1,0:T(8,128)S(1)}, u32[]{:S(2)}, u32[]{:S(2)}) collective-permute-start(f32[2,24,256]{2,1,0:T(8,128)S(1)} %get-tuple-element.62), channel_id=1, source_target_pairs={{0,1},{1,0},{2,3},{3,2},{4,5},{5,4},{6,7},{7,6},{8,9},{9,8},{10,11... | collective-permute-start | bytes 147464 | tf_op jit(solution)/shard_map/ppermute | solution.py:52
  15.0 3.8 %collective-permute-start.10 = (f32[24,256]{1,0:T(8,128)S(1)}, f32[24,256]{1,0:T(8,128)S(1)}, u32[]{:S(2)}, u32[]{:S(2)}) collective-permute-start(f32[24,256]{1,0:T(8,128)S(1)} %get-tuple-element.63), channel_id=1, source_target_pairs={{0,8},{1,9},{2,10},{3,11},{4,12},{5,13},{6,14},{7,15},{8,0},{9,1},... | collective-permute-start | bytes 73736 | tf_op jit(solution)/shard_map/ppermute | solution.py:52
  16.6 2.2 %collective-permute-start.11 = (f32[24,256]{1,0:T(8,128)S(1)}, f32[24,256]{1,0:T(8,128)S(1)}, u32[]{:S(2)}, u32[]{:S(2)}) collective-permute-start(f32[24,256]{1,0:T(8,128)S(1)} %get-tuple-element.64), channel_id=1, source_target_pairs={{0,1},{1,0},{2,3},{3,2},{4,5},{5,4},{6,7},{7,6},{8,16},{9,17},{10,... | collective-permute-start | bytes 73736 | tf_op jit(solution)/shard_map/ppermute | solution.py:52

commit v4 on v3

--- a/solution.py
+++ b/solution.py
@@ -159,7 +159,7 @@
 
 
 def faces_kernel(masks, low, high, faces, faces_dev, *outs):
-    new_low, new_high, flat_a, flat_b, deep_b, relay = outs
+    new_low, new_high, flat_a, flat_b, deep_b = outs
     rows, last = slot_rows(), SLOTS - 1
     first_rows = (rows == 0) & (masks[1] > 0.5)
     last_rows = (rows == last) & (masks[0] > 0.5)
@@ -176,7 +176,7 @@
     for axis in range(2):
         flat_a[axis] = jnp.where(even_dev, new_high[axis], new_low[axis])
         flat_b[axis] = jnp.where(even_dev, new_low[axis], new_high[axis])
-    relay[...] = faces[1]
+    flat_a[2] = faces[1]
     deep_b[...] = jnp.where(even, new_low[2], new_high[2])
 
 
@@ -310,16 +310,16 @@
 
 
 def finish_kernel(last_step, select, partial, *refs):
-    own, got_flat = refs[0:2], (refs[3], refs[2])
+    own, got_flat = refs[0:2], refs[2:4]
     own_deep = [ref[2] for ref in own]
     if last_step:
         got_deep = [ref[...] for ref in refs[4:6]]
         result, done, blocks, sent = refs[6:10]
     else:
-        known, deep_b, relay, relayed, z_low, z_high = refs[4:10]
-        got_deep = [jnp.where(relayed[...] > 0.5, relay[...], known[...]), deep_b[...]]
+        known, deep_b, relayed, z_low, z_high = refs[4:9]
+        got_deep = [jnp.where(relayed[...] > 0.5, got_flat[0][2], known[...]), deep_b[...]]
         own_deep = [z_low[...], z_high[...]]
-        done, outs, sends = refs[10], refs[11:13], refs[13:17]
+        done, outs, sends = refs[9], refs[10:12], refs[12:16]
     ghosts = []
     for face in range(6):
         axis, side = face // 2, face % 2
@@ -430,20 +430,19 @@
     masks = jnp.broadcast_to(jnp.where(flags == 1, 1.0, 0.0).reshape(2, 1, 1), (2, *FACE))
     faces = exchange(faces, "grp", 0)
     faces_dev = exchange(faces_dev, "dev", 0)
-    to_dev, to_grp = call(block_kernel, "blocks", [TO_DEV, TO_GRP], [masks, fields, low, high], 1 << 30)
+    to_dev, to_grp = call(block_kernel, "blocks", [TO_DEV, TO_GRP], [masks, fields, low, high], 1 << 24)
     block_grp = exchange(to_grp, "grp", 0)
     block_dev = exchange(to_dev, "dev", 0)
     new_low, new_high, *sends = call(
         faces_kernel,
         "faces",
-        [SIDE, SIDE, FLAT, FLAT, FACE, FACE],
+        [SIDE, SIDE, SIDE, FLAT, FACE],
         [masks, low, high, faces, faces_dev],
-        1 << 30,
+        1 << 24,
     )
+    flat_a = exchange(sends[0], "dev", 0)
     flat_b = exchange(sends[1], "dev", 1)
     deep_b = exchange(sends[2], "grp", 1)
-    flat_a = exchange(sends[0], "dev", 0)
-    relay = exchange(sends[3], "dev", 0)
     partial, deep_a, relayed, z_low, z_high = call(
         first_inner_kernel,
         "inner_0",
@@ -456,13 +455,13 @@
         functools.partial(finish_kernel, False),
         "finish_0",
         TABLES,
-        [select, partial, new_low, new_high, flat_b, flat_a, deep_a, deep_b, relay, relayed, z_low, z_high],
+        [select, partial, new_low, new_high, flat_a, flat_b, deep_a, deep_b, relayed, z_low, z_high],
     )
     own, sends = tables[:2], tables[2:]
+    flat_a = exchange(sends[0], "dev", 0)
     flat_b = exchange(sends[1], "dev", 1)
     deep_a = exchange(sends[2], "grp", 0)
     deep_b = exchange(sends[3], "grp", 1)
-    flat_a = exchange(sends[0], "dev", 0)
     (partial,) = call(inner_kernel, "inner_1", [STATE], [state, scale], 4 << 20)
     return pl.pallas_call(
         functools.partial(finish_kernel, True),
@@ -476,7 +475,7 @@
             pltpu.VMEM(fields.shape, jnp.float32),
             pltpu.SemaphoreType.DMA((2,)),
         ],
-    )(select, partial, *own, flat_b, flat_a, deep_a, deep_b)
+    )(select, partial, *own, flat_a, flat_b, deep_a, deep_b)
 
 
 def solution(mesh):

time: 20.5 us -> 20.1 us (0.980)
  starting transfers between devices: 9.65 us -> 8.49 us
  waiting for transfers between devices: 4.36 us -> 5.19 us
    ppermute x12 -> x11, starting transfers between devices: 9.65 us -> 8.49 us  [exchange(): return lax.ppermute(block, ('grp', 'dev'), partners(axis, offset))]
    ppermute x12 -> x11, waiting for transfers between devices: 4.36 us -> 5.19 us  [exchange(): return lax.ppermute(block, ('grp', 'dev'), partners(axis, offset))]
  transfers between devices with their start and end apart: 12 -> 11, of which waited for: 2 -> 2; matrix products, arithmetic and copies ran while one was open for 1% -> 1% of each run, Pallas kernels for 5% -> 6%
where the time goes in v4:
time: 20.1 us; the launch traced here: 19.9 us
  starting transfers between devices  8.49 us (42%)
  waiting for transfers between devices  5.19 us (26%)
  Pallas kernels  4.73 us (24%)
  between operations  1.37 us (7%)
    ppermute x11, starting transfers between devices, exchange(): return lax.ppermute(block, ('grp', 'dev'), partners(axis, offset))  8.49 us
    ppermute x11, waiting for transfers between devices, exchange(): return lax.ppermute(block, ('grp', 'dev'), partners(axis, offset))  5.19 us
    pallas_call x5, Pallas kernels, call(): pl.pallas_call(kernel, name=name, compiler_params=SMALL, out_shape=[shape...  1.93 us
    pallas_call x1, Pallas kernels, body(): pl.pallas_call(functools.partial(finish_kernel, True), name='finish_1', c...  1.41 us
    pallas_call x1, Pallas kernels, start(): pl.pallas_call(start_kernel, name='start', compiler_params=SMALL, out_sha...  1.39 us
  transfers between devices with their start and end apart: 11, of which 2 were waited for; matrix products, arithmetic and copies ran while one was open for 1% of the time, Pallas kernels for 6%

profile of v4, /device:TPU:0, one launch (start us, length us, event | category | flops | bytes accessed | tf_op | source)
XLA Modules:
  0.0 19.9 jit_solution(4191466890404390272)
XLA Ops:
  0.0 1.4 %start.1 = (f32[4,6,16,256]{3,2,1,0:T(8,128)S(1)}, f32[3,24,256]{2,1,0:T(8,128)S(1)}, f32[3,24,256]{2,1,0:T(8,128)S(1)}, f32[2,24,256]{2,1,0:T(8,128)S(1)}, f32[...) custom-call(f32[4,6,16,256]{3,2,1,0:T(8,128)} %fields.1, s32[4,6]{1,0:T(4,128)} %neighbors.1, ...), custom_call_target="tpu_custom_call" | custom-call | tf_op jit(solution)/shard_map/start/pallas_call | solution.py:411
  1.4 3.1 %collective-permute-start.2 = (f32[2,24,256]{2,1,0:T(8,128)S(1)}, f32[2,24,256]{2,1,0:T(8,128)S(1)}, u32[]{:S(2)}, u32[]{:S(2)}) collective-permute-start(f32[2,24,256]{2,1,0:T(8,128)S(1)} %get-tuple-element.44), channel_id=1, source_target_pairs={{0,8},{1,9},{2,10},{3,11},{4,12},{5,13},{6,14},{7,15},{8,0},{9,1},... | collective-permute-start | bytes 147464 | tf_op jit(solution)/shard_map/ppermute | solution.py:52
  4.5 0.0 collective-permute-start.3
  5.8 0.1 compare_select_fusion
  5.9 0.1 broadcast_in_dim.15.masks
  6.0 0.1 collective-permute-start.1
  6.1 0.5 %collective-permute-start = (f32[96,256]{1,0:T(8,128)S(1)}, f32[96,256]{1,0:T(8,128)S(1)}, u32[]{:S(2)}, u32[]{:S(2)}) collective-permute-start(f32[96,256]{1,0:T(8,128)S(1)} %get-tuple-element.42), channel_id=1, source_target_pairs={{0,1},{1,0},{2,3},{3,2},{4,5},{5,4},{6,7},{7,6},{8,9},{9,8},{10,11... | collective-permute-start | bytes 294920 | tf_op jit(solution)/shard_map/ppermute | solution.py:52
  6.6 0.0 collective-permute-done.2.faces
  6.6 0.0 collective-permute-done.3.faces_dev
  6.6 0.1 faces.1
  6.7 0.1 collective-permute-start.4
  6.8 2.0 %collective-permute-start.5 = (f32[2,24,256]{2,1,0:T(8,128)S(1)}, f32[2,24,256]{2,1,0:T(8,128)S(1)}, u32[]{:S(2)}, u32[]{:S(2)}) collective-permute-start(f32[2,24,256]{2,1,0:T(8,128)S(1)} %get-tuple-element.50), channel_id=1, source_target_pairs={{0,8},{1,2},{2,1},{3,4},{4,3},{5,6},{6,5},{7,15},{8,0},{9,10},{10,... | collective-permute-start | bytes 147464 | tf_op jit(solution)/shard_map/ppermute | solution.py:52
  8.8 0.0 collective-permute-start.6
  8.8 0.0 collective-permute-done.block_dev
  8.8 3.0 %collective-permute-done.1.block_grp = f32[120,256]{1,0:T(8,128)S(1)} collective-permute-done((f32[120,256]{1,0:T(8,128)S(1)}, f32[120,256]{1,0:T(8,128)S(1)}, u32[]{:S(2)}, u32[]{:S(2)}) %collective-permute-start.1) | collective-permute-done | bytes 122912 | tf_op jit(solution)/shard_map/ppermute | solution.py:52
  11.8 0.6 %inner_0.1 = (f32[2,384,128]{2,1,0:T(8,128)S(1)}, f32[24,256]{1,0:T(8,128)S(1)}, f32[24,256]{1,0:T(8,128)S(1)}, f32[24,256]{1,0:T(8,128)S(1)}, f32[24,256]{1,0:T(8,128)S(1)}) custom-call(f32[2,24,256]{2,1,0:T(8,128)S(1)} %broadcast_in_dim.15.masks, f32[4,24,128]{2,1,0:T(8,128)S(1)} %get-tuple-element.38.scale, ...), custom_call_target="tpu_custom_call" | custom-call | flops 4194304 | bytes 2097152 | tf_op jit(solution)/shard_map/inner_0/pallas_call | solution.py:397
  12.3 0.0 collective-permute-done.6.refs_5_
  12.3 0.0 collective-permute-done.5.refs_3_
  12.3 0.0 collective-permute-done.4.refs_2_
  12.4 0.8 %finish_0.1 = (f32[2,384,128]{2,1,0:T(8,128)S(1)}, f32[3,24,256]{2,1,0:T(8,128)S(1)}, f32[3,24,256]{2,1,0:T(8,128)S(1)}, f32[2,24,256]{2,1,0:T(8,128)S(1)}, f32[...) custom-call(f32[6,24,128]{2,1,0:T(8,128)S(1)} %get-tuple-element.34.select, ...), custom_call_target="tpu_custom_call" | custom-call | flops 1048576 | bytes 1048576 | tf_op jit(solution)/shard_map/finish_0/pallas_call | solution.py:397
  13.2 0.0 collective-permute-start.7
  13.2 1.5 %collective-permute-start.8 = (f32[2,24,256]{2,1,0:T(8,128)S(1)}, f32[2,24,256]{2,1,0:T(8,128)S(1)}, u32[]{:S(2)}, u32[]{:S(2)}) collective-permute-start(f32[2,24,256]{2,1,0:T(8,128)S(1)} %get-tuple-element.60), channel_id=1, source_target_pairs={{0,8},{1,2},{2,1},{3,4},{4,3},{5,6},{6,5},{7,15},{8,0},{9,10},{10,... | collective-permute-start | bytes 147464 | tf_op jit(solution)/shard_map/ppermute | solution.py:52
  14.7 0.6 %collective-permute-start.9 = (f32[24,256]{1,0:T(8,128)S(1)}, f32[24,256]{1,0:T(8,128)S(1)}, u32[]{:S(2)}, u32[]{:S(2)}) collective-permute-start(f32[24,256]{1,0:T(8,128)S(1)} %get-tuple-element.61), channel_id=1, source_target_pairs={{0,8},{1,9},{2,10},{3,11},{4,12},{5,13},{6,14},{7,15},{8,0},{9,1},... | collective-permute-start | bytes 73736 | tf_op jit(solution)/shard_map/ppermute | solution.py:52
  15.3 0.5 %collective-permute-start.10 = (f32[24,256]{1,0:T(8,128)S(1)}, f32[24,256]{1,0:T(8,128)S(1)}, u32[]{:S(2)}, u32[]{:S(2)}) collective-permute-start(f32[24,256]{1,0:T(8,128)S(1)} %get-tuple-element.62), channel_id=1, source_target_pairs={{0,1},{1,0},{2,3},{3,2},{4,5},{5,4},{6,7},{7,6},{8,16},{9,17},{10,... | collective-permute-start | bytes 73736 | tf_op jit(solution)/shard_map/ppermute | solution.py:52
  15.8 0.5 %inner_1.1.partial = f32[2,384,128]{2,1,0:T(8,128)S(1)} custom-call(f32[2,384,128]{2,1,0:T(8,128)S(1)} %get-tuple-element.56.state, f32[4,24,128]{2,1,0:T(8,128)S(1)} %get-tuple-element.38.scale), custom_call_target="tpu_custom_call" | custom-call | flops 4194304 | bytes 2097152 | tf_op jit(solution)/shard_map/inner_1/pallas_call | solution.py:397
  16.3 2.2 %collective-permute-done.9.refs_4_ = f32[24,256]{1,0:T(8,128)S(1)} collective-permute-done((f32[24,256]{1,0:T(8,128)S(1)}, f32[24,256]{1,0:T(8,128)S(1)}, u32[]{:S(2)}, u32[]{:S(2)}) %collective-permute-start.9) | collective-permute-done | bytes 24608 | tf_op jit(solution)/shard_map/ppermute | solution.py:52
  18.5 0.0 collective-permute-done.10.refs_5_
  18.5 0.0 collective-permute-done.7.refs_2_
  18.5 0.0 collective-permute-done.8.refs_3_
  18.5 1.4 %finish_1.1 = f32[4,6,16,256]{3,2,1,0:T(8,128)} custom-call(f32[6,24,128]{2,1,0:T(8,128)S(1)} %get-tuple-element.34.select, f32[2,384,128]{2,1,0:T(8,128)S(1)} %inner_1.1.partial, f32[3,24,256]{2,1,0:T(8,128)S(1)} %get-tuple-element.57.refs_0_, f32[3,24,256]{2,1,0:T(8,128)S(1)} %get-tuple-element.58.refs_1_, ...), custom_call_target="tpu_custom_call" | custom-call | tf_op jit(solution)/shard_map/finish_1/pallas_call | solution.py:466
  (1 shorter events, 0.0 us)
Async XLA Ops:
  1.4 5.2 %collective-permute-start.2 = (f32[2,24,256]{2,1,0:T(8,128)S(1)}, f32[2,24,256]{2,1,0:T(8,128)S(1)}, u32[]{:S(2)}, u32[]{:S(2)}) collective-permute-start(f32[2,24,256]{2,1,0:T(8,128)S(1)} %get-tuple-element.44), channel_id=1, source_target_pairs={{0,8},{1,9},{2,10},{3,11},{4,12},{5,13},{6,14},{7,15},{8,0},{9,1},... | collective-permute-start | bytes 147464 | tf_op jit(solution)/shard_map/ppermute | solution.py:52
  4.5 2.1 %collective-permute-start.3 = (f32[2,24,256]{2,1,0:T(8,128)S(1)}, f32[2,24,256]{2,1,0:T(8,128)S(1)}, u32[]{:S(2)}, u32[]{:S(2)}) collective-permute-start(f32[2,24,256]{2,1,0:T(8,128)S(1)} %get-tuple-element.45), channel_id=1, source_target_pairs={{0,1},{1,0},{2,3},{3,2},{4,5},{5,4},{6,7},{7,6},{8,9},{9,8},{10,11... | collective-permute-start | bytes 147464 | tf_op jit(solution)/shard_map/ppermute | solution.py:52
  6.0 5.8 %collective-permute-start.1 = (f32[120,256]{1,0:T(8,128)S(1)}, f32[120,256]{1,0:T(8,128)S(1)}, u32[]{:S(2)}, u32[]{:S(2)}) collective-permute-start(f32[120,256]{1,0:T(8,128)S(1)} %get-tuple-element.43), channel_id=1, source_target_pairs={{0,8},{1,9},{2,10},{3,11},{4,12},{5,13},{6,14},{7,15},{8,0},{9,1},... | collective-permute-start | bytes 368648 | tf_op jit(solution)/shard_map/ppermute | solution.py:52
  6.1 2.7 %collective-permute-start = (f32[96,256]{1,0:T(8,128)S(1)}, f32[96,256]{1,0:T(8,128)S(1)}, u32[]{:S(2)}, u32[]{:S(2)}) collective-permute-start(f32[96,256]{1,0:T(8,128)S(1)} %get-tuple-element.42), channel_id=1, source_target_pairs={{0,1},{1,0},{2,3},{3,2},{4,5},{5,4},{6,7},{7,6},{8,9},{9,8},{10,11... | collective-permute-start | bytes 294920 | tf_op jit(solution)/shard_map/ppermute | solution.py:52
  6.7 5.7 %collective-permute-start.4 = (f32[3,24,256]{2,1,0:T(8,128)S(1)}, f32[3,24,256]{2,1,0:T(8,128)S(1)}, u32[]{:S(2)}, u32[]{:S(2)}) collective-permute-start(f32[3,24,256]{2,1,0:T(8,128)S(1)} %get-tuple-element.49), channel_id=1, source_target_pairs={{0,1},{1,0},{2,3},{3,2},{4,5},{5,4},{6,7},{7,6},{8,9},{9,8},{10,11... | collective-permute-start | bytes 221192 | tf_op jit(solution)/shard_map/ppermute | solution.py:52
  6.8 5.6 %collective-permute-start.5 = (f32[2,24,256]{2,1,0:T(8,128)S(1)}, f32[2,24,256]{2,1,0:T(8,128)S(1)}, u32[]{:S(2)}, u32[]{:S(2)}) collective-permute-start(f32[2,24,256]{2,1,0:T(8,128)S(1)} %get-tuple-element.50), channel_id=1, source_target_pairs={{0,8},{1,2},{2,1},{3,4},{4,3},{5,6},{6,5},{7,15},{8,0},{9,10},{10,... | collective-permute-start | bytes 147464 | tf_op jit(solution)/shard_map/ppermute | solution.py:52
  8.8 3.5 %collective-permute-start.6 = (f32[24,256]{1,0:T(8,128)S(1)}, f32[24,256]{1,0:T(8,128)S(1)}, u32[]{:S(2)}, u32[]{:S(2)}) collective-permute-start(f32[24,256]{1,0:T(8,128)S(1)} %get-tuple-element.52), channel_id=1, source_target_pairs={{0,1},{1,0},{2,3},{3,2},{4,5},{5,4},{6,7},{7,6},{8,16},{9,17},{10,... | collective-permute-start | bytes 73736 | tf_op jit(solution)/shard_map/ppermute | solution.py:52
  13.2 5.3 %collective-permute-start.7 = (f32[2,24,256]{2,1,0:T(8,128)S(1)}, f32[2,24,256]{2,1,0:T(8,128)S(1)}, u32[]{:S(2)}, u32[]{:S(2)}) collective-permute-start(f32[2,24,256]{2,1,0:T(8,128)S(1)} %get-tuple-element.59), channel_id=1, source_target_pairs={{0,1},{1,0},{2,3},{3,2},{4,5},{5,4},{6,7},{7,6},{8,9},{9,8},{10,11... | collective-permute-start | bytes 147464 | tf_op jit(solution)/shard_map/ppermute | solution.py:52
  13.2 5.3 %collective-permute-start.8 = (f32[2,24,256]{2,1,0:T(8,128)S(1)}, f32[2,24,256]{2,1,0:T(8,128)S(1)}, u32[]{:S(2)}, u32[]{:S(2)}) collective-permute-start(f32[2,24,256]{2,1,0:T(8,128)S(1)} %get-tuple-element.60), channel_id=1, source_target_pairs={{0,8},{1,2},{2,1},{3,4},{4,3},{5,6},{6,5},{7,15},{8,0},{9,10},{10,... | collective-permute-start | bytes 147464 | tf_op jit(solution)/shard_map/ppermute | solution.py:52
  14.7 3.8 %collective-permute-start.9 = (f32[24,256]{1,0:T(8,128)S(1)}, f32[24,256]{1,0:T(8,128)S(1)}, u32[]{:S(2)}, u32[]{:S(2)}) collective-permute-start(f32[24,256]{1,0:T(8,128)S(1)} %get-tuple-element.61), channel_id=1, source_target_pairs={{0,8},{1,9},{2,10},{3,11},{4,12},{5,13},{6,14},{7,15},{8,0},{9,1},... | collective-permute-start | bytes 73736 | tf_op jit(solution)/shard_map/ppermute | solution.py:52
  15.3 3.2 %collective-permute-start.10 = (f32[24,256]{1,0:T(8,128)S(1)}, f32[24,256]{1,0:T(8,128)S(1)}, u32[]{:S(2)}, u32[]{:S(2)}) collective-permute-start(f32[24,256]{1,0:T(8,128)S(1)} %get-tuple-element.62), channel_id=1, source_target_pairs={{0,1},{1,0},{2,3},{3,2},{4,5},{5,4},{6,7},{7,6},{8,16},{9,17},{10,... | collective-permute-start | bytes 73736 | tf_op jit(solution)/shard_map/ppermute | solution.py:52

commit v5 on v4

--- a/solution.py
+++ b/solution.py
@@ -27,6 +27,8 @@
 FACE = (ROWS, PLANE)
 SIDE = (3, ROWS, PLANE)
 SOURCES = 4
+PARTS = 2
+SELECT = (3, 2 * ROWS, PARTS * SOURCES * ROWS)
 
 
 def partners(axis, offset):
@@ -117,11 +119,12 @@
     deep_b[...] = jnp.where(even, low[2], high[2])
 
 
-def fill_slot(state, slot, block):
+def fill_slot(state, slot, block, first=0, count=EDGE):
     for f in range(NFIELD):
         value = block(f)
         for h in range(2):
-            state[h, pl.ds(f * SLOTS + slot, EDGE, stride=ROWS), :] = value[:, h * HALF : (h + 1) * HALF]
+            rows = pl.ds(first * ROWS + f * SLOTS + slot, count, stride=ROWS)
+            state[h, rows, :] = value[:, h * HALF : (h + 1) * HALF]
 
 
 def slot_rows():
@@ -149,20 +152,20 @@
     return lax.rem(lax.axis_index(axis), 2) == 0
 
 
-def block_kernel(masks, fields, low, high, to_dev, to_grp):
+def block_kernel(mask_dev, fields, low, high, to_dev, to_grp):
     last, size = SLOTS - 1, NFIELD * EDGE
     for f in range(NFIELD):
         to_dev[f * EDGE : (f + 1) * EDGE] = fields[last, f]
         to_grp[f * EDGE : (f + 1) * EDGE] = fields[0, f]
     away = jnp.where(even_place("grp"), low[2], high[2])
-    to_grp[size : size + ROWS] = jnp.where(slot_rows() == 0, away, masks[0])
-
-
-def faces_kernel(masks, low, high, faces, faces_dev, *outs):
+    to_grp[size : size + ROWS] = jnp.where(slot_rows() == 0, away, mask_dev[...])
+
+
+def faces_kernel(mask_dev, mask_grp, low, high, faces, faces_dev, *outs):
     new_low, new_high, flat_a, flat_b, deep_b = outs
     rows, last = slot_rows(), SLOTS - 1
-    first_rows = (rows == 0) & (masks[1] > 0.5)
-    last_rows = (rows == last) & (masks[0] > 0.5)
+    first_rows = (rows == 0) & (mask_grp[...] > 0.5)
+    last_rows = (rows == last) & (mask_dev[...] > 0.5)
     even = even_place("grp")
     got_first, got_last, got_last_z = faces[0], faces_dev[0], faces_dev[1]
     for side, (raw, new) in enumerate(((low, new_low), (high, new_high))):
@@ -213,28 +216,34 @@
         came = 2 + lax.rem(lax.rem(dev if face < 4 else grp, 2) + face % 2 + 1, 2)
         for number in range(SLOTS):
             target = neighbors[number, face]
-            source = jnp.where(target < 0, 0, jnp.where(target // SLOTS == rank, 1, came))
+            source = jnp.where(target < 0, face % 2, jnp.where(target // SLOTS == rank, 1 - face % 2, came))
             first.append(source * ROWS + jnp.where(target < 0, number, target & (SLOTS - 1)))
-        select[face] = jnp.where(column == by_slot(first) + field * SLOTS, weights[face // 2], 0.0)
+        chosen = jnp.where(column == by_slot(first) + field * SLOTS, 1.0, 0.0)[:, : SOURCES * ROWS]
+        rows = pl.ds(face % 2 * ROWS, ROWS)
+        for part in range(PARTS):
+            select[face // 2, rows, pl.ds(part * SOURCES * ROWS, SOURCES * ROWS)] = chosen
 
 
 def start_kernel(fields, neighbors, orient, *refs):
     fetched, low, high, faces_grp, faces_dev, scale, select = refs[:7]
     state, near, turn, arrived = refs[7:]
     scalars = ((neighbors, near), (orient, turn))
-    blocks = tuple((fields.at[slot], fetched.at[slot]) for slot in range(SLOTS))
+    parts = [pl.ds(first, EDGE // 2) for first in (0, EDGE // 2)]
+    blocks = tuple((fields.at[:, :, part], fetched.at[:, :, part]) for part in parts)
     copies = [pltpu.make_async_copy(*pair, arrived.at[number]) for number, pair in enumerate((*scalars, *blocks))]
     for copy in copies:
         copy.start()
     for copy in copies[: len(scalars)]:
         copy.wait()
     plan_kernel(near, turn, scale, select)
-    for slot in range(SLOTS):
-        copies[len(scalars) + slot].wait()
-        fill_slot(state, slot, lambda f: fetched[slot, f])
     packer = Packer()
-    for x in range(EDGE):
-        packer.add(x, *plane_at(state, x))
+    for number, part in enumerate(parts):
+        copies[len(scalars) + number].wait()
+        first = number * (EDGE // 2)
+        for slot in range(SLOTS):
+            fill_slot(state, slot, lambda f: fetched[slot, f, part], first, EDGE // 2)
+        for x in range(first, first + EDGE // 2):
+            packer.add(x, *plane_at(state, x))
     write_tables(packer, state, (low, high))
     faces_grp[0] = gathered([low[0], high[0], low[1], high[1]], 0)
     faces_grp[1] = jnp.where(even_place("grp"), high[2], low[2])
@@ -242,10 +251,10 @@
     faces_dev[1] = gathered([low[2], high[2]], SLOTS - 1)
 
 
-def first_inner_kernel(masks, scale, fields, block_dev, block_grp, faces, low, high, new_low, new_high, *refs):
+def first_inner_kernel(mask_dev, mask_grp, scale, fields, block_dev, block_grp, faces, low, high, new_low, new_high, *refs):
     partial, got_deep, relayed, z_low, z_high, state = refs
     size = NFIELD * EDGE
-    swap_dev, swap_grp = masks[0] > 0.5, masks[1] > 0.5
+    swap_dev, swap_grp = mask_dev[...] > 0.5, mask_grp[...] > 0.5
 
     def block(slot):
         def of(f):
@@ -309,7 +318,7 @@
             partial[h, pl.ds(rows + 2 * tile, tile), :] = flow[2 * tile :]
 
 
-def finish_kernel(last_step, select, partial, *refs):
+def finish_kernel(last_step, scale, select, partial, *refs):
     own, got_flat = refs[0:2], refs[2:4]
     own_deep = [ref[2] for ref in own]
     if last_step:
@@ -321,13 +330,16 @@
         own_deep = [z_low[...], z_high[...]]
         done, outs, sends = refs[9], refs[10:12], refs[12:16]
     ghosts = []
-    for face in range(6):
-        axis, side = face // 2, face % 2
+    for axis in range(3):
         got = [ref[axis] for ref in got_flat] if axis < 2 else got_deep
         mine = [ref[axis] for ref in own] if axis < 2 else own_deep
-        tables = jnp.concatenate([mine[side], mine[1 - side], *got], axis=0)
-        chosen = select[face][:, : SOURCES * ROWS]
-        ghosts.append(jnp.dot(chosen, tables, precision=lax.Precision.HIGHEST, preferred_element_type=jnp.float32))
+        tables = jnp.concatenate([*mine, *got], axis=0)
+        near = tables.astype(jnp.bfloat16)
+        rest = (tables - near.astype(jnp.float32)).astype(jnp.bfloat16)
+        both = jnp.concatenate([near, rest], axis=0)
+        pair = jnp.dot(select[axis].astype(jnp.bfloat16), both, preferred_element_type=jnp.float32)
+        weight = jnp.concatenate([scale[axis]] * 2, axis=1)
+        ghosts += [weight * pair[:ROWS], weight * pair[ROWS:]]
     lane = iota((ROWS, HALF), 1)
     start_y, end_y = lane < EDGE, lane >= HALF - EDGE
     ends_z = (lane % EDGE == 0) | (lane % EDGE == EDGE - 1)
@@ -407,7 +419,7 @@
 
 
 def start(arguments):
-    shapes = (arguments[0].shape, SIDE, SIDE, FLAT, FLAT, (4, ROWS, HALF), (6, ROWS, HALF))
+    shapes = (arguments[0].shape, SIDE, SIDE, FLAT, FLAT, (4, ROWS, HALF), SELECT)
     return pl.pallas_call(
         start_kernel,
         name="start",
@@ -418,26 +430,31 @@
         scratch_shapes=[
             pltpu.VMEM(STATE, jnp.float32),
             *(pltpu.SMEM(array.shape, jnp.int32) for array in arguments[1:]),
-            pltpu.SemaphoreType.DMA((len(arguments) - 1 + SLOTS,)),
+            pltpu.SemaphoreType.DMA((len(arguments) + 1,)),
         ],
     )(*(pltpu.with_memory_space_constraint(array, pltpu.HBM) for array in arguments))
 
 
+def mask(flag):
+    return jnp.broadcast_to(jnp.where(flag == 1, 1.0, 0.0).reshape(1, 1), FACE)
+
+
 def body(fields, swap_dev, swap_grp, neighbors, orient):
     fields, low, high, faces, faces_dev, scale, select = start((fields, neighbors, orient))
-    swap_dev, swap_grp, faces = lax.optimization_barrier((swap_dev, swap_grp, faces))
-    flags = jnp.concatenate([swap_dev, swap_grp])
-    masks = jnp.broadcast_to(jnp.where(flags == 1, 1.0, 0.0).reshape(2, 1, 1), (2, *FACE))
+    swap_dev, faces = lax.optimization_barrier((swap_dev, faces))
     faces = exchange(faces, "grp", 0)
     faces_dev = exchange(faces_dev, "dev", 0)
-    to_dev, to_grp = call(block_kernel, "blocks", [TO_DEV, TO_GRP], [masks, fields, low, high], 1 << 24)
+    mask_dev = mask(swap_dev)
+    to_dev, to_grp = call(block_kernel, "blocks", [TO_DEV, TO_GRP], [mask_dev, fields, low, high], 1 << 24)
+    swap_grp, to_grp = lax.optimization_barrier((swap_grp, to_grp))
+    mask_grp = mask(swap_grp)
     block_grp = exchange(to_grp, "grp", 0)
     block_dev = exchange(to_dev, "dev", 0)
     new_low, new_high, *sends = call(
         faces_kernel,
         "faces",
         [SIDE, SIDE, SIDE, FLAT, FACE],
-        [masks, low, high, faces, faces_dev],
+        [mask_dev, mask_grp, low, high, faces, faces_dev],
         1 << 24,
     )
     flat_a = exchange(sends[0], "dev", 0)
@@ -447,7 +464,7 @@
         first_inner_kernel,
         "inner_0",
         [STATE, FACE, FACE, FACE, FACE],
-        [masks, scale, fields, block_dev, block_grp, faces, low, high, new_low, new_high],
+        [mask_dev, mask_grp, scale, fields, block_dev, block_grp, faces, low, high, new_low, new_high],
         4 << 20,
         [pltpu.VMEM(STATE, jnp.float32)],
     )
@@ -455,7 +472,7 @@
         functools.partial(finish_kernel, False),
         "finish_0",
         TABLES,
-        [select, partial, new_low, new_high, flat_a, flat_b, deep_a, deep_b, relayed, z_low, z_high],
+        [scale, select, partial, new_low, new_high, flat_a, flat_b, deep_a, deep_b, relayed, z_low, z_high],
     )
     own, sends = tables[:2], tables[2:]
     flat_a = exchange(sends[0], "dev", 0)
@@ -468,14 +485,14 @@
         name="finish_1",
         compiler_params=SMALL,
         out_shape=shaped(fields.shape),
-        in_specs=[spec(VECTOR)] * 8,
+        in_specs=[spec(VECTOR)] * 9,
         out_specs=spec(pl.ANY),
         scratch_shapes=[
             pltpu.VMEM(STATE, jnp.float32),
             pltpu.VMEM(fields.shape, jnp.float32),
             pltpu.SemaphoreType.DMA((2,)),
         ],
-    )(select, partial, *own, flat_a, flat_b, deep_a, deep_b)
+    )(scale, select, partial, *own, flat_a, flat_b, deep_a, deep_b)
 
 
 def solution(mesh):

time: 20.1 us -> 19.8 us (0.985)
  starting transfers between devices: 8.49 us -> 9.37 us
  waiting for transfers between devices: 5.19 us -> 4.47 us
  Pallas kernels: 4.73 us -> 4.4 us
    ppermute x11, starting transfers between devices: 8.49 us -> 9.37 us  [exchange(): return lax.ppermute(block, ('grp', 'dev'), partners(axis, offset))]
    ppermute x11, waiting for transfers between devices: 5.19 us -> 4.47 us  [exchange(): return lax.ppermute(block, ('grp', 'dev'), partners(axis, offset))]
  transfers between devices with their start and end apart: 11 -> 11, of which waited for: 2 -> 3; matrix products, arithmetic and copies ran while one was open for 1% -> 0% of each run, Pallas kernels for 6% -> 6%
where the time goes in v5:
time: 19.8 us; the launch traced here: 19.6 us
  starting transfers between devices  9.37 us (47%)
  waiting for transfers between devices  4.47 us (23%)
  Pallas kernels  4.4 us (22%)
  between operations  1.4 us (7%)
    ppermute x11, starting transfers between devices, exchange(): return lax.ppermute(block, ('grp', 'dev'), partners(axis, offset))  9.37 us
    ppermute x11, waiting for transfers between devices, exchange(): return lax.ppermute(block, ('grp', 'dev'), partners(axis, offset))  4.47 us
    pallas_call x5, Pallas kernels, call(): pl.pallas_call(kernel, name=name, compiler_params=SMALL, out_shape=[shape...  1.74 us
    pallas_call x1, Pallas kernels, start(): pl.pallas_call(start_kernel, name='start', compiler_params=SMALL, out_sha...  1.44 us
    pallas_call x1, Pallas kernels, body(): pl.pallas_call(functools.partial(finish_kernel, True), name='finish_1', c...  1.22 us
  transfers between devices with their start and end apart: 11, of which 3 were waited for; matrix products, arithmetic and copies ran while one was open for 0% of the time, Pallas kernels for 6%

profile of v5, /device:TPU:0, one launch (start us, length us, event | category | flops | bytes accessed | tf_op | source)
XLA Modules:
  0.0 19.6 jit_solution(16029927892041240582)
XLA Ops:
  0.0 1.4 %start.1 = (f32[4,6,16,256]{3,2,1,0:T(8,128)S(1)}, f32[3,24,256]{2,1,0:T(8,128)S(1)}, f32[3,24,256]{2,1,0:T(8,128)S(1)}, f32[2,24,256]{2,1,0:T(8,128)S(1)}, f32[...) custom-call(f32[4,6,16,256]{3,2,1,0:T(8,128)} %fields.1, s32[4,6]{1,0:T(4,128)} %neighbors.1, ...), custom_call_target="tpu_custom_call" | custom-call | tf_op jit(solution)/shard_map/start/pallas_call | solution.py:423
  1.4 3.1 %collective-permute-start.2 = (f32[2,24,256]{2,1,0:T(8,128)S(1)}, f32[2,24,256]{2,1,0:T(8,128)S(1)}, u32[]{:S(2)}, u32[]{:S(2)}) collective-permute-start(f32[2,24,256]{2,1,0:T(8,128)S(1)} %get-tuple-element.46), channel_id=1, source_target_pairs={{0,8},{1,9},{2,10},{3,11},{4,12},{5,13},{6,14},{7,15},{8,0},{9,1},... | collective-permute-start | bytes 147464 | tf_op jit(solution)/shard_map/ppermute | solution.py:54
  4.5 0.0 collective-permute-start.3
  5.2 0.1 collective-permute-start.1
  5.4 0.5 %collective-permute-start = (f32[96,256]{1,0:T(8,128)S(1)}, f32[96,256]{1,0:T(8,128)S(1)}, u32[]{:S(2)}, u32[]{:S(2)}) collective-permute-start(f32[96,256]{1,0:T(8,128)S(1)} %get-tuple-element.44), channel_id=1, source_target_pairs={{0,1},{1,0},{2,3},{3,2},{4,5},{5,4},{6,7},{7,6},{8,9},{9,8},{10,11... | collective-permute-start | bytes 294920 | tf_op jit(solution)/shard_map/ppermute | solution.py:54
  6.5 0.1 collective-permute-done.2.faces
  6.6 0.0 collective-permute-done.3.faces_dev
  6.6 0.1 faces.1
  6.7 0.1 collective-permute-start.4
  6.8 2.1 %collective-permute-start.5 = (f32[2,24,256]{2,1,0:T(8,128)S(1)}, f32[2,24,256]{2,1,0:T(8,128)S(1)}, u32[]{:S(2)}, u32[]{:S(2)}) collective-permute-start(f32[2,24,256]{2,1,0:T(8,128)S(1)} %get-tuple-element.52), channel_id=1, source_target_pairs={{0,8},{1,2},{2,1},{3,4},{4,3},{5,6},{6,5},{7,15},{8,0},{9,10},{10,... | collective-permute-start | bytes 147464 | tf_op jit(solution)/shard_map/ppermute | solution.py:54
  8.8 0.0 collective-permute-start.6
  8.9 0.0 collective-permute-done.block_dev
  8.9 2.2 %collective-permute-done.1.block_grp = f32[120,256]{1,0:T(8,128)S(1)} collective-permute-done((f32[120,256]{1,0:T(8,128)S(1)}, f32[120,256]{1,0:T(8,128)S(1)}, u32[]{:S(2)}, u32[]{:S(2)}) %collective-permute-start.1) | collective-permute-done | bytes 122912 | tf_op jit(solution)/shard_map/ppermute | solution.py:54
  11.0 0.5 %inner_0.1 = (f32[2,384,128]{2,1,0:T(8,128)S(1)}, f32[24,256]{1,0:T(8,128)S(1)}, f32[24,256]{1,0:T(8,128)S(1)}, f32[24,256]{1,0:T(8,128)S(1)}, f32[24,256]{1,0:T(8,128)S(1)}) custom-call(f32[24,256]{1,0:T(8,128)S(1)} %broadcast_in_dim.21.mask_dev, f32[24,256]{1,0:T(8,128)S(1)} %broadcast_in_dim.23.mask_grp, f32[4,24,128]{2,1,0:T(8,128)S(1)} %get-tuple-element.35.scale, ...), custom_call_target="tpu_custom_call" | custom-call | flops 4194304 | bytes 2097152 | tf_op jit(solution)/shard_map/inner_0/pallas_call | solution.py:409
  11.6 0.0 collective-permute-done.6.refs_5_
  11.6 0.0 collective-permute-done.5.refs_3_
  11.6 0.0 collective-permute-done.4.refs_2_
  11.6 0.6 %finish_0.1 = (f32[2,384,128]{2,1,0:T(8,128)S(1)}, f32[3,24,256]{2,1,0:T(8,128)S(1)}, f32[3,24,256]{2,1,0:T(8,128)S(1)}, f32[2,24,256]{2,1,0:T(8,128)S(1)}, f32[...) custom-call(f32[4,24,128]{2,1,0:T(8,128)S(1)} %get-tuple-element.35.scale, ...), custom_call_target="tpu_custom_call" | custom-call | flops 1048576 | bytes 1048576 | tf_op jit(solution)/shard_map/finish_0/pallas_call | solution.py:409
  12.3 0.1 collective-permute-start.7
  12.3 2.2 %collective-permute-start.8 = (f32[2,24,256]{2,1,0:T(8,128)S(1)}, f32[2,24,256]{2,1,0:T(8,128)S(1)}, u32[]{:S(2)}, u32[]{:S(2)}) collective-permute-start(f32[2,24,256]{2,1,0:T(8,128)S(1)} %get-tuple-element.62), channel_id=1, source_target_pairs={{0,8},{1,2},{2,1},{3,4},{4,3},{5,6},{6,5},{7,15},{8,0},{9,10},{10,... | collective-permute-start | bytes 147464 | tf_op jit(solution)/shard_map/ppermute | solution.py:54
  14.6 0.1 collective-permute-start.9
  14.7 1.1 %collective-permute-start.10 = (f32[24,256]{1,0:T(8,128)S(1)}, f32[24,256]{1,0:T(8,128)S(1)}, u32[]{:S(2)}, u32[]{:S(2)}) collective-permute-start(f32[24,256]{1,0:T(8,128)S(1)} %get-tuple-element.64), channel_id=1, source_target_pairs={{0,1},{1,0},{2,3},{3,2},{4,5},{5,4},{6,7},{7,6},{8,16},{9,17},{10,... | collective-permute-start | bytes 73736 | tf_op jit(solution)/shard_map/ppermute | solution.py:54
  15.7 0.5 %inner_1.1.partial = f32[2,384,128]{2,1,0:T(8,128)S(1)} custom-call(f32[2,384,128]{2,1,0:T(8,128)S(1)} %get-tuple-element.58.state, f32[4,24,128]{2,1,0:T(8,128)S(1)} %get-tuple-element.35.scale), custom_call_target="tpu_custom_call" | custom-call | flops 4194304 | bytes 2097152 | tf_op jit(solution)/shard_map/inner_1/pallas_call | solution.py:409
  16.2 2.2 %collective-permute-done.9.refs_4_ = f32[24,256]{1,0:T(8,128)S(1)} collective-permute-done((f32[24,256]{1,0:T(8,128)S(1)}, f32[24,256]{1,0:T(8,128)S(1)}, u32[]{:S(2)}, u32[]{:S(2)}) %collective-permute-start.9) | collective-permute-done | bytes 24608 | tf_op jit(solution)/shard_map/ppermute | solution.py:54
  18.4 0.0 collective-permute-done.10.refs_5_
  18.4 0.0 collective-permute-done.7.refs_2_
  18.4 0.0 collective-permute-done.8.refs_3_
  18.4 1.2 %finish_1.1 = f32[4,6,16,256]{3,2,1,0:T(8,128)} custom-call(f32[4,24,128]{2,1,0:T(8,128)S(1)} %get-tuple-element.35.scale, f32[3,48,192]{2,1,0:T(8,128)S(1)} %get-tuple-element.36.select, f32[2,384,128]{2,1,0:T(8,128)S(1)} %inner_1.1.partial, f32[3,24,256]{2,1,0:T(8,128)S(1)} %get-tuple-element.59.refs_0_, f32[3,24,256]{2,1,0:T(8,128)S(1)} %get-tuple-element.60.refs_1_, ...), custom_call_target="tpu_custom_call" | custom-call | tf_op jit(solution)/shard_map/finish_1/pallas_call | solution.py:483
  (3 shorter events, 0.0 us)
Async XLA Ops:
  1.4 5.2 %collective-permute-start.2 = (f32[2,24,256]{2,1,0:T(8,128)S(1)}, f32[2,24,256]{2,1,0:T(8,128)S(1)}, u32[]{:S(2)}, u32[]{:S(2)}) collective-permute-start(f32[2,24,256]{2,1,0:T(8,128)S(1)} %get-tuple-element.46), channel_id=1, source_target_pairs={{0,8},{1,9},{2,10},{3,11},{4,12},{5,13},{6,14},{7,15},{8,0},{9,1},... | collective-permute-start | bytes 147464 | tf_op jit(solution)/shard_map/ppermute | solution.py:54
  4.5 2.1 %collective-permute-start.3 = (f32[2,24,256]{2,1,0:T(8,128)S(1)}, f32[2,24,256]{2,1,0:T(8,128)S(1)}, u32[]{:S(2)}, u32[]{:S(2)}) collective-permute-start(f32[2,24,256]{2,1,0:T(8,128)S(1)} %get-tuple-element.47), channel_id=1, source_target_pairs={{0,1},{1,0},{2,3},{3,2},{4,5},{5,4},{6,7},{7,6},{8,9},{9,8},{10,11... | collective-permute-start | bytes 147464 | tf_op jit(solution)/shard_map/ppermute | solution.py:54
  5.2 5.8 %collective-permute-start.1 = (f32[120,256]{1,0:T(8,128)S(1)}, f32[120,256]{1,0:T(8,128)S(1)}, u32[]{:S(2)}, u32[]{:S(2)}) collective-permute-start(f32[120,256]{1,0:T(8,128)S(1)} %get-tuple-element.45), channel_id=1, source_target_pairs={{0,8},{1,9},{2,10},{3,11},{4,12},{5,13},{6,14},{7,15},{8,0},{9,1},... | collective-permute-start | bytes 368648 | tf_op jit(solution)/shard_map/ppermute | solution.py:54
  5.4 3.5 %collective-permute-start = (f32[96,256]{1,0:T(8,128)S(1)}, f32[96,256]{1,0:T(8,128)S(1)}, u32[]{:S(2)}, u32[]{:S(2)}) collective-permute-start(f32[96,256]{1,0:T(8,128)S(1)} %get-tuple-element.44), channel_id=1, source_target_pairs={{0,1},{1,0},{2,3},{3,2},{4,5},{5,4},{6,7},{7,6},{8,9},{9,8},{10,11... | collective-permute-start | bytes 294920 | tf_op jit(solution)/shard_map/ppermute | solution.py:54
  6.7 4.9 %collective-permute-start.4 = (f32[3,24,256]{2,1,0:T(8,128)S(1)}, f32[3,24,256]{2,1,0:T(8,128)S(1)}, u32[]{:S(2)}, u32[]{:S(2)}) collective-permute-start(f32[3,24,256]{2,1,0:T(8,128)S(1)} %get-tuple-element.51), channel_id=1, source_target_pairs={{0,1},{1,0},{2,3},{3,2},{4,5},{5,4},{6,7},{7,6},{8,9},{9,8},{10,11... | collective-permute-start | bytes 221192 | tf_op jit(solution)/shard_map/ppermute | solution.py:54
  6.8 4.9 %collective-permute-start.5 = (f32[2,24,256]{2,1,0:T(8,128)S(1)}, f32[2,24,256]{2,1,0:T(8,128)S(1)}, u32[]{:S(2)}, u32[]{:S(2)}) collective-permute-start(f32[2,24,256]{2,1,0:T(8,128)S(1)} %get-tuple-element.52), channel_id=1, source_target_pairs={{0,8},{1,2},{2,1},{3,4},{4,3},{5,6},{6,5},{7,15},{8,0},{9,10},{10,... | collective-permute-start | bytes 147464 | tf_op jit(solution)/shard_map/ppermute | solution.py:54
  8.8 2.8 %collective-permute-start.6 = (f32[24,256]{1,0:T(8,128)S(1)}, f32[24,256]{1,0:T(8,128)S(1)}, u32[]{:S(2)}, u32[]{:S(2)}) collective-permute-start(f32[24,256]{1,0:T(8,128)S(1)} %get-tuple-element.54), channel_id=1, source_target_pairs={{0,1},{1,0},{2,3},{3,2},{4,5},{5,4},{6,7},{7,6},{8,16},{9,17},{10,... | collective-permute-start | bytes 73736 | tf_op jit(solution)/shard_map/ppermute | solution.py:54
  12.3 6.2 %collective-permute-start.7 = (f32[2,24,256]{2,1,0:T(8,128)S(1)}, f32[2,24,256]{2,1,0:T(8,128)S(1)}, u32[]{:S(2)}, u32[]{:S(2)}) collective-permute-start(f32[2,24,256]{2,1,0:T(8,128)S(1)} %get-tuple-element.61), channel_id=1, source_target_pairs={{0,1},{1,0},{2,3},{3,2},{4,5},{5,4},{6,7},{7,6},{8,9},{9,8},{10,11... | collective-permute-start | bytes 147464 | tf_op jit(solution)/shard_map/ppermute | solution.py:54
  12.3 6.1 %collective-permute-start.8 = (f32[2,24,256]{2,1,0:T(8,128)S(1)}, f32[2,24,256]{2,1,0:T(8,128)S(1)}, u32[]{:S(2)}, u32[]{:S(2)}) collective-permute-start(f32[2,24,256]{2,1,0:T(8,128)S(1)} %get-tuple-element.62), channel_id=1, source_target_pairs={{0,8},{1,2},{2,1},{3,4},{4,3},{5,6},{6,5},{7,15},{8,0},{9,10},{10,... | collective-permute-start | bytes 147464 | tf_op jit(solution)/shard_map/ppermute | solution.py:54
  14.6 3.8 %collective-permute-start.9 = (f32[24,256]{1,0:T(8,128)S(1)}, f32[24,256]{1,0:T(8,128)S(1)}, u32[]{:S(2)}, u32[]{:S(2)}) collective-permute-start(f32[24,256]{1,0:T(8,128)S(1)} %get-tuple-element.63), channel_id=1, source_target_pairs={{0,8},{1,9},{2,10},{3,11},{4,12},{5,13},{6,14},{7,15},{8,0},{9,1},... | collective-permute-start | bytes 73736 | tf_op jit(solution)/shard_map/ppermute | solution.py:54
  14.7 3.8 %collective-permute-start.10 = (f32[24,256]{1,0:T(8,128)S(1)}, f32[24,256]{1,0:T(8,128)S(1)}, u32[]{:S(2)}, u32[]{:S(2)}) collective-permute-start(f32[24,256]{1,0:T(8,128)S(1)} %get-tuple-element.64), channel_id=1, source_target_pairs={{0,1},{1,0},{2,3},{3,2},{4,5},{5,4},{6,7},{7,6},{8,16},{9,17},{10,... | collective-permute-start | bytes 73736 | tf_op jit(solution)/shard_map/ppermute | solution.py:54

commit v6 on v5

--- a/solution.py
+++ b/solution.py
@@ -38,14 +38,12 @@
     for grp in range(sizes[0]):
         for dev in range(sizes[1]):
             own = (grp, dev)
-            step = 1 if (own[along] - offset) % 2 == 0 else -1
             partner = list(own)
-            partner[along] += step
+            partner[along] += 1 if (own[along] - offset) % 2 == 0 else -1
             if not 0 <= partner[along] < sizes[along]:
-                partner = list(own)
-                partner[1 - along] ^= 1
-                if partner[1 - along] >= sizes[1 - along]:
-                    partner = list(own)
+                if axis == "dev":
+                    continue
+                partner = [grp, dev ^ 1]
             route.append((grp * sizes[1] + dev, partner[0] * sizes[1] + partner[1]))
     return route
 

time: 19.8 us -> 23.1 us (1.17)
  the two profiles are of different devices: /device:TPU:0 before, /device:TPU:20 now
where the time goes in v6:
time: 23.1 us; the launch traced here: 22.9 us
  starting transfers between devices  10.5 us (45%)
  waiting for transfers between devices  6.59 us (29%)
  Pallas kernels  4.4 us (19%)
  between operations  1.39 us (6%)
    ppermute x11, starting transfers between devices, exchange(): return lax.ppermute(block, ('grp', 'dev'), partners(axis, offset))  10.5 us
    ppermute x11, waiting for transfers between devices, exchange(): return lax.ppermute(block, ('grp', 'dev'), partners(axis, offset))  6.59 us
    pallas_call x5, Pallas kernels, call(): pl.pallas_call(kernel, name=name, compiler_params=SMALL, out_shape=[shape...  1.74 us
    pallas_call x1, Pallas kernels, start(): pl.pallas_call(start_kernel, name='start', compiler_params=SMALL, out_sha...  1.44 us
    pallas_call x1, Pallas kernels, body(): pl.pallas_call(functools.partial(finish_kernel, True), name='finish_1', c...  1.22 us
  transfers between devices with their start and end apart: 11, of which 4 were waited for; matrix products, arithmetic and copies ran while one was open for 0% of the time, Pallas kernels for 5%

profile of v6, /device:TPU:20, one launch (start us, length us, event | category | flops | bytes accessed | tf_op | source)
XLA Modules:
  0.0 22.9 jit_solution(16197112061635720437)
XLA Ops:
  0.0 1.4 %start.1 = (f32[4,6,16,256]{3,2,1,0:T(8,128)S(1)}, f32[3,24,256]{2,1,0:T(8,128)S(1)}, f32[3,24,256]{2,1,0:T(8,128)S(1)}, f32[2,24,256]{2,1,0:T(8,128)S(1)}, f32[...) custom-call(f32[4,6,16,256]{3,2,1,0:T(8,128)} %fields.1, s32[4,6]{1,0:T(4,128)} %neighbors.1, ...), custom_call_target="tpu_custom_call" | custom-call | tf_op jit(solution)/shard_map/start/pallas_call | solution.py:421
  1.4 1.6 %collective-permute-start.2 = (f32[2,24,256]{2,1,0:T(8,128)S(1)}, f32[2,24,256]{2,1,0:T(8,128)S(1)}, u32[]{:S(2)}, u32[]{:S(2)}) collective-permute-start(f32[2,24,256]{2,1,0:T(8,128)S(1)} %get-tuple-element.46), channel_id=1, source_target_pairs={{0,8},{1,9},{2,10},{3,11},{4,12},{5,13},{6,14},{7,15},{8,0},{9,1},... | collective-permute-start | bytes 147464 | tf_op jit(solution)/shard_map/ppermute | solution.py:52
  3.1 0.0 collective-permute-start.3
  3.8 0.5 %collective-permute-start.1 = (f32[120,256]{1,0:T(8,128)S(1)}, f32[120,256]{1,0:T(8,128)S(1)}, u32[]{:S(2)}, u32[]{:S(2)}) collective-permute-start(f32[120,256]{1,0:T(8,128)S(1)} %get-tuple-element.45), channel_id=1, source_target_pairs={{0,8},{1,9},{2,10},{3,11},{4,12},{5,13},{6,14},{7,15},{8,0},{9,1},... | collective-permute-start | bytes 368648 | tf_op jit(solution)/shard_map/ppermute | solution.py:52
  4.3 0.2 collective-permute-start
  5.2 0.4 %collective-permute-done.2.faces = f32[2,24,256]{2,1,0:T(8,128)S(1)} collective-permute-done((f32[2,24,256]{2,1,0:T(8,128)S(1)}, f32[2,24,256]{2,1,0:T(8,128)S(1)}, u32[]{:S(2)}, u32[]{:S(2)}) %collective-permute-start.2) | collective-permute-done | bytes 49184 | tf_op jit(solution)/shard_map/ppermute | solution.py:52
  5.6 0.0 collective-permute-done.3.faces_dev
  5.6 0.1 faces.1
  5.7 0.1 collective-permute-start.4
  5.7 3.4 %collective-permute-start.5 = (f32[2,24,256]{2,1,0:T(8,128)S(1)}, f32[2,24,256]{2,1,0:T(8,128)S(1)}, u32[]{:S(2)}, u32[]{:S(2)}) collective-permute-start(f32[2,24,256]{2,1,0:T(8,128)S(1)} %get-tuple-element.52), channel_id=1, source_target_pairs={{1,2},{2,1},{3,4},{4,3},{5,6},{6,5},{9,10},{10,9},{11,12},{12,11},... | collective-permute-start | bytes 147464 | tf_op jit(solution)/shard_map/ppermute | solution.py:52
  9.2 0.5 %collective-permute-start.6 = (f32[24,256]{1,0:T(8,128)S(1)}, f32[24,256]{1,0:T(8,128)S(1)}, u32[]{:S(2)}, u32[]{:S(2)}) collective-permute-start(f32[24,256]{1,0:T(8,128)S(1)} %get-tuple-element.54), channel_id=1, source_target_pairs={{0,1},{1,0},{2,3},{3,2},{4,5},{5,4},{6,7},{7,6},{8,16},{9,17},{10,... | collective-permute-start | bytes 73736 | tf_op jit(solution)/shard_map/ppermute | solution.py:52
  9.7 0.0 collective-permute-done.block_dev
  9.7 0.0 collective-permute-done.1.block_grp
  9.7 0.6 %inner_0.1 = (f32[2,384,128]{2,1,0:T(8,128)S(1)}, f32[24,256]{1,0:T(8,128)S(1)}, f32[24,256]{1,0:T(8,128)S(1)}, f32[24,256]{1,0:T(8,128)S(1)}, f32[24,256]{1,0:T(8,128)S(1)}) custom-call(f32[24,256]{1,0:T(8,128)S(1)} %broadcast_in_dim.21.mask_dev, f32[24,256]{1,0:T(8,128)S(1)} %broadcast_in_dim.23.mask_grp, f32[4,24,128]{2,1,0:T(8,128)S(1)} %get-tuple-element.35.scale, ...), custom_call_target="tpu_custom_call" | custom-call | flops 4194304 | bytes 2097152 | tf_op jit(solution)/shard_map/inner_0/pallas_call | solution.py:407
  10.3 2.8 %collective-permute-done.6.refs_5_ = f32[24,256]{1,0:T(8,128)S(1)} collective-permute-done((f32[24,256]{1,0:T(8,128)S(1)}, f32[24,256]{1,0:T(8,128)S(1)}, u32[]{:S(2)}, u32[]{:S(2)}) %collective-permute-start.6) | collective-permute-done | bytes 24608 | tf_op jit(solution)/shard_map/ppermute | solution.py:52
  13.1 0.0 collective-permute-done.5.refs_3_
  13.1 0.0 collective-permute-done.4.refs_2_
  13.1 0.6 %finish_0.1 = (f32[2,384,128]{2,1,0:T(8,128)S(1)}, f32[3,24,256]{2,1,0:T(8,128)S(1)}, f32[3,24,256]{2,1,0:T(8,128)S(1)}, f32[2,24,256]{2,1,0:T(8,128)S(1)}, f32[...) custom-call(f32[4,24,128]{2,1,0:T(8,128)S(1)} %get-tuple-element.35.scale, ...), custom_call_target="tpu_custom_call" | custom-call | flops 1048576 | bytes 1048576 | tf_op jit(solution)/shard_map/finish_0/pallas_call | solution.py:407
  13.7 0.1 collective-permute-start.7
  13.8 2.8 %collective-permute-start.8 = (f32[2,24,256]{2,1,0:T(8,128)S(1)}, f32[2,24,256]{2,1,0:T(8,128)S(1)}, u32[]{:S(2)}, u32[]{:S(2)}) collective-permute-start(f32[2,24,256]{2,1,0:T(8,128)S(1)} %get-tuple-element.62), channel_id=1, source_target_pairs={{1,2},{2,1},{3,4},{4,3},{5,6},{6,5},{9,10},{10,9},{11,12},{12,11},... | collective-permute-start | bytes 147464 | tf_op jit(solution)/shard_map/ppermute | solution.py:52
  16.6 1.3 %collective-permute-start.9 = (f32[24,256]{1,0:T(8,128)S(1)}, f32[24,256]{1,0:T(8,128)S(1)}, u32[]{:S(2)}, u32[]{:S(2)}) collective-permute-start(f32[24,256]{1,0:T(8,128)S(1)} %get-tuple-element.63), channel_id=1, source_target_pairs={{0,8},{1,9},{2,10},{3,11},{4,12},{5,13},{6,14},{7,15},{8,0},{9,1},... | collective-permute-start | bytes 73736 | tf_op jit(solution)/shard_map/ppermute | solution.py:52
  17.9 0.0 collective-permute-start.10
  17.9 0.5 %inner_1.1.partial = f32[2,384,128]{2,1,0:T(8,128)S(1)} custom-call(f32[2,384,128]{2,1,0:T(8,128)S(1)} %get-tuple-element.58.state, f32[4,24,128]{2,1,0:T(8,128)S(1)} %get-tuple-element.35.scale), custom_call_target="tpu_custom_call" | custom-call | flops 4194304 | bytes 2097152 | tf_op jit(solution)/shard_map/inner_1/pallas_call | solution.py:407
  18.3 2.1 %collective-permute-done.9.refs_4_ = f32[24,256]{1,0:T(8,128)S(1)} collective-permute-done((f32[24,256]{1,0:T(8,128)S(1)}, f32[24,256]{1,0:T(8,128)S(1)}, u32[]{:S(2)}, u32[]{:S(2)}) %collective-permute-start.9) | collective-permute-done | bytes 24608 | tf_op jit(solution)/shard_map/ppermute | solution.py:52
  20.5 1.2 %collective-permute-done.10.refs_5_ = f32[24,256]{1,0:T(8,128)S(1)} collective-permute-done((f32[24,256]{1,0:T(8,128)S(1)}, f32[24,256]{1,0:T(8,128)S(1)}, u32[]{:S(2)}, u32[]{:S(2)}) %collective-permute-start.10) | collective-permute-done | bytes 24608 | tf_op jit(solution)/shard_map/ppermute | solution.py:52
  21.7 0.0 collective-permute-done.7.refs_2_
  21.7 0.0 collective-permute-done.8.refs_3_
  21.7 1.2 %finish_1.1 = f32[4,6,16,256]{3,2,1,0:T(8,128)} custom-call(f32[4,24,128]{2,1,0:T(8,128)S(1)} %get-tuple-element.35.scale, f32[3,48,192]{2,1,0:T(8,128)S(1)} %get-tuple-element.36.select, f32[2,384,128]{2,1,0:T(8,128)S(1)} %inner_1.1.partial, f32[3,24,256]{2,1,0:T(8,128)S(1)} %get-tuple-element.59.refs_0_, f32[3,24,256]{2,1,0:T(8,128)S(1)} %get-tuple-element.60.refs_1_, ...), custom_call_target="tpu_custom_call" | custom-call | tf_op jit(solution)/shard_map/finish_1/pallas_call | solution.py:481
  (3 shorter events, 0.0 us)
Async XLA Ops:
  1.4 4.2 %collective-permute-start.2 = (f32[2,24,256]{2,1,0:T(8,128)S(1)}, f32[2,24,256]{2,1,0:T(8,128)S(1)}, u32[]{:S(2)}, u32[]{:S(2)}) collective-permute-start(f32[2,24,256]{2,1,0:T(8,128)S(1)} %get-tuple-element.46), channel_id=1, source_target_pairs={{0,8},{1,9},{2,10},{3,11},{4,12},{5,13},{6,14},{7,15},{8,0},{9,1},... | collective-permute-start | bytes 147464 | tf_op jit(solution)/shard_map/ppermute | solution.py:52
  3.1 2.5 %collective-permute-start.3 = (f32[2,24,256]{2,1,0:T(8,128)S(1)}, f32[2,24,256]{2,1,0:T(8,128)S(1)}, u32[]{:S(2)}, u32[]{:S(2)}) collective-permute-start(f32[2,24,256]{2,1,0:T(8,128)S(1)} %get-tuple-element.47), channel_id=1, source_target_pairs={{0,1},{1,0},{2,3},{3,2},{4,5},{5,4},{6,7},{7,6},{8,9},{9,8},{10,11... | collective-permute-start | bytes 147464 | tf_op jit(solution)/shard_map/ppermute | solution.py:52
  3.8 5.9 %collective-permute-start.1 = (f32[120,256]{1,0:T(8,128)S(1)}, f32[120,256]{1,0:T(8,128)S(1)}, u32[]{:S(2)}, u32[]{:S(2)}) collective-permute-start(f32[120,256]{1,0:T(8,128)S(1)} %get-tuple-element.45), channel_id=1, source_target_pairs={{0,8},{1,9},{2,10},{3,11},{4,12},{5,13},{6,14},{7,15},{8,0},{9,1},... | collective-permute-start | bytes 368648 | tf_op jit(solution)/shard_map/ppermute | solution.py:52
  4.3 5.4 %collective-permute-start = (f32[96,256]{1,0:T(8,128)S(1)}, f32[96,256]{1,0:T(8,128)S(1)}, u32[]{:S(2)}, u32[]{:S(2)}) collective-permute-start(f32[96,256]{1,0:T(8,128)S(1)} %get-tuple-element.44), channel_id=1, source_target_pairs={{0,1},{1,0},{2,3},{3,2},{4,5},{5,4},{6,7},{7,6},{8,9},{9,8},{10,11... | collective-permute-start | bytes 294920 | tf_op jit(solution)/shard_map/ppermute | solution.py:52
  5.7 7.4 %collective-permute-start.4 = (f32[3,24,256]{2,1,0:T(8,128)S(1)}, f32[3,24,256]{2,1,0:T(8,128)S(1)}, u32[]{:S(2)}, u32[]{:S(2)}) collective-permute-start(f32[3,24,256]{2,1,0:T(8,128)S(1)} %get-tuple-element.51), channel_id=1, source_target_pairs={{0,1},{1,0},{2,3},{3,2},{4,5},{5,4},{6,7},{7,6},{8,9},{9,8},{10,11... | collective-permute-start | bytes 221192 | tf_op jit(solution)/shard_map/ppermute | solution.py:52
  5.7 7.3 %collective-permute-start.5 = (f32[2,24,256]{2,1,0:T(8,128)S(1)}, f32[2,24,256]{2,1,0:T(8,128)S(1)}, u32[]{:S(2)}, u32[]{:S(2)}) collective-permute-start(f32[2,24,256]{2,1,0:T(8,128)S(1)} %get-tuple-element.52), channel_id=1, source_target_pairs={{1,2},{2,1},{3,4},{4,3},{5,6},{6,5},{9,10},{10,9},{11,12},{12,11},... | collective-permute-start | bytes 147464 | tf_op jit(solution)/shard_map/ppermute | solution.py:52
  9.2 3.9 %collective-permute-start.6 = (f32[24,256]{1,0:T(8,128)S(1)}, f32[24,256]{1,0:T(8,128)S(1)}, u32[]{:S(2)}, u32[]{:S(2)}) collective-permute-start(f32[24,256]{1,0:T(8,128)S(1)} %get-tuple-element.54), channel_id=1, source_target_pairs={{0,1},{1,0},{2,3},{3,2},{4,5},{5,4},{6,7},{7,6},{8,16},{9,17},{10,... | collective-permute-start | bytes 73736 | tf_op jit(solution)/shard_map/ppermute | solution.py:52
  13.7 8.0 %collective-permute-start.7 = (f32[2,24,256]{2,1,0:T(8,128)S(1)}, f32[2,24,256]{2,1,0:T(8,128)S(1)}, u32[]{:S(2)}, u32[]{:S(2)}) collective-permute-start(f32[2,24,256]{2,1,0:T(8,128)S(1)} %get-tuple-element.61), channel_id=1, source_target_pairs={{0,1},{1,0},{2,3},{3,2},{4,5},{5,4},{6,7},{7,6},{8,9},{9,8},{10,11... | collective-permute-start | bytes 147464 | tf_op jit(solution)/shard_map/ppermute | solution.py:52
  13.8 7.9 %collective-permute-start.8 = (f32[2,24,256]{2,1,0:T(8,128)S(1)}, f32[2,24,256]{2,1,0:T(8,128)S(1)}, u32[]{:S(2)}, u32[]{:S(2)}) collective-permute-start(f32[2,24,256]{2,1,0:T(8,128)S(1)} %get-tuple-element.62), channel_id=1, source_target_pairs={{1,2},{2,1},{3,4},{4,3},{5,6},{6,5},{9,10},{10,9},{11,12},{12,11},... | collective-permute-start | bytes 147464 | tf_op jit(solution)/shard_map/ppermute | solution.py:52
  16.6 3.9 %collective-permute-start.9 = (f32[24,256]{1,0:T(8,128)S(1)}, f32[24,256]{1,0:T(8,128)S(1)}, u32[]{:S(2)}, u32[]{:S(2)}) collective-permute-start(f32[24,256]{1,0:T(8,128)S(1)} %get-tuple-element.63), channel_id=1, source_target_pairs={{0,8},{1,9},{2,10},{3,11},{4,12},{5,13},{6,14},{7,15},{8,0},{9,1},... | collective-permute-start | bytes 73736 | tf_op jit(solution)/shard_map/ppermute | solution.py:52
  17.9 3.8 %collective-permute-start.10 = (f32[24,256]{1,0:T(8,128)S(1)}, f32[24,256]{1,0:T(8,128)S(1)}, u32[]{:S(2)}, u32[]{:S(2)}) collective-permute-start(f32[24,256]{1,0:T(8,128)S(1)} %get-tuple-element.64), channel_id=1, source_target_pairs={{0,1},{1,0},{2,3},{3,2},{4,5},{5,4},{6,7},{7,6},{8,16},{9,17},{10,... | collective-permute-start | bytes 73736 | tf_op jit(solution)/shard_map/ppermute | solution.py:52

commit v7 on v5

--- a/solution.py
+++ b/solution.py
@@ -318,53 +318,66 @@
             partial[h, pl.ds(rows + 2 * tile, tile), :] = flow[2 * tile :]
 
 
-def finish_kernel(last_step, scale, select, partial, *refs):
-    own, got_flat = refs[0:2], refs[2:4]
-    own_deep = [ref[2] for ref in own]
-    if last_step:
-        got_deep = [ref[...] for ref in refs[4:6]]
-        result, done, blocks, sent = refs[6:10]
-    else:
-        known, deep_b, relayed, z_low, z_high = refs[4:9]
-        got_deep = [jnp.where(relayed[...] > 0.5, got_flat[0][2], known[...]), deep_b[...]]
-        own_deep = [z_low[...], z_high[...]]
-        done, outs, sends = refs[9], refs[10:12], refs[12:16]
-    ghosts = []
-    for axis in range(3):
-        got = [ref[axis] for ref in got_flat] if axis < 2 else got_deep
-        mine = [ref[axis] for ref in own] if axis < 2 else own_deep
-        tables = jnp.concatenate([*mine, *got], axis=0)
-        near = tables.astype(jnp.bfloat16)
-        rest = (tables - near.astype(jnp.float32)).astype(jnp.bfloat16)
-        both = jnp.concatenate([near, rest], axis=0)
-        pair = jnp.dot(select[axis].astype(jnp.bfloat16), both, preferred_element_type=jnp.float32)
-        weight = jnp.concatenate([scale[axis]] * 2, axis=1)
-        ghosts += [weight * pair[:ROWS], weight * pair[ROWS:]]
+def ghosts_of(axis, scale, select, tables):
+    tables = jnp.concatenate(tables, axis=0)
+    near = tables.astype(jnp.bfloat16)
+    rest = (tables - near.astype(jnp.float32)).astype(jnp.bfloat16)
+    both = jnp.concatenate([near, rest], axis=0)
+    pair = jnp.dot(select[axis].astype(jnp.bfloat16), both, preferred_element_type=jnp.float32)
+    weight = jnp.concatenate([scale[axis]] * 2, axis=1)
+    return weight * pair[:ROWS], weight * pair[ROWS:]
+
+
+def side_by_side(low, high, even):
+    return jnp.where(even, low, high), jnp.where(even, high, low)
+
+
+def sides_kernel(scale, select, partial, low, high, flat_a, flat_b, done):
+    sources = (low, high, flat_a, flat_b)
+    x_low, x_high = ghosts_of(0, scale, select, [ref[0] for ref in sources])
+    y_low, y_high = ghosts_of(1, scale, select, [ref[1] for ref in sources])
     lane = iota((ROWS, HALF), 1)
-    start_y, end_y = lane < EDGE, lane >= HALF - EDGE
-    ends_z = (lane % EDGE == 0) | (lane % EDGE == EDGE - 1)
-    even_group, even_place = (lane // EDGE) % 2 == 0, lane % 2 == 0
-    y_pairs, z_pairs = [], []
+    inside = (lane < EDGE, lane >= HALF - EDGE)
+    even = (lane // EDGE) % 2 == 0
+    pairs = []
     for h in range(2):
         lanes = slice(h * HALF, (h + 1) * HALF)
-        low, high = ghosts[2][:, lanes], turned(ghosts[3][:, lanes], -EDGE)
-        y_pairs.append((jnp.where(even_group, low, high), jnp.where(even_group, high, low)))
-        low, high = ghosts[4][:, lanes], turned(ghosts[5][:, lanes], EDGE - 1)
-        z_pairs.append((jnp.where(even_place, low, high), jnp.where(even_place, high, low)))
+        pairs.append(side_by_side(y_low[:, lanes], turned(y_high[:, lanes], -EDGE), even))
+    for x in range(EDGE):
+        ends = turned(pairs[x // GROUPS][x % 2], -EDGE * (x % GROUPS))
+        for h, value in enumerate(plane_at(partial, x)):
+            value = value + jnp.where(inside[h], ends, 0.0)
+            if x == 0:
+                value = value + x_low[:, h * HALF : (h + 1) * HALF]
+            if x == EDGE - 1:
+                value = value + x_high[:, h * HALF : (h + 1) * HALF]
+            done[h, pl.ds(x * ROWS, ROWS), :] = value
+
+
+def finish_kernel(last_step, scale, select, partial, *refs):
+    if last_step:
+        low, high, deep_a, deep_b = refs[:4]
+        tables = [low[2], high[2], deep_a[...], deep_b[...]]
+        result, done, blocks, sent = refs[4:8]
+    else:
+        known, deep_b, flat_a, relayed, z_low, z_high = refs[:6]
+        tables = [z_low[...], z_high[...], jnp.where(relayed[...] > 0.5, flat_a[2], known[...]), deep_b[...]]
+        done, outs, sends = refs[6], refs[7:9], refs[9:13]
+    z_low, z_high = ghosts_of(2, scale, select, tables)
+    lane = iota((ROWS, HALF), 1)
+    ends_z = (lane % EDGE == 0) | (lane % EDGE == EDGE - 1)
+    pairs = []
+    for h in range(2):
+        lanes = slice(h * HALF, (h + 1) * HALF)
+        pairs.append(side_by_side(z_low[:, lanes], turned(z_high[:, lanes], EDGE - 1), lane % 2 == 0))
     packer = None if last_step else Packer()
     copies = []
     for x in range(EDGE):
-        halves = list(plane_at(partial, x))
-        ends = turned(y_pairs[x // GROUPS][x % 2], -EDGE * (x % GROUPS))
-        for h in range(2):
-            value = halves[h] + jnp.where(start_y if h == 0 else end_y, ends, 0.0)
-            value = value + jnp.where(ends_z, turned(z_pairs[h][x % 2], -x), 0.0)
-            if x == 0:
-                value = value + ghosts[0][:, h * HALF : (h + 1) * HALF]
-            if x == EDGE - 1:
-                value = value + ghosts[1][:, h * HALF : (h + 1) * HALF]
+        halves = []
+        for h, value in enumerate(plane_at(partial, x)):
+            value = value + jnp.where(ends_z, turned(pairs[h][x % 2], -x), 0.0)
             done[h, pl.ds(x * ROWS, ROWS), :] = value
-            halves[h] = value
+            halves.append(value)
         if not last_step:
             packer.add(x, *halves)
         elif x % 8 == 7:
@@ -468,11 +481,12 @@
         4 << 20,
         [pltpu.VMEM(STATE, jnp.float32)],
     )
+    (partial,) = call(sides_kernel, "sides_0", [STATE], [scale, select, partial, new_low, new_high, flat_a, flat_b])
     state, *tables = call(
         functools.partial(finish_kernel, False),
         "finish_0",
         TABLES,
-        [scale, select, partial, new_low, new_high, flat_a, flat_b, deep_a, deep_b, relayed, z_low, z_high],
+        [scale, select, partial, deep_a, deep_b, flat_a, relayed, z_low, z_high],
     )
     own, sends = tables[:2], tables[2:]
     flat_a = exchange(sends[0], "dev", 0)
@@ -480,19 +494,20 @@
     deep_a = exchange(sends[2], "grp", 0)
     deep_b = exchange(sends[3], "grp", 1)
     (partial,) = call(inner_kernel, "inner_1", [STATE], [state, scale], 4 << 20)
+    (partial,) = call(sides_kernel, "sides_1", [STATE], [scale, select, partial, *own, flat_a, flat_b])
     return pl.pallas_call(
         functools.partial(finish_kernel, True),
         name="finish_1",
         compiler_params=SMALL,
         out_shape=shaped(fields.shape),
-        in_specs=[spec(VECTOR)] * 9,
+        in_specs=[spec(VECTOR)] * 7,
         out_specs=spec(pl.ANY),
         scratch_shapes=[
             pltpu.VMEM(STATE, jnp.float32),
             pltpu.VMEM(fields.shape, jnp.float32),
             pltpu.SemaphoreType.DMA((2,)),
         ],
-    )(scale, select, partial, *own, flat_a, flat_b, deep_a, deep_b)
+    )(scale, select, partial, *own, deep_a, deep_b)
 
 
 def solution(mesh):

time: 19.8 us -> 19.7 us (level)
  waiting for transfers between devices: 4.47 us -> 3.76 us
  Pallas kernels: 4.4 us -> 4.92 us
    ppermute x11, waiting for transfers between devices: 4.47 us -> 3.76 us  [exchange(): return lax.ppermute(block, ('grp', 'dev'), partners(axis, offset))]
    pallas_call x5 -> x7, Pallas kernels: 1.74 us -> 2.34 us  [call(): pl.pallas_call(kernel, name=name, compiler_params=SMALL, out_shape=[shape...]
  transfers between devices with their start and end apart: 11 -> 11, of which waited for: 3 -> 4; matrix products, arithmetic and copies ran while one was open for 0% -> 0% of each run, Pallas kernels for 6% -> 9%
where the time goes in v7:
time: 19.7 us; the launch traced here: 19.5 us
  starting transfers between devices  9.37 us (48%)
  Pallas kernels  4.92 us (25%)
  waiting for transfers between devices  3.76 us (19%)
  between operations  1.42 us (7%)
    ppermute x11, starting transfers between devices, exchange(): return lax.ppermute(block, ('grp', 'dev'), partners(axis, offset))  9.37 us
    ppermute x11, waiting for transfers between devices, exchange(): return lax.ppermute(block, ('grp', 'dev'), partners(axis, offset))  3.76 us
    pallas_call x7, Pallas kernels, call(): pl.pallas_call(kernel, name=name, compiler_params=SMALL, out_shape=[shape...  2.34 us
    pallas_call x1, Pallas kernels, start(): pl.pallas_call(start_kernel, name='start', compiler_params=SMALL, out_sha...  1.44 us
    pallas_call x1, Pallas kernels, body(): pl.pallas_call(functools.partial(finish_kernel, True), name='finish_1', c...  1.14 us
  transfers between devices with their start and end apart: 11, of which 4 were waited for; matrix products, arithmetic and copies ran while one was open for 0% of the time, Pallas kernels for 9%

profile of v7, /device:TPU:0, one launch (start us, length us, event | category | flops | bytes accessed | tf_op | source)
XLA Modules:
  0.0 19.5 jit_solution(17650860216916389276)
XLA Ops:
  0.0 1.4 %start.1 = (f32[4,6,16,256]{3,2,1,0:T(8,128)S(1)}, f32[3,24,256]{2,1,0:T(8,128)S(1)}, f32[3,24,256]{2,1,0:T(8,128)S(1)}, f32[2,24,256]{2,1,0:T(8,128)S(1)}, f32[...) custom-call(f32[4,6,16,256]{3,2,1,0:T(8,128)} %fields.1, s32[4,6]{1,0:T(4,128)} %neighbors.1, ...), custom_call_target="tpu_custom_call" | custom-call | tf_op jit(solution)/shard_map/start/pallas_call | solution.py:436
  1.4 3.1 %collective-permute-start.2 = (f32[2,24,256]{2,1,0:T(8,128)S(1)}, f32[2,24,256]{2,1,0:T(8,128)S(1)}, u32[]{:S(2)}, u32[]{:S(2)}) collective-permute-start(f32[2,24,256]{2,1,0:T(8,128)S(1)} %get-tuple-element.46), channel_id=1, source_target_pairs={{0,8},{1,9},{2,10},{3,11},{4,12},{5,13},{6,14},{7,15},{8,0},{9,1},... | collective-permute-start | bytes 147464 | tf_op jit(solution)/shard_map/ppermute | solution.py:54
  4.5 0.0 collective-permute-start.3
  5.2 0.1 collective-permute-start.1
  5.4 0.5 %collective-permute-start = (f32[96,256]{1,0:T(8,128)S(1)}, f32[96,256]{1,0:T(8,128)S(1)}, u32[]{:S(2)}, u32[]{:S(2)}) collective-permute-start(f32[96,256]{1,0:T(8,128)S(1)} %get-tuple-element.44), channel_id=1, source_target_pairs={{0,1},{1,0},{2,3},{3,2},{4,5},{5,4},{6,7},{7,6},{8,9},{9,8},{10,11... | collective-permute-start | bytes 294920 | tf_op jit(solution)/shard_map/ppermute | solution.py:54
  6.5 0.1 collective-permute-done.2.faces
  6.6 0.0 collective-permute-done.3.faces_dev
  6.6 0.1 faces.1
  6.7 0.1 collective-permute-start.4
  6.8 2.1 %collective-permute-start.5 = (f32[2,24,256]{2,1,0:T(8,128)S(1)}, f32[2,24,256]{2,1,0:T(8,128)S(1)}, u32[]{:S(2)}, u32[]{:S(2)}) collective-permute-start(f32[2,24,256]{2,1,0:T(8,128)S(1)} %get-tuple-element.52), channel_id=1, source_target_pairs={{0,8},{1,2},{2,1},{3,4},{4,3},{5,6},{6,5},{7,15},{8,0},{9,10},{10,... | collective-permute-start | bytes 147464 | tf_op jit(solution)/shard_map/ppermute | solution.py:54
  8.8 0.0 collective-permute-start.6
  8.9 0.0 collective-permute-done.block_dev
  8.9 2.2 %collective-permute-done.1.block_grp = f32[120,256]{1,0:T(8,128)S(1)} collective-permute-done((f32[120,256]{1,0:T(8,128)S(1)}, f32[120,256]{1,0:T(8,128)S(1)}, u32[]{:S(2)}, u32[]{:S(2)}) %collective-permute-start.1) | collective-permute-done | bytes 122912 | tf_op jit(solution)/shard_map/ppermute | solution.py:54
  11.0 0.5 %inner_0.1 = (f32[2,384,128]{2,1,0:T(8,128)S(1)}, f32[24,256]{1,0:T(8,128)S(1)}, f32[24,256]{1,0:T(8,128)S(1)}, f32[24,256]{1,0:T(8,128)S(1)}, f32[24,256]{1,0:T(8,128)S(1)}) custom-call(f32[24,256]{1,0:T(8,128)S(1)} %broadcast_in_dim.21.mask_dev, f32[24,256]{1,0:T(8,128)S(1)} %broadcast_in_dim.23.mask_grp, f32[4,24,128]{2,1,0:T(8,128)S(1)} %get-tuple-element.35.scale, ...), custom_call_target="tpu_custom_call" | custom-call | flops 4194304 | bytes 2097152 | tf_op jit(solution)/shard_map/inner_0/pallas_call | solution.py:422
  11.6 0.0 collective-permute-done.5.flat_b
  11.6 0.0 collective-permute-done.4.flat_a.refs_2_
  11.6 0.3 %sides_0.1.partial = f32[2,384,128]{2,1,0:T(8,128)S(1)} custom-call(f32[4,24,128]{2,1,0:T(8,128)S(1)} %get-tuple-element.35.scale, f32[3,48,192]{2,1,0:T(8,128)S(1)} %get-tuple-element.36.select, f32[2,384,128]{2,1,0:T(8,128)S(1)} %get-tuple-element.50.partial, f32[3,24,256]{2,1,0:T(8,128)S(1)} %get-tuple-element.48.new_low.low, ...), custom_call_target="tpu_custom_call" | custom-call | flops 1048576 | bytes 1048576 | tf_op jit(solution)/shard_map/sides_0/pallas_call | solution.py:422
  11.9 0.0 collective-permute-done.6.refs_1_
  12.0 0.6 %finish_0.1 = (f32[2,384,128]{2,1,0:T(8,128)S(1)}, f32[3,24,256]{2,1,0:T(8,128)S(1)}, f32[3,24,256]{2,1,0:T(8,128)S(1)}, f32[2,24,256]{2,1,0:T(8,128)S(1)}, f32[...) custom-call(f32[4,24,128]{2,1,0:T(8,128)S(1)} %get-tuple-element.35.scale, ...), custom_call_target="tpu_custom_call" | custom-call | flops 1048576 | bytes 1048576 | tf_op jit(solution)/shard_map/finish_0/pallas_call | solution.py:422
  12.5 0.1 collective-permute-start.7
  12.6 1.9 %collective-permute-start.8 = (f32[2,24,256]{2,1,0:T(8,128)S(1)}, f32[2,24,256]{2,1,0:T(8,128)S(1)}, u32[]{:S(2)}, u32[]{:S(2)}) collective-permute-start(f32[2,24,256]{2,1,0:T(8,128)S(1)} %get-tuple-element.62), channel_id=1, source_target_pairs={{0,8},{1,2},{2,1},{3,4},{4,3},{5,6},{6,5},{7,15},{8,0},{9,10},{10,... | collective-permute-start | bytes 147464 | tf_op jit(solution)/shard_map/ppermute | solution.py:54
  14.5 0.2 %collective-permute-start.9 = (f32[24,256]{1,0:T(8,128)S(1)}, f32[24,256]{1,0:T(8,128)S(1)}, u32[]{:S(2)}, u32[]{:S(2)}) collective-permute-start(f32[24,256]{1,0:T(8,128)S(1)} %get-tuple-element.63), channel_id=1, source_target_pairs={{0,8},{1,9},{2,10},{3,11},{4,12},{5,13},{6,14},{7,15},{8,0},{9,1},... | collective-permute-start | bytes 73736 | tf_op jit(solution)/shard_map/ppermute | solution.py:54
  14.7 1.3 %collective-permute-start.10 = (f32[24,256]{1,0:T(8,128)S(1)}, f32[24,256]{1,0:T(8,128)S(1)}, u32[]{:S(2)}, u32[]{:S(2)}) collective-permute-start(f32[24,256]{1,0:T(8,128)S(1)} %get-tuple-element.64), channel_id=1, source_target_pairs={{0,1},{1,0},{2,3},{3,2},{4,5},{5,4},{6,7},{7,6},{8,16},{9,17},{10,... | collective-permute-start | bytes 73736 | tf_op jit(solution)/shard_map/ppermute | solution.py:54
  16.0 0.5 %inner_1.1.partial = f32[2,384,128]{2,1,0:T(8,128)S(1)} custom-call(f32[2,384,128]{2,1,0:T(8,128)S(1)} %get-tuple-element.58.state, f32[4,24,128]{2,1,0:T(8,128)S(1)} %get-tuple-element.35.scale), custom_call_target="tpu_custom_call" | custom-call | flops 4194304 | bytes 2097152 | tf_op jit(solution)/shard_map/inner_1/pallas_call | solution.py:422
  16.5 0.0 collective-permute-done.7.flat_a
  16.5 0.3 %collective-permute-done.8.flat_b = f32[2,24,256]{2,1,0:T(8,128)S(1)} collective-permute-done((f32[2,24,256]{2,1,0:T(8,128)S(1)}, f32[2,24,256]{2,1,0:T(8,128)S(1)}, u32[]{:S(2)}, u32[]{:S(2)}) %collective-permute-start.8) | collective-permute-done | bytes 49184 | tf_op jit(solution)/shard_map/ppermute | solution.py:54
  16.8 0.3 %sides_1.1.partial = f32[2,384,128]{2,1,0:T(8,128)S(1)} custom-call(f32[4,24,128]{2,1,0:T(8,128)S(1)} %get-tuple-element.35.scale, f32[3,48,192]{2,1,0:T(8,128)S(1)} %get-tuple-element.36.select, f32[2,384,128]{2,1,0:T(8,128)S(1)} %inner_1.1.partial, f32[3,24,256]{2,1,0:T(8,128)S(1)} %get-tuple-element.59.low.refs_0_, ...), custom_call_target="tpu_custom_call" | custom-call | flops 1048576 | bytes 1048576 | tf_op jit(solution)/shard_map/sides_1/pallas_call | solution.py:422
  17.1 1.2 %collective-permute-done.9.refs_2_ = f32[24,256]{1,0:T(8,128)S(1)} collective-permute-done((f32[24,256]{1,0:T(8,128)S(1)}, f32[24,256]{1,0:T(8,128)S(1)}, u32[]{:S(2)}, u32[]{:S(2)}) %collective-permute-start.9) | collective-permute-done | bytes 24608 | tf_op jit(solution)/shard_map/ppermute | solution.py:54
  18.3 0.0 collective-permute-done.10.refs_3_
  18.3 1.1 %finish_1.1 = f32[4,6,16,256]{3,2,1,0:T(8,128)} custom-call(f32[4,24,128]{2,1,0:T(8,128)S(1)} %get-tuple-element.35.scale, f32[3,48,192]{2,1,0:T(8,128)S(1)} %get-tuple-element.36.select, f32[2,384,128]{2,1,0:T(8,128)S(1)} %sides_1.1.partial, f32[3,24,256]{2,1,0:T(8,128)S(1)} %get-tuple-element.59.low.refs_0_, ...), custom_call_target="tpu_custom_call" | custom-call | tf_op jit(solution)/shard_map/finish_1/pallas_call | solution.py:498
  (3 shorter events, 0.0 us)
Async XLA Ops:
  1.4 5.2 %collective-permute-start.2 = (f32[2,24,256]{2,1,0:T(8,128)S(1)}, f32[2,24,256]{2,1,0:T(8,128)S(1)}, u32[]{:S(2)}, u32[]{:S(2)}) collective-permute-start(f32[2,24,256]{2,1,0:T(8,128)S(1)} %get-tuple-element.46), channel_id=1, source_target_pairs={{0,8},{1,9},{2,10},{3,11},{4,12},{5,13},{6,14},{7,15},{8,0},{9,1},... | collective-permute-start | bytes 147464 | tf_op jit(solution)/shard_map/ppermute | solution.py:54
  4.5 2.1 %collective-permute-start.3 = (f32[2,24,256]{2,1,0:T(8,128)S(1)}, f32[2,24,256]{2,1,0:T(8,128)S(1)}, u32[]{:S(2)}, u32[]{:S(2)}) collective-permute-start(f32[2,24,256]{2,1,0:T(8,128)S(1)} %get-tuple-element.47), channel_id=1, source_target_pairs={{0,1},{1,0},{2,3},{3,2},{4,5},{5,4},{6,7},{7,6},{8,9},{9,8},{10,11... | collective-permute-start | bytes 147464 | tf_op jit(solution)/shard_map/ppermute | solution.py:54
  5.2 5.8 %collective-permute-start.1 = (f32[120,256]{1,0:T(8,128)S(1)}, f32[120,256]{1,0:T(8,128)S(1)}, u32[]{:S(2)}, u32[]{:S(2)}) collective-permute-start(f32[120,256]{1,0:T(8,128)S(1)} %get-tuple-element.45), channel_id=1, source_target_pairs={{0,8},{1,9},{2,10},{3,11},{4,12},{5,13},{6,14},{7,15},{8,0},{9,1},... | collective-permute-start | bytes 368648 | tf_op jit(solution)/shard_map/ppermute | solution.py:54
  5.4 3.5 %collective-permute-start = (f32[96,256]{1,0:T(8,128)S(1)}, f32[96,256]{1,0:T(8,128)S(1)}, u32[]{:S(2)}, u32[]{:S(2)}) collective-permute-start(f32[96,256]{1,0:T(8,128)S(1)} %get-tuple-element.44), channel_id=1, source_target_pairs={{0,1},{1,0},{2,3},{3,2},{4,5},{5,4},{6,7},{7,6},{8,9},{9,8},{10,11... | collective-permute-start | bytes 294920 | tf_op jit(solution)/shard_map/ppermute | solution.py:54
  6.7 4.9 %collective-permute-start.4 = (f32[3,24,256]{2,1,0:T(8,128)S(1)}, f32[3,24,256]{2,1,0:T(8,128)S(1)}, u32[]{:S(2)}, u32[]{:S(2)}) collective-permute-start(f32[3,24,256]{2,1,0:T(8,128)S(1)} %get-tuple-element.51), channel_id=1, source_target_pairs={{0,1},{1,0},{2,3},{3,2},{4,5},{5,4},{6,7},{7,6},{8,9},{9,8},{10,11... | collective-permute-start | bytes 221192 | tf_op jit(solution)/shard_map/ppermute | solution.py:54
  6.8 4.8 %collective-permute-start.5 = (f32[2,24,256]{2,1,0:T(8,128)S(1)}, f32[2,24,256]{2,1,0:T(8,128)S(1)}, u32[]{:S(2)}, u32[]{:S(2)}) collective-permute-start(f32[2,24,256]{2,1,0:T(8,128)S(1)} %get-tuple-element.52), channel_id=1, source_target_pairs={{0,8},{1,2},{2,1},{3,4},{4,3},{5,6},{6,5},{7,15},{8,0},{9,10},{10,... | collective-permute-start | bytes 147464 | tf_op jit(solution)/shard_map/ppermute | solution.py:54
  8.8 3.1 %collective-permute-start.6 = (f32[24,256]{1,0:T(8,128)S(1)}, f32[24,256]{1,0:T(8,128)S(1)}, u32[]{:S(2)}, u32[]{:S(2)}) collective-permute-start(f32[24,256]{1,0:T(8,128)S(1)} %get-tuple-element.54), channel_id=1, source_target_pairs={{0,1},{1,0},{2,3},{3,2},{4,5},{5,4},{6,7},{7,6},{8,16},{9,17},{10,... | collective-permute-start | bytes 73736 | tf_op jit(solution)/shard_map/ppermute | solution.py:54
  12.5 3.9 %collective-permute-start.7 = (f32[2,24,256]{2,1,0:T(8,128)S(1)}, f32[2,24,256]{2,1,0:T(8,128)S(1)}, u32[]{:S(2)}, u32[]{:S(2)}) collective-permute-start(f32[2,24,256]{2,1,0:T(8,128)S(1)} %get-tuple-element.61), channel_id=1, source_target_pairs={{0,1},{1,0},{2,3},{3,2},{4,5},{5,4},{6,7},{7,6},{8,9},{9,8},{10,11... | collective-permute-start | bytes 147464 | tf_op jit(solution)/shard_map/ppermute | solution.py:54
  12.6 4.2 %collective-permute-start.8 = (f32[2,24,256]{2,1,0:T(8,128)S(1)}, f32[2,24,256]{2,1,0:T(8,128)S(1)}, u32[]{:S(2)}, u32[]{:S(2)}) collective-permute-start(f32[2,24,256]{2,1,0:T(8,128)S(1)} %get-tuple-element.62), channel_id=1, source_target_pairs={{0,8},{1,2},{2,1},{3,4},{4,3},{5,6},{6,5},{7,15},{8,0},{9,10},{10,... | collective-permute-start | bytes 147464 | tf_op jit(solution)/shard_map/ppermute | solution.py:54
  14.5 3.8 %collective-permute-start.9 = (f32[24,256]{1,0:T(8,128)S(1)}, f32[24,256]{1,0:T(8,128)S(1)}, u32[]{:S(2)}, u32[]{:S(2)}) collective-permute-start(f32[24,256]{1,0:T(8,128)S(1)} %get-tuple-element.63), channel_id=1, source_target_pairs={{0,8},{1,9},{2,10},{3,11},{4,12},{5,13},{6,14},{7,15},{8,0},{9,1},... | collective-permute-start | bytes 73736 | tf_op jit(solution)/shard_map/ppermute | solution.py:54
  14.7 3.6 %collective-permute-start.10 = (f32[24,256]{1,0:T(8,128)S(1)}, f32[24,256]{1,0:T(8,128)S(1)}, u32[]{:S(2)}, u32[]{:S(2)}) collective-permute-start(f32[24,256]{1,0:T(8,128)S(1)} %get-tuple-element.64), channel_id=1, source_target_pairs={{0,1},{1,0},{2,3},{3,2},{4,5},{5,4},{6,7},{7,6},{8,16},{9,17},{10,... | collective-permute-start | bytes 73736 | tf_op jit(solution)/shard_map/ppermute | solution.py:54

commit v8 on v7

--- a/solution.py
+++ b/solution.py
@@ -1,4 +1,3 @@
-import functools
 import math
 
 import jax
@@ -24,6 +23,7 @@
 conc_rates = (0.08, 0.04)
 
 STATE = (2, EDGE * ROWS, HALF)
+SPARE = (2, (EDGE + 1) * ROWS, HALF)
 FACE = (ROWS, PLANE)
 SIDE = (3, ROWS, PLANE)
 SOURCES = 4
@@ -81,9 +81,11 @@
         taken = (self.group == at) | (self.group == (at + GROUPS - 1) % GROUPS)
         before = self.y[half][odd]
         self.y[half][odd] = ends if before is None else jnp.where(taken, ends, before)
-        taken = (self.place == x) | (self.place == (x + EDGE - 1) % EDGE)
+        at = EDGE - 1 - x
+        odd = at % 2
+        taken = (self.place == at) | (self.place == (at + EDGE - 1) % EDGE)
         for h, value in enumerate((left, right)):
-            moved = turned(value, x)
+            moved = turned(value, at)
             before = self.z[h][odd]
             self.z[h][odd] = moved if before is None else jnp.where(taken, moved, before)
 
@@ -332,7 +334,9 @@
     return jnp.where(even, low, high), jnp.where(even, high, low)
 
 
-def sides_kernel(scale, select, partial, low, high, flat_a, flat_b, done):
+def sides_kernel(scale, select, partial, low, high, flat_a, flat_b, done, blocks=None):
+    if blocks is not None:
+        blocks, done = done, blocks
     sources = (low, high, flat_a, flat_b)
     x_low, x_high = ghosts_of(0, scale, select, [ref[0] for ref in sources])
     y_low, y_high = ghosts_of(1, scale, select, [ref[1] for ref in sources])
@@ -352,50 +356,61 @@
             if x == EDGE - 1:
                 value = value + x_high[:, h * HALF : (h + 1) * HALF]
             done[h, pl.ds(x * ROWS, ROWS), :] = value
-
-
-def finish_kernel(last_step, scale, select, partial, *refs):
-    if last_step:
-        low, high, deep_a, deep_b = refs[:4]
-        tables = [low[2], high[2], deep_a[...], deep_b[...]]
-        result, done, blocks, sent = refs[4:8]
-    else:
-        known, deep_b, flat_a, relayed, z_low, z_high = refs[:6]
-        tables = [z_low[...], z_high[...], jnp.where(relayed[...] > 0.5, flat_a[2], known[...]), deep_b[...]]
-        done, outs, sends = refs[6], refs[7:9], refs[9:13]
+    if blocks is not None:
+        for slot in range(SLOTS):
+            for f in range(NFIELD):
+                for h in range(2):
+                    rows = pl.ds(f * SLOTS + slot, EDGE, stride=ROWS)
+                    blocks[slot, f, :, h * HALF : (h + 1) * HALF] = done[h, rows, :]
+
+
+def z_pairs(scale, select, tables):
     z_low, z_high = ghosts_of(2, scale, select, tables)
-    lane = iota((ROWS, HALF), 1)
-    ends_z = (lane % EDGE == 0) | (lane % EDGE == EDGE - 1)
-    pairs = []
-    for h in range(2):
-        lanes = slice(h * HALF, (h + 1) * HALF)
-        pairs.append(side_by_side(z_low[:, lanes], turned(z_high[:, lanes], EDGE - 1), lane % 2 == 0))
-    packer = None if last_step else Packer()
-    copies = []
+    even = iota((ROWS, HALF), 1) % 2 == 0
+    halves = [slice(h * HALF, (h + 1) * HALF) for h in range(2)]
+    return [side_by_side(z_low[:, lanes], turned(z_high[:, lanes], EDGE - 1), even) for lanes in halves]
+
+
+def ends_of(shape):
+    place = iota(shape, 1) % EDGE
+    return (place == 0) | (place == EDGE - 1)
+
+
+def finish_kernel(scale, select, partial, known, deep_b, flat_a, relayed, z_low, z_high, done, *outs):
+    deep_a = jnp.where(relayed[...] > 0.5, flat_a[2], known[...])
+    pairs = z_pairs(scale, select, [z_low[...], z_high[...], deep_a, deep_b[...]])
+    ends = ends_of((ROWS, HALF))
+    packer = Packer()
     for x in range(EDGE):
-        halves = []
+        halves, at = [], EDGE - 1 - x
         for h, value in enumerate(plane_at(partial, x)):
-            value = value + jnp.where(ends_z, turned(pairs[h][x % 2], -x), 0.0)
+            value = value + jnp.where(ends, turned(pairs[h][at % 2], -at), 0.0)
             done[h, pl.ds(x * ROWS, ROWS), :] = value
             halves.append(value)
-        if not last_step:
-            packer.add(x, *halves)
-        elif x % 8 == 7:
-            first = x - 7
-            for slot in range(SLOTS):
-                for f in range(NFIELD):
-                    rows = pl.ds(first * ROWS + f * SLOTS + slot, 8, stride=ROWS)
-                    for h in range(2):
-                        lanes = pl.ds(h * HALF, HALF)
-                        blocks[slot, f, first : first + 8, lanes] = done[h, rows, :]
-            part = pl.ds(first, 8)
-            copy = pltpu.make_async_copy(blocks.at[:, :, part], result.at[:, :, part], sent.at[x // 8])
-            copy.start()
-            copies.append(copy)
+        packer.add(x, *halves)
+    emit_faces(packer, done, outs[0:2], outs[2:6])
+
+
+def last_kernel(scale, select, partial, low, high, deep_a, deep_b, result, rows_of, blocks, sent):
+    for h, pair in enumerate(z_pairs(scale, select, [low[2], high[2], deep_a[...], deep_b[...]])):
+        for odd in range(2):
+            rows_of[h, odd] = pair[odd]
+    shape = (EDGE, HALF)
+    ends, even = ends_of(shape), iota(shape, 0) % 2 == 0
+    copies = []
+    for slot in range(SLOTS):
+        for f in range(NFIELD):
+            row = pl.ds(f * SLOTS + slot, 1)
+            for h in range(2):
+                both = [jnp.broadcast_to(rows_of[h, odd, row, :], shape) for odd in (1, 0)]
+                ghost = pltpu.roll(jnp.where(even, *both), HALF - EDGE + 1, 1, stride=1, stride_axis=0)
+                lanes = pl.ds(h * HALF, HALF)
+                blocks[slot, f, :, lanes] = partial[slot, f, :, lanes] + jnp.where(ends, ghost, 0.0)
+        copy = pltpu.make_async_copy(blocks.at[slot], result.at[slot], sent.at[slot])
+        copy.start()
+        copies.append(copy)
     for copy in copies:
         copy.wait()
-    if not last_step:
-        emit_faces(packer, done, outs, sends)
 
 
 def spec(space):
@@ -441,7 +456,7 @@
         in_specs=[spec(pl.ANY)] * len(arguments),
         out_specs=[spec(VECTOR)] * len(shapes),
         scratch_shapes=[
-            pltpu.VMEM(STATE, jnp.float32),
+            pltpu.VMEM(SPARE, jnp.float32),
             *(pltpu.SMEM(array.shape, jnp.int32) for array in arguments[1:]),
             pltpu.SemaphoreType.DMA((len(arguments) + 1,)),
         ],
@@ -479,11 +494,11 @@
         [STATE, FACE, FACE, FACE, FACE],
         [mask_dev, mask_grp, scale, fields, block_dev, block_grp, faces, low, high, new_low, new_high],
         4 << 20,
-        [pltpu.VMEM(STATE, jnp.float32)],
+        [pltpu.VMEM(SPARE, jnp.float32)],
     )
     (partial,) = call(sides_kernel, "sides_0", [STATE], [scale, select, partial, new_low, new_high, flat_a, flat_b])
     state, *tables = call(
-        functools.partial(finish_kernel, False),
+        finish_kernel,
         "finish_0",
         TABLES,
         [scale, select, partial, deep_a, deep_b, flat_a, relayed, z_low, z_high],
@@ -494,20 +509,20 @@
     deep_a = exchange(sends[2], "grp", 0)
     deep_b = exchange(sends[3], "grp", 1)
     (partial,) = call(inner_kernel, "inner_1", [STATE], [state, scale], 4 << 20)
-    (partial,) = call(sides_kernel, "sides_1", [STATE], [scale, select, partial, *own, flat_a, flat_b])
+    blocks, _ = call(sides_kernel, "sides_1", [fields.shape, SPARE], [scale, select, partial, *own, flat_a, flat_b])
     return pl.pallas_call(
-        functools.partial(finish_kernel, True),
+        last_kernel,
         name="finish_1",
         compiler_params=SMALL,
         out_shape=shaped(fields.shape),
         in_specs=[spec(VECTOR)] * 7,
         out_specs=spec(pl.ANY),
         scratch_shapes=[
-            pltpu.VMEM(STATE, jnp.float32),
+            pltpu.VMEM((2, 2, ROWS, HALF), jnp.float32),
             pltpu.VMEM(fields.shape, jnp.float32),
-            pltpu.SemaphoreType.DMA((2,)),
+            pltpu.SemaphoreType.DMA((SLOTS,)),
         ],
-    )(scale, select, partial, *own, deep_a, deep_b)
+    )(scale, select, blocks, *own, deep_a, deep_b)
 
 
 def solution(mesh):

time: 19.7 us -> 19.7 us (level)
  Pallas kernels: 4.92 us -> 5.75 us
  waiting for transfers between devices: 3.76 us -> 2.95 us
    pallas_call x7, Pallas kernels: 2.34 us -> 3.16 us  [call(): pl.pallas_call(kernel, name=name, compiler_params=SMALL, out_shape=[shape...]
    ppermute x11, waiting for transfers between devices: 3.76 us -> 2.95 us  [exchange(): return lax.ppermute(block, ('grp', 'dev'), partners(axis, offset))]
  transfers between devices with their start and end apart: 11 -> 11, of which waited for: 4 -> 4; matrix products, arithmetic and copies ran while one was open for 0% -> 0% of each run, Pallas kernels for 9% -> 13%
where the time goes in v8:
time: 19.7 us; the launch traced here: 19.5 us
  starting transfers between devices  9.37 us (48%)
  Pallas kernels  5.75 us (29%)
  waiting for transfers between devices  2.95 us (15%)
  between operations  1.41 us (7%)
    ppermute x11, starting transfers between devices, exchange(): return lax.ppermute(block, ('grp', 'dev'), partners(axis, offset))  9.37 us
    pallas_call x7, Pallas kernels, call(): pl.pallas_call(kernel, name=name, compiler_params=SMALL, out_shape=[shape...  3.16 us
    ppermute x11, waiting for transfers between devices, exchange(): return lax.ppermute(block, ('grp', 'dev'), partners(axis, offset))  2.95 us
    pallas_call x1, Pallas kernels, start(): pl.pallas_call(start_kernel, name='start', compiler_params=SMALL, out_sha...  1.44 us
    pallas_call x1, Pallas kernels, body(): pl.pallas_call(last_kernel, name='finish_1', compiler_params=SMALL, out_s...  1.15 us
  transfers between devices with their start and end apart: 11, of which 4 were waited for; matrix products, arithmetic and copies ran while one was open for 0% of the time, Pallas kernels for 13%

profile of v8, /device:TPU:0, one launch (start us, length us, event | category | flops | bytes accessed | tf_op | source)
XLA Modules:
  0.0 19.5 jit_solution(3411946024912679071)
XLA Ops:
  0.0 1.4 %start.1 = (f32[4,6,16,256]{3,2,1,0:T(8,128)S(1)}, f32[3,24,256]{2,1,0:T(8,128)S(1)}, f32[3,24,256]{2,1,0:T(8,128)S(1)}, f32[2,24,256]{2,1,0:T(8,128)S(1)}, f32[...) custom-call(f32[4,6,16,256]{3,2,1,0:T(8,128)} %fields.1, s32[4,6]{1,0:T(4,128)} %neighbors.1, ...), custom_call_target="tpu_custom_call" | custom-call | tf_op jit(solution)/shard_map/start/pallas_call | solution.py:451
  1.5 3.1 %collective-permute-start.2 = (f32[2,24,256]{2,1,0:T(8,128)S(1)}, f32[2,24,256]{2,1,0:T(8,128)S(1)}, u32[]{:S(2)}, u32[]{:S(2)}) collective-permute-start(f32[2,24,256]{2,1,0:T(8,128)S(1)} %get-tuple-element.47), channel_id=1, source_target_pairs={{0,8},{1,9},{2,10},{3,11},{4,12},{5,13},{6,14},{7,15},{8,0},{9,1},... | collective-permute-start | bytes 147464 | tf_op jit(solution)/shard_map/ppermute | solution.py:54
  4.5 0.0 collective-permute-start.3
  5.2 0.1 collective-permute-start.1
  5.4 0.5 %collective-permute-start = (f32[96,256]{1,0:T(8,128)S(1)}, f32[96,256]{1,0:T(8,128)S(1)}, u32[]{:S(2)}, u32[]{:S(2)}) collective-permute-start(f32[96,256]{1,0:T(8,128)S(1)} %get-tuple-element.45), channel_id=1, source_target_pairs={{0,1},{1,0},{2,3},{3,2},{4,5},{5,4},{6,7},{7,6},{8,9},{9,8},{10,11... | collective-permute-start | bytes 294920 | tf_op jit(solution)/shard_map/ppermute | solution.py:54
  6.5 0.1 collective-permute-done.2.faces
  6.6 0.0 collective-permute-done.3.faces_dev
  6.6 0.1 faces.1
  6.7 0.1 collective-permute-start.4
  6.8 2.1 %collective-permute-start.5 = (f32[2,24,256]{2,1,0:T(8,128)S(1)}, f32[2,24,256]{2,1,0:T(8,128)S(1)}, u32[]{:S(2)}, u32[]{:S(2)}) collective-permute-start(f32[2,24,256]{2,1,0:T(8,128)S(1)} %get-tuple-element.53), channel_id=1, source_target_pairs={{0,8},{1,2},{2,1},{3,4},{4,3},{5,6},{6,5},{7,15},{8,0},{9,10},{10,... | collective-permute-start | bytes 147464 | tf_op jit(solution)/shard_map/ppermute | solution.py:54
  8.8 0.0 collective-permute-start.6
  8.9 0.0 collective-permute-done.block_dev
  8.9 2.2 %collective-permute-done.1.block_grp = f32[120,256]{1,0:T(8,128)S(1)} collective-permute-done((f32[120,256]{1,0:T(8,128)S(1)}, f32[120,256]{1,0:T(8,128)S(1)}, u32[]{:S(2)}, u32[]{:S(2)}) %collective-permute-start.1) | collective-permute-done | bytes 122912 | tf_op jit(solution)/shard_map/ppermute | solution.py:54
  11.0 0.6 %inner_0.1 = (f32[2,384,128]{2,1,0:T(8,128)S(1)}, f32[24,256]{1,0:T(8,128)S(1)}, f32[24,256]{1,0:T(8,128)S(1)}, f32[24,256]{1,0:T(8,128)S(1)}, f32[24,256]{1,0:T(8,128)S(1)}) custom-call(f32[24,256]{1,0:T(8,128)S(1)} %broadcast_in_dim.21.mask_dev, f32[24,256]{1,0:T(8,128)S(1)} %broadcast_in_dim.23.mask_grp, f32[4,24,128]{2,1,0:T(8,128)S(1)} %get-tuple-element.36.scale, ...), custom_call_target="tpu_custom_call" | custom-call | flops 4194304 | bytes 2097152 | tf_op jit(solution)/shard_map/inner_0/pallas_call | solution.py:437
  11.6 0.0 collective-permute-done.5.flat_b
  11.6 0.0 collective-permute-done.4.flat_a
  11.6 0.3 %sides_0.1.partial = f32[2,384,128]{2,1,0:T(8,128)S(1)} custom-call(f32[4,24,128]{2,1,0:T(8,128)S(1)} %get-tuple-element.36.scale, f32[3,48,192]{2,1,0:T(8,128)S(1)} %get-tuple-element.37.select, f32[2,384,128]{2,1,0:T(8,128)S(1)} %get-tuple-element.51.partial, f32[3,24,256]{2,1,0:T(8,128)S(1)} %get-tuple-element.49.new_low.low, ...), custom_call_target="tpu_custom_call" | custom-call | flops 1048576 | bytes 1048576 | tf_op jit(solution)/shard_map/sides_0/pallas_call | solution.py:437
  12.0 0.0 collective-permute-done.6.deep_b
  12.0 0.6 %finish_0.1 = (f32[2,384,128]{2,1,0:T(8,128)S(1)}, f32[3,24,256]{2,1,0:T(8,128)S(1)}, f32[3,24,256]{2,1,0:T(8,128)S(1)}, f32[2,24,256]{2,1,0:T(8,128)S(1)}, f32[...) custom-call(f32[4,24,128]{2,1,0:T(8,128)S(1)} %get-tuple-element.36.scale, ...), custom_call_target="tpu_custom_call" | custom-call | flops 1048576 | bytes 1048576 | tf_op jit(solution)/shard_map/finish_0/pallas_call | solution.py:437
  12.6 0.1 collective-permute-start.7
  12.6 1.9 %collective-permute-start.8 = (f32[2,24,256]{2,1,0:T(8,128)S(1)}, f32[2,24,256]{2,1,0:T(8,128)S(1)}, u32[]{:S(2)}, u32[]{:S(2)}) collective-permute-start(f32[2,24,256]{2,1,0:T(8,128)S(1)} %get-tuple-element.63), channel_id=1, source_target_pairs={{0,8},{1,2},{2,1},{3,4},{4,3},{5,6},{6,5},{7,15},{8,0},{9,10},{10,... | collective-permute-start | bytes 147464 | tf_op jit(solution)/shard_map/ppermute | solution.py:54
  14.5 0.2 %collective-permute-start.9 = (f32[24,256]{1,0:T(8,128)S(1)}, f32[24,256]{1,0:T(8,128)S(1)}, u32[]{:S(2)}, u32[]{:S(2)}) collective-permute-start(f32[24,256]{1,0:T(8,128)S(1)} %get-tuple-element.65), channel_id=1, source_target_pairs={{0,8},{1,9},{2,10},{3,11},{4,12},{5,13},{6,14},{7,15},{8,0},{9,1},... | collective-permute-start | bytes 73736 | tf_op jit(solution)/shard_map/ppermute | solution.py:54
  14.7 1.3 %collective-permute-start.10 = (f32[24,256]{1,0:T(8,128)S(1)}, f32[24,256]{1,0:T(8,128)S(1)}, u32[]{:S(2)}, u32[]{:S(2)}) collective-permute-start(f32[24,256]{1,0:T(8,128)S(1)} %get-tuple-element.66), channel_id=1, source_target_pairs={{0,1},{1,0},{2,3},{3,2},{4,5},{5,4},{6,7},{7,6},{8,16},{9,17},{10,... | collective-permute-start | bytes 73736 | tf_op jit(solution)/shard_map/ppermute | solution.py:54
  16.0 0.5 %inner_1.1.partial = f32[2,384,128]{2,1,0:T(8,128)S(1)} custom-call(f32[2,384,128]{2,1,0:T(8,128)S(1)} %get-tuple-element.59.state, f32[4,24,128]{2,1,0:T(8,128)S(1)} %get-tuple-element.36.scale), custom_call_target="tpu_custom_call" | custom-call | flops 4194304 | bytes 2097152 | tf_op jit(solution)/shard_map/inner_1/pallas_call | solution.py:437
  16.5 0.0 collective-permute-done.7.flat_a
  16.5 0.3 %collective-permute-done.8.flat_b = f32[2,24,256]{2,1,0:T(8,128)S(1)} collective-permute-done((f32[2,24,256]{2,1,0:T(8,128)S(1)}, f32[2,24,256]{2,1,0:T(8,128)S(1)}, u32[]{:S(2)}, u32[]{:S(2)}) %collective-permute-start.8) | collective-permute-done | bytes 49184 | tf_op jit(solution)/shard_map/ppermute | solution.py:54
  16.8 1.1 %sides_1.1 = (f32[4,6,16,256]{3,2,1,0:T(8,128)S(1)}, f32[2,408,128]{2,1,0:T(8,128)}) custom-call(f32[4,24,128]{2,1,0:T(8,128)S(1)} %get-tuple-element.36.scale, f32[3,48,192]{2,1,0:T(8,128)S(1)} %get-tuple-element.37.select, f32[2,384,128]{2,1,0:T(8,128)S(1)} %inner_1.1.partial, f32[3,24,256]{2,1,0:T(8,128)S(1)} %get-tuple-element.60.low, ...), custom_call_target="tpu_custom_call" | custom-call | flops 1048576 | bytes 1048576 | tf_op jit(solution)/shard_map/sides_1/pallas_call | solution.py:437
  17.9 0.4 %collective-permute-done.9.deep_a = f32[24,256]{1,0:T(8,128)S(1)} collective-permute-done((f32[24,256]{1,0:T(8,128)S(1)}, f32[24,256]{1,0:T(8,128)S(1)}, u32[]{:S(2)}, u32[]{:S(2)}) %collective-permute-start.9) | collective-permute-done | bytes 24608 | tf_op jit(solution)/shard_map/ppermute | solution.py:54
  18.3 0.0 collective-permute-done.10.deep_b
  18.3 1.1 %finish_1.1 = f32[4,6,16,256]{3,2,1,0:T(8,128)} custom-call(f32[4,24,128]{2,1,0:T(8,128)S(1)} %get-tuple-element.36.scale, f32[3,48,192]{2,1,0:T(8,128)S(1)} %get-tuple-element.37.select, f32[4,6,16,256]{3,2,1,0:T(8,128)S(1)} %get-tuple-element.64.partial, f32[3,24,256]{2,1,0:T(8,128)S(1)} %get-tuple-element.60.low, ...), custom_call_target="tpu_custom_call" | custom-call | tf_op jit(solution)/shard_map/finish_1/pallas_call | solution.py:513
  (3 shorter events, 0.0 us)
Async XLA Ops:
  1.5 5.2 %collective-permute-start.2 = (f32[2,24,256]{2,1,0:T(8,128)S(1)}, f32[2,24,256]{2,1,0:T(8,128)S(1)}, u32[]{:S(2)}, u32[]{:S(2)}) collective-permute-start(f32[2,24,256]{2,1,0:T(8,128)S(1)} %get-tuple-element.47), channel_id=1, source_target_pairs={{0,8},{1,9},{2,10},{3,11},{4,12},{5,13},{6,14},{7,15},{8,0},{9,1},... | collective-permute-start | bytes 147464 | tf_op jit(solution)/shard_map/ppermute | solution.py:54
  4.5 2.1 %collective-permute-start.3 = (f32[2,24,256]{2,1,0:T(8,128)S(1)}, f32[2,24,256]{2,1,0:T(8,128)S(1)}, u32[]{:S(2)}, u32[]{:S(2)}) collective-permute-start(f32[2,24,256]{2,1,0:T(8,128)S(1)} %get-tuple-element.48), channel_id=1, source_target_pairs={{0,1},{1,0},{2,3},{3,2},{4,5},{5,4},{6,7},{7,6},{8,9},{9,8},{10,11... | collective-permute-start | bytes 147464 | tf_op jit(solution)/shard_map/ppermute | solution.py:54
  5.2 5.8 %collective-permute-start.1 = (f32[120,256]{1,0:T(8,128)S(1)}, f32[120,256]{1,0:T(8,128)S(1)}, u32[]{:S(2)}, u32[]{:S(2)}) collective-permute-start(f32[120,256]{1,0:T(8,128)S(1)} %get-tuple-element.46), channel_id=1, source_target_pairs={{0,8},{1,9},{2,10},{3,11},{4,12},{5,13},{6,14},{7,15},{8,0},{9,1},... | collective-permute-start | bytes 368648 | tf_op jit(solution)/shard_map/ppermute | solution.py:54
  5.4 3.5 %collective-permute-start = (f32[96,256]{1,0:T(8,128)S(1)}, f32[96,256]{1,0:T(8,128)S(1)}, u32[]{:S(2)}, u32[]{:S(2)}) collective-permute-start(f32[96,256]{1,0:T(8,128)S(1)} %get-tuple-element.45), channel_id=1, source_target_pairs={{0,1},{1,0},{2,3},{3,2},{4,5},{5,4},{6,7},{7,6},{8,9},{9,8},{10,11... | collective-permute-start | bytes 294920 | tf_op jit(solution)/shard_map/ppermute | solution.py:54
  6.7 4.9 %collective-permute-start.4 = (f32[3,24,256]{2,1,0:T(8,128)S(1)}, f32[3,24,256]{2,1,0:T(8,128)S(1)}, u32[]{:S(2)}, u32[]{:S(2)}) collective-permute-start(f32[3,24,256]{2,1,0:T(8,128)S(1)} %get-tuple-element.52), channel_id=1, source_target_pairs={{0,1},{1,0},{2,3},{3,2},{4,5},{5,4},{6,7},{7,6},{8,9},{9,8},{10,11... | collective-permute-start | bytes 221192 | tf_op jit(solution)/shard_map/ppermute | solution.py:54
  6.8 4.8 %collective-permute-start.5 = (f32[2,24,256]{2,1,0:T(8,128)S(1)}, f32[2,24,256]{2,1,0:T(8,128)S(1)}, u32[]{:S(2)}, u32[]{:S(2)}) collective-permute-start(f32[2,24,256]{2,1,0:T(8,128)S(1)} %get-tuple-element.53), channel_id=1, source_target_pairs={{0,8},{1,2},{2,1},{3,4},{4,3},{5,6},{6,5},{7,15},{8,0},{9,10},{10,... | collective-permute-start | bytes 147464 | tf_op jit(solution)/shard_map/ppermute | solution.py:54
  8.8 3.1 %collective-permute-start.6 = (f32[24,256]{1,0:T(8,128)S(1)}, f32[24,256]{1,0:T(8,128)S(1)}, u32[]{:S(2)}, u32[]{:S(2)}) collective-permute-start(f32[24,256]{1,0:T(8,128)S(1)} %get-tuple-element.55), channel_id=1, source_target_pairs={{0,1},{1,0},{2,3},{3,2},{4,5},{5,4},{6,7},{7,6},{8,16},{9,17},{10,... | collective-permute-start | bytes 73736 | tf_op jit(solution)/shard_map/ppermute | solution.py:54
  12.6 3.9 %collective-permute-start.7 = (f32[2,24,256]{2,1,0:T(8,128)S(1)}, f32[2,24,256]{2,1,0:T(8,128)S(1)}, u32[]{:S(2)}, u32[]{:S(2)}) collective-permute-start(f32[2,24,256]{2,1,0:T(8,128)S(1)} %get-tuple-element.62), channel_id=1, source_target_pairs={{0,1},{1,0},{2,3},{3,2},{4,5},{5,4},{6,7},{7,6},{8,9},{9,8},{10,11... | collective-permute-start | bytes 147464 | tf_op jit(solution)/shard_map/ppermute | solution.py:54
  12.6 4.2 %collective-permute-start.8 = (f32[2,24,256]{2,1,0:T(8,128)S(1)}, f32[2,24,256]{2,1,0:T(8,128)S(1)}, u32[]{:S(2)}, u32[]{:S(2)}) collective-permute-start(f32[2,24,256]{2,1,0:T(8,128)S(1)} %get-tuple-element.63), channel_id=1, source_target_pairs={{0,8},{1,2},{2,1},{3,4},{4,3},{5,6},{6,5},{7,15},{8,0},{9,10},{10,... | collective-permute-start | bytes 147464 | tf_op jit(solution)/shard_map/ppermute | solution.py:54
  14.5 3.8 %collective-permute-start.9 = (f32[24,256]{1,0:T(8,128)S(1)}, f32[24,256]{1,0:T(8,128)S(1)}, u32[]{:S(2)}, u32[]{:S(2)}) collective-permute-start(f32[24,256]{1,0:T(8,128)S(1)} %get-tuple-element.65), channel_id=1, source_target_pairs={{0,8},{1,9},{2,10},{3,11},{4,12},{5,13},{6,14},{7,15},{8,0},{9,1},... | collective-permute-start | bytes 73736 | tf_op jit(solution)/shard_map/ppermute | solution.py:54
  14.7 3.6 %collective-permute-start.10 = (f32[24,256]{1,0:T(8,128)S(1)}, f32[24,256]{1,0:T(8,128)S(1)}, u32[]{:S(2)}, u32[]{:S(2)}) collective-permute-start(f32[24,256]{1,0:T(8,128)S(1)} %get-tuple-element.66), channel_id=1, source_target_pairs={{0,1},{1,0},{2,3},{3,2},{4,5},{5,4},{6,7},{7,6},{8,16},{9,17},{10,... | collective-permute-start | bytes 73736 | tf_op jit(solution)/shard_map/ppermute | solution.py:54
